TPU v7x, 512 devices: a whole 4x4x16 slice. The times are simulated.
512 devices in a mesh: edata: 64 (over z, y), llm: 8 (over x, core).
Axes of the slice: x: 4, y: 4, z: 16, core: 2. Of those that a mesh axis runs over, the one named last changes fastest.
Arguments:
- grad_rows: bfloat16 [32768, 3200], P(('edata', 'llm')), may hold values from -6 to 6
- row_target: int32 [32768, 1], P(('edata', 'llm')), may hold values from 0 to 63; in each aligned block of 64 rows (0 to 63, 64 to 127, ...) at most 2 rows name the same one
- stored_context: bfloat16 [65536, 2048], P('edata', 'llm'), may hold values from -448 to 448
- block_scale: float32 [65536, 16], P('edata', 'llm'), may hold values from 0.002 to 0.008
- w_out: bfloat16 [2048, 3200], P('llm', 'edata'), may hold values from -0.125 to 0.125
- layer_scale: float32 [3200], replicated, may hold values from 0.3 to 3
Outputs:
- grad_context: bfloat16 [65536, 2048], P('edata', 'llm')
- grad_weight: float32 [3200, 2048], P('edata', 'llm')
- grad_scale: float32 [3200], replicated
Inputs may be any that keep to these rules, and one draw needn't show every extreme that they name: `row_target`: among the 64 rows of one device, no encoder device is named by more than 2 rows, and some encoder device is named by exactly 2 rows.
All inputs are finite; a program needn't handle non-finite values.
Results may differ from a plain program's by a relative error of at most 0.0049.
Values may be sent and summed in bfloat16 or wider, within the bound.
No kernel may reach another device: no remote copies, remote signals or barrier semaphores. Data moves between devices by JAX's collectives and lax.ppermute only.
A program may use at most 128 MiB of HBM per device.

v0:
```python
import math

import jax
import jax.numpy as jnp
from jax import lax
from jax.sharding import PartitionSpec as P

BLOCK = 128


def on_device(grad_rows, row_target, stored_context, block_scale, w_out, layer_scale):
    encoders = lax.axis_size("edata")
    owners = lax.axis_size("llm")
    source_rows = grad_rows.shape[0]
    features = grad_rows.shape[1]
    slot_count = stored_context.shape[0]
    capacity = slot_count // (encoders * owners)
    weights = lax.all_gather(w_out, "edata", axis=1, tiled=True)
    targets = row_target[:, 0]
    chosen = (targets[:, None] == jnp.arange(encoders, dtype=jnp.int32)[None, :]).astype(jnp.int32)
    arrival = jnp.sum(chosen * (jnp.cumsum(chosen, axis=0) - 1), axis=1)
    position = targets * capacity + arrival
    outgoing = jnp.zeros((encoders * capacity, features), jnp.bfloat16).at[position].set(grad_rows)
    arrived = lax.all_to_all(outgoing, "edata", split_axis=0, concat_axis=0, tiled=True)
    grad_slots = lax.all_gather(arrived, "llm", axis=0, tiled=True)
    stored = stored_context.astype(jnp.float32).reshape(slot_count, -1, BLOCK)
    context = (stored * block_scale[:, :, None]).reshape(slot_count, -1).astype(jnp.bfloat16)
    scaled = (grad_slots.astype(jnp.float32) * layer_scale[None, :]).astype(jnp.bfloat16)
    recomputed = jnp.dot(context, weights, preferred_element_type=jnp.float32)
    grad_context = lax.dot_general(
        scaled, weights, (((1,), (1,)), ((), ())), preferred_element_type=jnp.float32
    ).astype(jnp.bfloat16)
    partial_scale = jnp.sum(grad_slots.astype(jnp.float32) * recomputed, axis=0)
    rescale = 1.0 / math.sqrt(source_rows * encoders * owners)
    grad_weight = (
        lax.psum_scatter(
            lax.dot_general(
                scaled, context, (((0,), (0,)), ((), ())), preferred_element_type=jnp.float32
            ),
            "edata",
            scatter_dimension=0,
            tiled=True,
        )
        * rescale
    )
    grad_scale = lax.psum(partial_scale, ("edata", "llm")) * rescale
    return (grad_context, grad_weight, grad_scale)


def solution(mesh):
    in_specs = (
        P(("edata", "llm"), None),
        P(("edata", "llm"), None),
        P("edata", "llm"),
        P("edata", "llm"),
        P("llm", "edata"),
        P(),
    )
    out_specs = (P("edata", "llm"), P("edata", "llm"), P())
    return jax.shard_map(
        on_device, mesh=mesh, in_specs=in_specs, out_specs=out_specs, check_vma=False
    )
```

profile of v0, /device:TPU:1, one launch (start us, length us, event | category | flops | bytes accessed | tf_op | source)
XLA Modules:
  0.0 544.8 jit_solution(8658354963138312212)
XLA Ops:
  9.5 1.9 scatter_custom_fusion
  11.4 1.2 all_to_all.8
  12.7 19.3 %all-to-all-start = ((bf16[64,2,3200]{2,1,0:T(2,128)(2,1)}), bf16[64,2,3200]{2,1,0:T(2,128)(2,1)S(1)}, u32[]{:S(2)}, u32[]{:S(2)}) async-start(bf16[64,2,3200]{2,1,0:T(2,128)(2,1)} %all_to_all.8), calls=%async_computation | async-start | bytes 1638400 | tf_op jit(solution)/shard_map/all_to_all | solution.py:24
  32.7 41.8 %all-to-all-done = bf16[64,2,3200]{2,1,0:T(2,128)(2,1)S(1)} async-done(((bf16[64,2,3200]{2,1,0:T(2,128)(2,1)}), bf16[64,2,3200]{2,1,0:T(2,128)(2,1)S(1)}, u32[]{:S(2)}, u32[]{:S(2)}) %all-to-all-start) | async-done | bytes 819232 | tf_op jit(solution)/shard_map/all_to_all | solution.py:24
  74.6 1.2 all_to_all.10
  76.0 1.3 dynamic-slice.4
  78.0 92.2 %all-gather.6.cloned.1.call-done = bf16[64,50,256]{2,1,0:T(8,128)(2,1)} async-done(((bf16[1,50,256]{2,1,0:T(8,128)(2,1)}), bf16[64,50,256]{2,1,0:T(8,128)(2,1)}) %all-gather.6.cloned.1.call-update) | async-done | bytes 1638416 | tf_op jit(solution)/shard_map/all_gather | solution.py:18
  170.1 3.7 reshape.23
  173.8 53.5 %all-gather.4.cloned.1.call-done = bf16[1024,3200]{1,0:T(8,128)(2,1)} async-done(((bf16[128,3200]{1,0:T(8,128)(2,1)}), bf16[1024,3200]{1,0:T(8,128)(2,1)}) %all-gather.4.cloned.1.call-update) | async-done | bytes 6553616 | tf_op jit(solution)/shard_map/all_gather | solution.py:25
  227.3 1.2 mul.49
  228.5 1.0 copy-done.1
  229.5 5.0 fusion.3
  234.5 140.3 %fusion = f32[56,256]{1,0:T(8,128)S(1)} fusion(f32[3200,256]{1,0:T(8,128)S(1)} %fusion.3), kind=kCustom, calls=%all-reduce-scatter | all-reduce-scatter fusion | flops 917505 | bytes 3336192
  374.8 1.6 collective-permute-start
  376.4 1.6 collective-permute-start.1
  378.0 1.3 collective-permute-start.2
  379.3 1.3 collective-permute-start.3
  380.6 10.5 %collective-permute-start.6 = (f32[42,256]{1,0:T(8,128)S(1)}, f32[42,256]{1,0:T(8,128)S(1)}, u32[]{:S(2)}, u32[]{:S(2)}) collective-permute-start(f32[42,256]{1,0:T(8,128)S(1)} %slice), channel_id=1, source_target_pairs={{0,56},{8,64},{16,72},{24,80},{32,88},{40,96},{48,104},{56,112},{6... | collective-permute-start | bytes 129032
  391.1 5.9 %fusion.2 = f32[3200]{0:T(1024)S(1)} fusion(bf16[1024,3200]{1,0:T(8,128)(2,1)} %all-gather.4.cloned.1.call-done, bf16[3200,256]{1,0:T(8,128)(2,1)} %reshape.23, f32[128,8,2,128]{3,2,1,0:T(2,128)} %bitcast.23, bf16[1024,256]{1,0:T(8,128)(2,1)} %param.8), kind=kOutput, calls=%fused_computation.4 | convolution fusion | flops 1688335232 | bytes 9777664 | tf_op jit(solution)/shard_map/dot_general | solution.py:29
  397.0 2.7 fusion.7
  399.7 128.7 %psum.7 = f32[3200]{0:T(1024)S(1)} all-reduce(f32[3200]{0:T(1024)S(1)} %fusion.2), channel_id=1, replica_groups=mesh['edata'=64,'llm'=8] {'edata','llm'}, use_global_device_ids=true, to_apply=%region_5.6 | all-reduce | flops 3200 | bytes 25600 | tf_op jit(solution)/shard_map/psum | solution.py:46
  528.4 1.3 collective-permute-start.4
  529.7 5.2 collective-permute-start.5
  536.2 1.1 concatenate
  (31 shorter events, 5.2 us)
Async XLA Ops:
  7.2 68.6 %copy-start.2 = (f32[1024,2]{0,1:T(2,128)S(1)}, f32[1024,2]{0,1:T(2,128)}, u32[]{:S(2)}) copy-start(f32[1024,2]{0,1:T(2,128)} %param.9) | copy-start | bytes 24580
  7.2 222.3 %copy-start.3 = (f32[3200]{0:T(1024)S(1)}, f32[3200]{0:T(1024)}, u32[]{:S(2)}) copy-start(f32[3200]{0:T(1024)} %param.11) | copy-start | bytes 38404
  12.7 61.9 %all-to-all-start = ((bf16[64,2,3200]{2,1,0:T(2,128)(2,1)}), bf16[64,2,3200]{2,1,0:T(2,128)(2,1)S(1)}, u32[]{:S(2)}, u32[]{:S(2)}) async-start(bf16[64,2,3200]{2,1,0:T(2,128)(2,1)} %all_to_all.8), calls=%async_computation | async-start | bytes 1638400 | tf_op jit(solution)/shard_map/all_to_all | solution.py:24
  31.9 138.2 %all-gather.6.cloned.1.call-start = ((), (), s32[]{:S(2)}) async-start(), calls=%async_computation.2 | async-start | bytes 1863680 | tf_op jit(solution)/shard_map/all_gather | solution.py:18
  32.7 194.6 %all-gather.4.cloned.1.call-start = ((), (), s32[]{:S(2)}) async-start(), calls=%async_computation.1 | async-start | bytes 7372800 | tf_op jit(solution)/shard_map/all_gather | solution.py:25
  228.5 1.0 copy-start.1
  374.8 22.2 %slice-start = ((s8[6553600]{0:T(1024)(128)(4,1)}), s8[4194304]{0:T(1024)(128)(4,1)S(1)}, s32[]{:S(2)}) async-start(s8[6553600]{0:T(1024)(128)(4,1)} %bitcast.27), calls=%async_computation.3 | async-start | bytes 8388608
  374.8 22.1 %copy-start = (bf16[3200,256]{1,0:T(8,128)(2,1)S(1)}, bf16[3200,256]{1,0:T(8,128)(2,1)}, u32[]{:S(2)}) copy-start(bf16[3200,256]{1,0:T(8,128)(2,1)} %reshape.23) | copy-start | bytes 4915204
  374.8 22.1 %slice-start.1 = ((s8[6553600]{0:T(1024)(128)(4,1)}), s8[2359296]{0:T(1024)(128)(4,1)S(1)}, s32[]{:S(2)}) async-start(s8[6553600]{0:T(1024)(128)(4,1)} %bitcast.27), calls=%async_computation.4 | async-start | bytes 4718592
  374.8 154.9 %collective-permute-start = (f32[56,256]{1,0:T(8,128)S(1)}, f32[56,256]{1,0:T(8,128)S(1)}, u32[]{:S(2)}, u32[]{:S(2)}) collective-permute-start(f32[56,256]{1,0:T(8,128)S(1)} %fusion), channel_id=1, source_target_pairs={{0,8},{8,16},{16,24},{24,32},{32,40},{40,48},{48,56},{56,64},{64,7... | collective-permute-start | bytes 172040
  376.4 159.2 %collective-permute-start.1 = (f32[56,256]{1,0:T(8,128)S(1)}, f32[56,256]{1,0:T(8,128)S(1)}, u32[]{:S(2)}, u32[]{:S(2)}) collective-permute-start(f32[56,256]{1,0:T(8,128)S(1)} %fusion), channel_id=1, source_target_pairs={{0,16},{8,24},{16,32},{24,40},{32,48},{40,56},{48,64},{56,72},{64,... | collective-permute-start | bytes 172040
  378.0 157.6 %collective-permute-start.2 = (f32[56,256]{1,0:T(8,128)S(1)}, f32[56,256]{1,0:T(8,128)S(1)}, u32[]{:S(2)}, u32[]{:S(2)}) collective-permute-start(f32[56,256]{1,0:T(8,128)S(1)} %fusion), channel_id=1, source_target_pairs={{0,24},{8,32},{16,40},{24,48},{32,56},{40,64},{48,72},{56,80},{64,... | collective-permute-start | bytes 172040
  379.3 156.3 %collective-permute-start.3 = (f32[56,256]{1,0:T(8,128)S(1)}, f32[56,256]{1,0:T(8,128)S(1)}, u32[]{:S(2)}, u32[]{:S(2)}) collective-permute-start(f32[56,256]{1,0:T(8,128)S(1)} %fusion), channel_id=1, source_target_pairs={{0,32},{8,40},{16,48},{24,56},{32,64},{40,72},{48,80},{56,88},{64,... | collective-permute-start | bytes 172040
  380.6 147.9 %collective-permute-start.6 = (f32[42,256]{1,0:T(8,128)S(1)}, f32[42,256]{1,0:T(8,128)S(1)}, u32[]{:S(2)}, u32[]{:S(2)}) collective-permute-start(f32[42,256]{1,0:T(8,128)S(1)} %slice), channel_id=1, source_target_pairs={{0,56},{8,64},{16,72},{24,80},{32,88},{40,96},{48,104},{56,112},{6... | collective-permute-start | bytes 129032
  528.4 7.2 %collective-permute-start.4 = (f32[56,256]{1,0:T(8,128)S(1)}, f32[56,256]{1,0:T(8,128)S(1)}, u32[]{:S(2)}, u32[]{:S(2)}) collective-permute-start(f32[56,256]{1,0:T(8,128)S(1)} %fusion), channel_id=1, source_target_pairs={{0,40},{8,48},{16,56},{24,64},{32,72},{40,80},{48,88},{56,96},{64,... | collective-permute-start | bytes 172040
  529.7 6.5 %collective-permute-start.5 = (f32[56,256]{1,0:T(8,128)S(1)}, f32[56,256]{1,0:T(8,128)S(1)}, u32[]{:S(2)}, u32[]{:S(2)}) collective-permute-start(f32[56,256]{1,0:T(8,128)S(1)} %fusion), channel_id=1, source_target_pairs={{0,48},{8,56},{16,64},{24,72},{32,80},{40,88},{48,96},{56,104},{64... | collective-permute-start | bytes 172040
Sparse Core Ops, SparseCore 0:
  35.7 134.3 all-gather.5
  172.3 55.0 all-gather.3
where the time goes:
time: 549 us; the launch traced here: 545 us
  blocking collectives  269 us (49%)
  waiting for transfers between devices  189 us (34%)
  starting transfers between devices  42.1 us (8%)
  between operations  14.9 us (3%)
  matrix products  13.6 us (2%)
  local copies, waits for them, and re-layouts  12.8 us (2%)
    unnamed x1, blocking collectives  140 us
    psum x1, blocking collectives, on_device(): grad_scale = lax.psum(partial_scale, ('edata', 'llm')) * rescale  129 us
    all_gather x1, waiting for transfers between devices, on_device(): weights = lax.all_gather(w_out, 'edata', axis=1, tiled=True)  92.2 us
    all_gather x1, waiting for transfers between devices, on_device(): grad_slots = lax.all_gather(arrived, 'llm', axis=0, tiled=True)  53.5 us
    all_to_all x1, waiting for transfers between devices, on_device(): lax.all_to_all(outgoing, 'edata', split_axis=0, concat_axis=0, tiled=True)  41.8 us
    unnamed x7, starting transfers between devices  22.7 us
    all_to_all x1, starting transfers between devices, on_device(): lax.all_to_all(outgoing, 'edata', split_axis=0, concat_axis=0, tiled=True)  19.3 us
  transfers between devices with their start and end apart: 10, of which 4 were waited for; matrix products, arithmetic and copies ran while one was open for 3% of the time, Pallas kernels for 0%

commit v1 on v0

v1 whole, which is shorter than its diff:
```python
import math

import jax
import jax.numpy as jnp
from jax import lax
from jax.sharding import Mesh
from jax.sharding import PartitionSpec as P

BLOCK = 128
F32 = jnp.float32
BF16 = jnp.bfloat16


def group_pairs(size, group, stride, shift):
    pairs = []
    for i in range(size):
        digit = (i // stride) % group
        pairs.append((i, i + ((digit + shift) % group - digit) * stride))
    return pairs


def exchange(blocks, axis, size, group, stride):
    digit = (lax.axis_index(axis) // stride) % group
    got = [lax.dynamic_index_in_dim(blocks, digit, 0, keepdims=False)]
    for shift in range(1, group):
        block = lax.dynamic_index_in_dim(blocks, (digit + shift) % group, 0, keepdims=False)
        got.append(lax.ppermute(block, axis, group_pairs(size, group, stride, shift)))
    return got


def sum_all(value, axis, size, group, stride):
    total = value
    for shift in range(1, group):
        total = total + lax.ppermute(value, axis, group_pairs(size, group, stride, shift))
    return total


def on_device(grad_rows, row_target, stored_context, block_scale, w_out, layer_scale):
    nz, ny, nx, nc = (lax.axis_size(a) for a in ("z", "y", "x", "c"))
    encoders, owners = nz * ny, nx * nc
    source_rows, features = grad_rows.shape
    slot_count, width = stored_context.shape
    capacity = slot_count // (encoders * owners)
    own = features // encoders

    stored = stored_context.astype(F32).reshape(slot_count, -1, BLOCK)
    context = (stored * block_scale[:, :, None]).reshape(slot_count, width).astype(BF16)
    send = context.reshape(owners, encoders, capacity, width).transpose(1, 0, 2, 3)
    send = send.reshape(encoders, owners * capacity, width)
    slots = lax.all_to_all(send, ("z", "y"), split_axis=0, concat_axis=0, tiled=True)
    slots = slots.reshape(slot_count, width)

    pad = 16
    extra = jnp.zeros((pad, features), BF16).at[0, :source_rows].set(row_target[:, 0].astype(BF16))
    rows = lax.all_gather(jnp.concatenate([grad_rows, extra], axis=0), ("x", "c"), axis=0, tiled=True)
    weights = lax.all_gather(w_out.T, "z", axis=0, tiled=False)
    weights = lax.all_gather(weights, "y", axis=1, tiled=False).reshape(features, width)

    targets = rows.reshape(owners, source_rows + pad, features)[:, source_rows, :source_rows].astype(jnp.int32)
    place = jnp.arange(source_rows, dtype=jnp.int32)
    same = (targets[:, :, None] == targets[:, None, :]) & (place[None, None, :] < place[None, :, None])
    arrival = jnp.sum(same.astype(jnp.int32), axis=2)
    owner = jnp.arange(owners, dtype=jnp.int32)[:, None]
    slot = targets * (owners * capacity) + owner * capacity + arrival
    slot = jnp.pad(slot, ((0, 0), (0, pad)), constant_values=-1).reshape(-1)
    select = (slot[:, None] == jnp.arange(slot_count, dtype=jnp.int32)[None, :]).astype(BF16)

    row_context = jnp.dot(select, slots, preferred_element_type=F32).astype(BF16)
    partial = lax.dot_general(rows, row_context, (((0,), (0,)), ((), ())), preferred_element_type=F32)

    scaled = (rows.astype(F32) * layer_scale[None, :]).astype(BF16)
    live = jnp.dot(scaled, weights, preferred_element_type=F32).astype(BF16)
    back = lax.dot_general(select, live, (((0,), (0,)), ((), ())), preferred_element_type=F32).astype(BF16)
    back = back.reshape(encoders, owners * capacity, width)
    back = lax.all_to_all(back, ("z", "y"), split_axis=0, concat_axis=0, tiled=True)
    back = back.reshape(encoders, owners, capacity, width).transpose(1, 0, 2, 3)
    grad_context = back.reshape(slot_count, width)

    rescale = 1.0 / math.sqrt(source_rows * encoders * owners)
    scale_part = jnp.sum(weights.astype(F32) * partial, axis=1).reshape(features // BLOCK, BLOCK)
    scale_part = sum_all(scale_part, "c", nc, nc, 1)
    scale_part = sum_all(scale_part, "x", nx, nx, 1)
    scale_part = sum_all(scale_part, "y", ny, ny, 1)
    scale_part = sum_all(scale_part, "z", nz, 4, 1)
    scale_part = sum_all(scale_part, "z", nz, nz // 4, 4)
    grad_scale = scale_part.reshape(features) * rescale

    blocks = partial.astype(BF16).reshape(nz, ny, own, width).transpose(1, 0, 2, 3)
    total = sum(b.astype(F32) for b in exchange(blocks, "y", ny, ny, 1))
    blocks = total.astype(BF16).reshape(nz // 4, 4, own, width).transpose(1, 0, 2, 3)
    total = sum(b.astype(F32) for b in exchange(blocks, "z", nz, 4, 1))
    total = sum(exchange(total, "z", nz, nz // 4, 4))
    place = lax.axis_index(("z", "y")) * own
    own_scale = lax.dynamic_slice(layer_scale, (place,), (own,))
    grad_weight = total * (own_scale * rescale)[:, None]
    return (grad_context, grad_weight, grad_scale)


def solution(mesh):
    finer = Mesh(mesh.devices.reshape(16, 4, 4, 2), ("z", "y", "x", "c"))
    edata, llm = ("z", "y"), ("x", "c")
    in_specs = (
        P(edata + llm, None),
        P(edata + llm, None),
        P(edata, llm),
        P(edata, llm),
        P(llm, edata),
        P(),
    )
    out_specs = (P(edata, llm), P(edata, llm), P())
    return jax.shard_map(
        on_device, mesh=finer, in_specs=in_specs, out_specs=out_specs, check_vma=False
    )
```

time: 549 us -> 273 us (0.50)
  the two profiles are of different devices: /device:TPU:1 before, /device:TPU:2 now
where the time goes in v1:
time: 273 us; the launch traced here: 272 us
  starting transfers between devices  111 us (41%)
  waiting for transfers between devices  79.1 us (29%)
  blocking collectives  38.5 us (14%)
  between operations  14.7 us (5%)
  local copies, waits for them, and re-layouts  11.7 us (4%)
  matrix products  11.4 us (4%)
  other arithmetic  5.81 us (2%)
    ppermute x13, starting transfers between devices, sum_all(): lax.ppermute(value, axis, group_pairs(size, group, stride, shift))  52 us
    all_gather x1, blocking collectives, on_device(): weights = lax.all_gather(w_out.T, 'z', axis=0, tiled=False)  38.5 us
    all_gather x1, waiting for transfers between devices, on_device(): lax.all_gather(jnp.concatenate([grad_rows, extra], axis=0), ('x', 'c'), a...  38.3 us
    ppermute x9, starting transfers between devices, exchange(): lax.ppermute(block, axis, group_pairs(size, group, stride, shift))  33.1 us
    all_gather x1, waiting for transfers between devices, on_device(): lax.all_gather(weights, 'y', axis=1, tiled=False).reshape(features, width)  19.1 us
    all_to_all x1, starting transfers between devices, on_device(): lax.all_to_all(back, ('z', 'y'), split_axis=0, concat_axis=0, tiled=True)  15.6 us
    ppermute x13, waiting for transfers between devices, sum_all(): lax.ppermute(value, axis, group_pairs(size, group, stride, shift))  13.4 us
    all_to_all x1, starting transfers between devices, on_device(): lax.all_to_all(send, ('z', 'y'), split_axis=0, concat_axis=0, tiled=True)  10.1 us
  transfers between devices with their start and end apart: 26, of which 7 were waited for; matrix products, arithmetic and copies ran while one was open for 8% of the time, Pallas kernels for 0%

profile of v1, /device:TPU:2, one launch (start us, length us, event | category | flops | bytes accessed | tf_op | source)
XLA Modules:
  0.0 272.1 jit_solution(1332972611963041942)
XLA Ops:
  7.2 38.5 %all-gather.2 = bf16[16,50,256]{2,1,0:T(8,128)(2,1)S(1)} all-gather(bf16[1,50,256]{2,1,0:T(8,128)(2,1)} %bitcast.78), channel_id=2, replica_groups=mesh['z'=16,'y'=4,'x'=4,'c'=2] {'z'}, dimensions={0}, use_global_device_ids=true | all-gather | bytes 435200 | tf_op jit(solution)/shard_map/all_gather | solution.py:56
  52.1 10.1 %all-to-all-start.1 = ((bf16[64,16,256]{2,1,0:T(8,128)(2,1)}), bf16[64,16,256]{2,1,0:T(8,128)(2,1)S(1)}, u32[]{:S(2)}, u32[]{:S(2)}) async-start(bf16[64,16,256]{2,1,0:T(8,128)(2,1)} %copy.36), calls=%async_computation.1 | async-start | bytes 1048576 | tf_op jit(solution)/shard_map/all_to_all | solution.py:50
  62.4 19.1 %all-gather.8.cloned.1.call-done = bf16[16,200,256]{2,0,1:T(8,128)(2,1)} async-done(((bf16[16,50,256]{2,0,1:T(8,128)(2,1)}), bf16[16,200,256]{2,0,1:T(8,128)(2,1)}) %all-gather.8.cloned.1.call-update) | async-done | bytes 1638416 | tf_op jit(solution)/shard_map/all_gather | solution.py:57
  83.4 38.3 %all-gather.6.cloned.1.call-done = bf16[640,3200]{1,0:T(8,128)(2,1)} async-done(((bf16[80,3200]{1,0:T(8,128)(2,1)}), bf16[640,3200]{1,0:T(8,128)(2,1)}) %all-gather.6.cloned.1.call-update) | async-done | bytes 4096016 | tf_op jit(solution)/shard_map/all_gather | solution.py:55
  123.0 5.9 %multiply_reduce_fusion = (f32[3200]{0:T(1024)S(1)}, bf16[3200,256]{1,0:T(8,128)(2,1)}) fusion(bf16[16,200,256]{2,1,0:T(8,128)(2,1)S(1)} %copy.32, bf16[640,3200]{1,0:T(8,128)(2,1)} %all-gather.6.cloned.1.call-done, bf16[1024,256]{1,0:T(8,128)(2,1)S(1)} %bitcast.76, s32[640]{0:T(1024)S(1)} %eq.45), kind=kOutput, calls=%fused_computation.3 | convolution fusion | flops 1388213120 | bytes 7912448 | tf_op jit(solution)/shard_map/dot_general | solution.py:69
  131.1 5.5 %fusion.6 = bf16[1024,256]{1,0:T(8,128)(2,1)} fusion(s32[640]{0:T(1024)S(1)} %eq.45, bf16[3200,256]{1,0:T(8,128)(2,1)S(1)} %bitcast.75, bf16[640,3200]{1,0:T(8,128)(2,1)} %all-gather.6.cloned.1.call-done, f32[3200]{0:T(1024)S(1)} %copy-done.2), kind=kOutput, calls=%fused_computation.9 | convolution fusion | flops 1391345664 | bytes 6274048 | tf_op jit(solution)/shard_map/dot_general | solution.py:73
  136.5 15.6 %all-to-all-start = ((bf16[64,16,256]{2,1,0:T(8,128)(2,1)}), bf16[64,16,256]{2,1,0:T(8,128)(2,1)S(1)}, u32[]{:S(2)}, u32[]{:S(2)}) async-start(bf16[64,16,256]{2,1,0:T(8,128)(2,1)} %bitcast.7), calls=%async_computation | async-start | bytes 1048576 | tf_op jit(solution)/shard_map/all_to_all | solution.py:75
  154.7 3.5 %collective-permute-start.12 = (f32[25,128]{1,0:T(8,128)S(1)}, f32[25,128]{1,0:T(8,128)S(1)}, u32[]{:S(2)}, u32[]{:S(2)}) collective-permute-start(f32[25,128]{1,0:T(8,128)S(1)} %bitcast_add_fusion.1), channel_id=1, source_target_pairs={{0,6},{2,0},{4,2},{6,4},{1,7},{3,1},{5,3},{7,5},{8,14},{10,8},{12,... | collective-permute-start | bytes 38408 | tf_op jit(solution)/shard_map/ppermute | solution.py:34
  161.1 3.2 %collective-permute-start.10 = (f32[25,128]{1,0:T(8,128)S(1)}, f32[25,128]{1,0:T(8,128)S(1)}, u32[]{:S(2)}, u32[]{:S(2)}) collective-permute-start(f32[25,128]{1,0:T(8,128)S(1)} %bitcast_add_fusion.1), channel_id=1, source_target_pairs={{0,2},{2,4},{4,6},{6,0},{1,3},{3,5},{5,7},{7,1},{8,10},{10,12},{12... | collective-permute-start | bytes 38408 | tf_op jit(solution)/shard_map/ppermute | solution.py:34
  165.5 4.7 %collective-permute-start.2 = (bf16[16,50,256]{2,1,0:T(8,128)(2,1)}, bf16[16,50,256]{2,1,0:T(8,128)(2,1)S(1)}, u32[]{:S(2)}, u32[]{:S(2)}) collective-permute-start(bf16[16,50,256]{2,1,0:T(8,128)(2,1)} %get-tuple-element.18), channel_id=1, source_target_pairs={{0,24},{8,0},{16,8},{24,16},{1,25},{9,1},{17,9},{25,17},{2,26},{10... | collective-permute-start | bytes 1228808 | tf_op jit(solution)/shard_map/ppermute | solution.py:27
  175.7 4.3 %collective-permute-start.15 = (f32[25,128]{1,0:T(8,128)S(1)}, f32[25,128]{1,0:T(8,128)S(1)}, u32[]{:S(2)}, u32[]{:S(2)}) collective-permute-start(f32[25,128]{1,0:T(8,128)S(1)} %add_add_fusion.2), channel_id=1, source_target_pairs={{0,24},{8,0},{16,8},{24,16},{1,25},{9,1},{17,9},{25,17},{2,26},{10... | collective-permute-start | bytes 38408 | tf_op jit(solution)/shard_map/ppermute | solution.py:34
  180.0 3.4 %collective-permute-start.14 = (f32[25,128]{1,0:T(8,128)S(1)}, f32[25,128]{1,0:T(8,128)S(1)}, u32[]{:S(2)}, u32[]{:S(2)}) collective-permute-start(f32[25,128]{1,0:T(8,128)S(1)} %add_add_fusion.2), channel_id=1, source_target_pairs={{0,16},{8,24},{16,0},{24,8},{1,17},{9,25},{17,1},{25,9},{2,18},{10... | collective-permute-start | bytes 38408 | tf_op jit(solution)/shard_map/ppermute | solution.py:34
  183.4 8.3 %collective-permute-done.15 = f32[25,128]{1,0:T(8,128)S(1)} collective-permute-done((f32[25,128]{1,0:T(8,128)S(1)}, f32[25,128]{1,0:T(8,128)S(1)}, u32[]{:S(2)}, u32[]{:S(2)}) %collective-permute-start.15) | collective-permute-done | bytes 12832 | tf_op jit(solution)/shard_map/ppermute | solution.py:34
  198.9 5.0 %collective-permute-start.18 = (f32[25,128]{1,0:T(8,128)S(1)}, f32[25,128]{1,0:T(8,128)S(1)}, u32[]{:S(2)}, u32[]{:S(2)}) collective-permute-start(f32[25,128]{1,0:T(8,128)S(1)} %add_add_fusion.1), channel_id=1, source_target_pairs={{0,96},{32,0},{64,32},{96,64},{128,224},{160,128},{192,160},{224,1... | collective-permute-start | bytes 38408 | tf_op jit(solution)/shard_map/ppermute | solution.py:34
  205.9 3.3 %collective-permute-start.16 = (f32[25,128]{1,0:T(8,128)S(1)}, f32[25,128]{1,0:T(8,128)S(1)}, u32[]{:S(2)}, u32[]{:S(2)}) collective-permute-start(f32[25,128]{1,0:T(8,128)S(1)} %add_add_fusion.1), channel_id=1, source_target_pairs={{0,32},{32,64},{64,96},{96,0},{128,160},{160,192},{192,224},{224,1... | collective-permute-start | bytes 38408 | tf_op jit(solution)/shard_map/ppermute | solution.py:34
  210.6 4.3 %collective-permute-start.5 = (bf16[4,50,256]{2,1,0:T(8,128)(2,1)S(1)}, bf16[4,50,256]{2,1,0:T(8,128)(2,1)S(1)}, u32[]{:S(2)}, u32[]{:S(2)}) collective-permute-start(bf16[4,50,256]{2,1,0:T(8,128)(2,1)S(1)} %get-tuple-element.21), channel_id=1, source_target_pairs={{0,96},{32,0},{64,32},{96,64},{128,224},{160,128},{192,160},{224,1... | collective-permute-start | bytes 307208 | tf_op jit(solution)/shard_map/ppermute | solution.py:27
  214.9 3.0 %collective-permute-start.4 = (bf16[4,50,256]{2,1,0:T(8,128)(2,1)S(1)}, bf16[4,50,256]{2,1,0:T(8,128)(2,1)S(1)}, u32[]{:S(2)}, u32[]{:S(2)}) collective-permute-start(bf16[4,50,256]{2,1,0:T(8,128)(2,1)S(1)} %get-tuple-element.22), channel_id=1, source_target_pairs={{0,64},{32,96},{64,0},{96,32},{128,192},{160,224},{192,128},{224,1... | collective-permute-start | bytes 307208 | tf_op jit(solution)/shard_map/ppermute | solution.py:27
  219.9 6.0 %collective-permute-start.21 = (f32[25,128]{1,0:T(8,128)S(1)}, f32[25,128]{1,0:T(8,128)S(1)}, u32[]{:S(2)}, u32[]{:S(2)}) collective-permute-start(f32[25,128]{1,0:T(8,128)S(1)} %add_add_fusion), channel_id=1, source_target_pairs={{0,384},{32,416},{64,448},{96,480},{128,0},{160,32},{192,64},{224,... | collective-permute-start | bytes 38408 | tf_op jit(solution)/shard_map/ppermute | solution.py:34
  225.9 8.1 %collective-permute-start.20 = (f32[25,128]{1,0:T(8,128)S(1)}, f32[25,128]{1,0:T(8,128)S(1)}, u32[]{:S(2)}, u32[]{:S(2)}) collective-permute-start(f32[25,128]{1,0:T(8,128)S(1)} %add_add_fusion), channel_id=1, source_target_pairs={{0,256},{32,288},{64,320},{96,352},{128,384},{160,416},{192,448},{... | collective-permute-start | bytes 38408 | tf_op jit(solution)/shard_map/ppermute | solution.py:34
  234.1 6.2 %collective-permute-start.19 = (f32[25,128]{1,0:T(8,128)S(1)}, f32[25,128]{1,0:T(8,128)S(1)}, u32[]{:S(2)}, u32[]{:S(2)}) collective-permute-start(f32[25,128]{1,0:T(8,128)S(1)} %add_add_fusion), channel_id=1, source_target_pairs={{0,128},{32,160},{64,192},{96,224},{128,256},{160,288},{192,320},{... | collective-permute-start | bytes 38408 | tf_op jit(solution)/shard_map/ppermute | solution.py:34
  240.4 3.5 %collective-permute-start.8 = (f32[50,256]{1,0:T(8,128)S(1)}, f32[50,256]{1,0:T(8,128)S(1)}, u32[]{:S(2)}, u32[]{:S(2)}) collective-permute-start(f32[50,256]{1,0:T(8,128)S(1)} %get-tuple-element.24), channel_id=1, source_target_pairs={{0,384},{32,416},{64,448},{96,480},{128,0},{160,32},{192,64},{224,... | collective-permute-start | bytes 153608 | tf_op jit(solution)/shard_map/ppermute | solution.py:27
  244.0 6.4 %collective-permute-start.7 = (f32[50,256]{1,0:T(8,128)S(1)}, f32[50,256]{1,0:T(8,128)S(1)}, u32[]{:S(2)}, u32[]{:S(2)}) collective-permute-start(f32[50,256]{1,0:T(8,128)S(1)} %get-tuple-element.25), channel_id=1, source_target_pairs={{0,256},{32,288},{64,320},{96,352},{128,384},{160,416},{192,448},{... | collective-permute-start | bytes 153608 | tf_op jit(solution)/shard_map/ppermute | solution.py:27
  250.4 3.7 %collective-permute-start.6 = (f32[50,256]{1,0:T(8,128)S(1)}, f32[50,256]{1,0:T(8,128)S(1)}, u32[]{:S(2)}, u32[]{:S(2)}) collective-permute-start(f32[50,256]{1,0:T(8,128)S(1)} %get-tuple-element.23), channel_id=1, source_target_pairs={{0,128},{32,160},{64,192},{96,224},{128,256},{160,288},{192,320},{... | collective-permute-start | bytes 153608 | tf_op jit(solution)/shard_map/ppermute | solution.py:27
  254.8 7.0 %collective-permute-done.7 = f32[50,256]{1,0:T(8,128)S(1)} collective-permute-done((f32[50,256]{1,0:T(8,128)S(1)}, f32[50,256]{1,0:T(8,128)S(1)}, u32[]{:S(2)}, u32[]{:S(2)}) %collective-permute-start.7) | collective-permute-done | bytes 51232 | tf_op jit(solution)/shard_map/ppermute | solution.py:27
  (73 shorter events, 40.3 us)
Async XLA Ops:
  7.2 74.3 %all-gather.8.cloned.1.call-start = ((), (), s32[]{:S(2)}) async-start(), calls=%async_computation.3 | async-start | bytes 2048000 | tf_op jit(solution)/shard_map/all_gather | solution.py:57
  46.6 75.2 %all-gather.6.cloned.1.call-start = ((), (), s32[]{:S(2)}) async-start(), calls=%async_computation.2 | async-start | bytes 4608000 | tf_op jit(solution)/shard_map/all_gather | solution.py:55
  52.1 70.8 %all-to-all-start.1 = ((bf16[64,16,256]{2,1,0:T(8,128)(2,1)}), bf16[64,16,256]{2,1,0:T(8,128)(2,1)S(1)}, u32[]{:S(2)}, u32[]{:S(2)}) async-start(bf16[64,16,256]{2,1,0:T(8,128)(2,1)} %copy.36), calls=%async_computation.1 | async-start | bytes 1048576 | tf_op jit(solution)/shard_map/all_to_all | solution.py:50
  128.9 25.7 %collective-permute-start.9 = (f32[25,128]{1,0:T(8,128)S(1)}, f32[25,128]{1,0:T(8,128)S(1)}, u32[]{:S(2)}, u32[]{:S(2)}) collective-permute-start(f32[25,128]{1,0:T(8,128)S(1)} %bitcast.77), channel_id=1, source_target_pairs={{0,1},{1,0},{2,3},{3,2},{4,5},{5,4},{6,7},{7,6},{8,9},{9,8},{10,11... | collective-permute-start | bytes 38408 | tf_op jit(solution)/shard_map/ppermute | solution.py:34
  136.5 127.2 %all-to-all-start = ((bf16[64,16,256]{2,1,0:T(8,128)(2,1)}), bf16[64,16,256]{2,1,0:T(8,128)(2,1)S(1)}, u32[]{:S(2)}, u32[]{:S(2)}) async-start(bf16[64,16,256]{2,1,0:T(8,128)(2,1)} %bitcast.7), calls=%async_computation | async-start | bytes 1048576 | tf_op jit(solution)/shard_map/all_to_all | solution.py:75
  154.7 18.3 %collective-permute-start.12 = (f32[25,128]{1,0:T(8,128)S(1)}, f32[25,128]{1,0:T(8,128)S(1)}, u32[]{:S(2)}, u32[]{:S(2)}) collective-permute-start(f32[25,128]{1,0:T(8,128)S(1)} %bitcast_add_fusion.1), channel_id=1, source_target_pairs={{0,6},{2,0},{4,2},{6,4},{1,7},{3,1},{5,3},{7,5},{8,14},{10,8},{12,... | collective-permute-start | bytes 38408 | tf_op jit(solution)/shard_map/ppermute | solution.py:34
  158.2 17.5 %collective-permute-start.11 = (f32[25,128]{1,0:T(8,128)S(1)}, f32[25,128]{1,0:T(8,128)S(1)}, u32[]{:S(2)}, u32[]{:S(2)}) collective-permute-start(f32[25,128]{1,0:T(8,128)S(1)} %bitcast_add_fusion.1), channel_id=1, source_target_pairs={{0,4},{2,6},{4,0},{6,2},{1,5},{3,7},{5,1},{7,3},{8,12},{10,14},{12... | collective-permute-start | bytes 38408 | tf_op jit(solution)/shard_map/ppermute | solution.py:34
  161.1 14.6 %collective-permute-start.10 = (f32[25,128]{1,0:T(8,128)S(1)}, f32[25,128]{1,0:T(8,128)S(1)}, u32[]{:S(2)}, u32[]{:S(2)}) collective-permute-start(f32[25,128]{1,0:T(8,128)S(1)} %bitcast_add_fusion.1), channel_id=1, source_target_pairs={{0,2},{2,4},{4,6},{6,0},{1,3},{3,5},{5,7},{7,1},{8,10},{10,12},{12... | collective-permute-start | bytes 38408 | tf_op jit(solution)/shard_map/ppermute | solution.py:34
  165.5 40.4 %collective-permute-start.2 = (bf16[16,50,256]{2,1,0:T(8,128)(2,1)}, bf16[16,50,256]{2,1,0:T(8,128)(2,1)S(1)}, u32[]{:S(2)}, u32[]{:S(2)}) collective-permute-start(bf16[16,50,256]{2,1,0:T(8,128)(2,1)} %get-tuple-element.18), channel_id=1, source_target_pairs={{0,24},{8,0},{16,8},{24,16},{1,25},{9,1},{17,9},{25,17},{2,26},{10... | collective-permute-start | bytes 1228808 | tf_op jit(solution)/shard_map/ppermute | solution.py:27
  170.1 39.1 %collective-permute-start.1 = (bf16[16,50,256]{2,1,0:T(8,128)(2,1)}, bf16[16,50,256]{2,1,0:T(8,128)(2,1)S(1)}, u32[]{:S(2)}, u32[]{:S(2)}) collective-permute-start(bf16[16,50,256]{2,1,0:T(8,128)(2,1)} %get-tuple-element.19), channel_id=1, source_target_pairs={{0,16},{8,24},{16,0},{24,8},{1,17},{9,25},{17,1},{25,9},{2,18},{10... | collective-permute-start | bytes 1228808 | tf_op jit(solution)/shard_map/ppermute | solution.py:27
  172.9 36.3 %collective-permute-start = (bf16[16,50,256]{2,1,0:T(8,128)(2,1)}, bf16[16,50,256]{2,1,0:T(8,128)(2,1)}, u32[]{:S(2)}, u32[]{:S(2)}) collective-permute-start(bf16[16,50,256]{2,1,0:T(8,128)(2,1)} %get-tuple-element.17), channel_id=1, source_target_pairs={{0,8},{8,16},{16,24},{24,0},{1,9},{9,17},{17,25},{25,1},{2,10},{10... | collective-permute-start | bytes 1228808 | tf_op jit(solution)/shard_map/ppermute | solution.py:27
  175.7 16.0 %collective-permute-start.15 = (f32[25,128]{1,0:T(8,128)S(1)}, f32[25,128]{1,0:T(8,128)S(1)}, u32[]{:S(2)}, u32[]{:S(2)}) collective-permute-start(f32[25,128]{1,0:T(8,128)S(1)} %add_add_fusion.2), channel_id=1, source_target_pairs={{0,24},{8,0},{16,8},{24,16},{1,25},{9,1},{17,9},{25,17},{2,26},{10... | collective-permute-start | bytes 38408 | tf_op jit(solution)/shard_map/ppermute | solution.py:34
  180.0 16.6 %collective-permute-start.14 = (f32[25,128]{1,0:T(8,128)S(1)}, f32[25,128]{1,0:T(8,128)S(1)}, u32[]{:S(2)}, u32[]{:S(2)}) collective-permute-start(f32[25,128]{1,0:T(8,128)S(1)} %add_add_fusion.2), channel_id=1, source_target_pairs={{0,16},{8,24},{16,0},{24,8},{1,17},{9,25},{17,1},{25,9},{2,18},{10... | collective-permute-start | bytes 38408 | tf_op jit(solution)/shard_map/ppermute | solution.py:34
  198.9 19.0 %collective-permute-start.18 = (f32[25,128]{1,0:T(8,128)S(1)}, f32[25,128]{1,0:T(8,128)S(1)}, u32[]{:S(2)}, u32[]{:S(2)}) collective-permute-start(f32[25,128]{1,0:T(8,128)S(1)} %add_add_fusion.1), channel_id=1, source_target_pairs={{0,96},{32,0},{64,32},{96,64},{128,224},{160,128},{192,160},{224,1... | collective-permute-start | bytes 38408 | tf_op jit(solution)/shard_map/ppermute | solution.py:34
  203.9 15.9 %collective-permute-start.17 = (f32[25,128]{1,0:T(8,128)S(1)}, f32[25,128]{1,0:T(8,128)S(1)}, u32[]{:S(2)}, u32[]{:S(2)}) collective-permute-start(f32[25,128]{1,0:T(8,128)S(1)} %add_add_fusion.1), channel_id=1, source_target_pairs={{0,64},{32,96},{64,0},{96,32},{128,192},{160,224},{192,128},{224,1... | collective-permute-start | bytes 38408 | tf_op jit(solution)/shard_map/ppermute | solution.py:34
  205.9 14.0 %collective-permute-start.16 = (f32[25,128]{1,0:T(8,128)S(1)}, f32[25,128]{1,0:T(8,128)S(1)}, u32[]{:S(2)}, u32[]{:S(2)}) collective-permute-start(f32[25,128]{1,0:T(8,128)S(1)} %add_add_fusion.1), channel_id=1, source_target_pairs={{0,32},{32,64},{64,96},{96,0},{128,160},{160,192},{192,224},{224,1... | collective-permute-start | bytes 38408 | tf_op jit(solution)/shard_map/ppermute | solution.py:34
  210.6 23.5 %collective-permute-start.5 = (bf16[4,50,256]{2,1,0:T(8,128)(2,1)S(1)}, bf16[4,50,256]{2,1,0:T(8,128)(2,1)S(1)}, u32[]{:S(2)}, u32[]{:S(2)}) collective-permute-start(bf16[4,50,256]{2,1,0:T(8,128)(2,1)S(1)} %get-tuple-element.21), channel_id=1, source_target_pairs={{0,96},{32,0},{64,32},{96,64},{128,224},{160,128},{192,160},{224,1... | collective-permute-start | bytes 307208 | tf_op jit(solution)/shard_map/ppermute | solution.py:27
  214.9 25.4 %collective-permute-start.4 = (bf16[4,50,256]{2,1,0:T(8,128)(2,1)S(1)}, bf16[4,50,256]{2,1,0:T(8,128)(2,1)S(1)}, u32[]{:S(2)}, u32[]{:S(2)}) collective-permute-start(bf16[4,50,256]{2,1,0:T(8,128)(2,1)S(1)} %get-tuple-element.22), channel_id=1, source_target_pairs={{0,64},{32,96},{64,0},{96,32},{128,192},{160,224},{192,128},{224,1... | collective-permute-start | bytes 307208 | tf_op jit(solution)/shard_map/ppermute | solution.py:27
  217.9 22.4 %collective-permute-start.3 = (bf16[4,50,256]{2,1,0:T(8,128)(2,1)S(1)}, bf16[4,50,256]{2,1,0:T(8,128)(2,1)S(1)}, u32[]{:S(2)}, u32[]{:S(2)}) collective-permute-start(bf16[4,50,256]{2,1,0:T(8,128)(2,1)S(1)} %get-tuple-element.20), channel_id=1, source_target_pairs={{0,32},{32,64},{64,96},{96,0},{128,160},{160,192},{192,224},{224,1... | collective-permute-start | bytes 307208 | tf_op jit(solution)/shard_map/ppermute | solution.py:27
  219.9 30.5 %collective-permute-start.21 = (f32[25,128]{1,0:T(8,128)S(1)}, f32[25,128]{1,0:T(8,128)S(1)}, u32[]{:S(2)}, u32[]{:S(2)}) collective-permute-start(f32[25,128]{1,0:T(8,128)S(1)} %add_add_fusion), channel_id=1, source_target_pairs={{0,384},{32,416},{64,448},{96,480},{128,0},{160,32},{192,64},{224,... | collective-permute-start | bytes 38408 | tf_op jit(solution)/shard_map/ppermute | solution.py:34
  225.9 28.2 %collective-permute-start.20 = (f32[25,128]{1,0:T(8,128)S(1)}, f32[25,128]{1,0:T(8,128)S(1)}, u32[]{:S(2)}, u32[]{:S(2)}) collective-permute-start(f32[25,128]{1,0:T(8,128)S(1)} %add_add_fusion), channel_id=1, source_target_pairs={{0,256},{32,288},{64,320},{96,352},{128,384},{160,416},{192,448},{... | collective-permute-start | bytes 38408 | tf_op jit(solution)/shard_map/ppermute | solution.py:34
  234.1 20.1 %collective-permute-start.19 = (f32[25,128]{1,0:T(8,128)S(1)}, f32[25,128]{1,0:T(8,128)S(1)}, u32[]{:S(2)}, u32[]{:S(2)}) collective-permute-start(f32[25,128]{1,0:T(8,128)S(1)} %add_add_fusion), channel_id=1, source_target_pairs={{0,128},{32,160},{64,192},{96,224},{128,256},{160,288},{192,320},{... | collective-permute-start | bytes 38408 | tf_op jit(solution)/shard_map/ppermute | solution.py:34
  240.4 14.3 %collective-permute-start.8 = (f32[50,256]{1,0:T(8,128)S(1)}, f32[50,256]{1,0:T(8,128)S(1)}, u32[]{:S(2)}, u32[]{:S(2)}) collective-permute-start(f32[50,256]{1,0:T(8,128)S(1)} %get-tuple-element.24), channel_id=1, source_target_pairs={{0,384},{32,416},{64,448},{96,480},{128,0},{160,32},{192,64},{224,... | collective-permute-start | bytes 153608 | tf_op jit(solution)/shard_map/ppermute | solution.py:27
  244.0 17.9 %collective-permute-start.7 = (f32[50,256]{1,0:T(8,128)S(1)}, f32[50,256]{1,0:T(8,128)S(1)}, u32[]{:S(2)}, u32[]{:S(2)}) collective-permute-start(f32[50,256]{1,0:T(8,128)S(1)} %get-tuple-element.25), channel_id=1, source_target_pairs={{0,256},{32,288},{64,320},{96,352},{128,384},{160,416},{192,448},{... | collective-permute-start | bytes 153608 | tf_op jit(solution)/shard_map/ppermute | solution.py:27
  (5 other events, 113.3 us)
Sparse Core Ops, SparseCore 0:
  46.7 34.7 all-gather.7
  83.6 38.1 all-gather.5

commit v2 on v0

v2 whole, which is shorter than its diff:
```python
import math

import jax
import jax.numpy as jnp
from jax import lax
from jax.experimental import pallas as pl
from jax.experimental.pallas import tpu as pltpu
from jax.sharding import Mesh
from jax.sharding import PartitionSpec as P

BLOCK = 128
F32 = jnp.float32
BF16 = jnp.bfloat16
I32 = jnp.int32
Z = ("h", "l")
ROWS_FIRST = (((0,), (0,)), ((), ()))
LANES_LAST = (((1,), (1,)), ((), ()))


def call(kernel, out_shape, args, flops, scalars=0, scratch=(), after=()):
    whole = pl.BlockSpec(memory_space=pltpu.VMEM)
    count, more = len(args), len(after)

    def body(*refs):
        kernel(*refs[:count], *refs[count + more :])

    specs = [pl.BlockSpec(memory_space=pltpu.SMEM)] * scalars + [whole] * (count - scalars)
    return pl.pallas_call(
        body,
        out_shape=out_shape,
        in_specs=specs + [pl.BlockSpec(memory_space=pl.ANY)] * more,
        out_specs=jax.tree.map(lambda _: whole, out_shape),
        scratch_shapes=list(scratch),
        compiler_params=pltpu.CompilerParams(vmem_limit_bytes=48 * 2**20),
        cost_estimate=pl.CostEstimate(flops=flops, bytes_accessed=4 * 2**20, transcendentals=0),
    )(*args, *after)


def swap_matrix(inner, outer, capacity, dtype):
    size = inner * outer * capacity
    row = lax.broadcasted_iota(I32, (size, size), 0)
    col = lax.broadcasted_iota(I32, (size, size), 1)
    o, i, a = row // (inner * capacity), (row // capacity) % inner, row % capacity
    return (col == (i * outer + o) * capacity + a).astype(dtype)


def context_kernel(owners, encoders, capacity, place, stored, scale, *refs):
    sends, send = refs[:-1], refs[-1]
    group = 8
    slab = group * capacity
    matrix = swap_matrix(owners, group, capacity, BF16)
    parts = []
    for b in range(scale.shape[1]):
        part = stored[:, b * BLOCK : (b + 1) * BLOCK].astype(F32) * scale[:, b : b + 1]
        parts.append(part.astype(BF16))
    context = jnp.concatenate(parts, axis=1)
    block = owners * capacity
    for g in range(encoders // group):
        picked = [context[(l * encoders + g * group) * capacity :][:slab] for l in range(owners)]
        moved = jnp.dot(matrix, jnp.concatenate(picked, axis=0), preferred_element_type=F32).astype(BF16)
        for e in range(group):
            z, y = divmod(g * group + e, send.shape[0])
            send[y, z] = moved[e * block : (e + 1) * block, :]
    for k, out in enumerate(sends):
        out[...] = send[lax.rem(place[1] + k, len(sends))]


def rows_kernel(capacity, own_owner, rows, target_col, target_row, mine):
    count, features = rows.shape
    earlier = lax.broadcasted_iota(I32, (count, count), 1) < lax.broadcasted_iota(I32, (count, count), 0)
    same = jnp.where((target_col[...] == target_row[...]) & earlier, 1.0, 0.0)
    arrival = jnp.sum(same, axis=1, keepdims=True)
    low = arrival + (own_owner[0] * capacity).astype(F32)
    lane = lax.broadcasted_iota(I32, (count, BLOCK), 1)
    tail = jnp.where(lane == 0, target_col[...].astype(F32), jnp.where(lane == 1, low, 0.0))
    mine[:, :features] = rows[...]
    mine[:, features:] = tail.astype(BF16)


def stack_kernel(*refs):
    out, count = refs[-1], refs[0].shape[0]
    for k, ref in enumerate(refs[:-1]):
        out[k * count : (k + 1) * count, :] = ref[...]


def selection(tail, per_target, slot_count):
    tail = tail.astype(F32)
    slot = (tail[:, 0:1] * per_target + tail[:, 1:2]).astype(I32)
    lanes = lax.broadcasted_iota(I32, (tail.shape[0], slot_count), 1)
    return (lanes == slot).astype(BF16)


def outer_kernel(nz, ny, per_target, place, slots, *refs):
    gathered, (kept, *sends), (total, ordered) = refs[: -ny - 2], refs[-ny - 2 : -2], refs[-2:]
    features, width = total.shape
    own = features // (nz * ny)
    slot_count = slots.shape[0]
    contexts = []
    for rows in gathered:
        select = selection(rows[:, features:], per_target, slot_count)
        contexts.append(jnp.dot(select, slots[...], preferred_element_type=F32).astype(BF16))
    step = 5 * BLOCK
    for i in range(features // step):
        part = 0.0
        for rows, context in zip(gathered, contexts):
            part += lax.dot_general(rows[:, i * step : (i + 1) * step], context, ROWS_FIRST, preferred_element_type=F32)
        total[i * step : (i + 1) * step, :] = part
    for z in range(nz):
        for y in range(ny):
            ordered[y, z * own : (z + 1) * own, :] = total[(z * ny + y) * own : (z * ny + y + 1) * own, :]
    kept[...] = ordered[place[1]]
    for k, send in enumerate(sends, 1):
        send[...] = ordered[lax.rem(place[1] + k, ny)].astype(BF16)


def back_kernel(nz, ny, per_target, place, scale, w0, w1, w2, w3, *refs):
    gathered, (out, wide, weights) = refs[:-3], refs[-3:]
    features, width = weights.shape
    own = features // (nz * ny)
    here_y = place[1]
    for k, piece in enumerate((w0, w1, w2, w3)):
        y = lax.rem(here_y + ny - k, ny)
        wide[pl.ds(y, 1)] = piece[...].astype(F32)[None]
    for z in range(nz):
        for y in range(ny):
            at = (z * ny + y) * own
            weights[at : at + own, :] = wide[y, z]
    slot_count = out.shape[0]
    step = 5 * BLOCK
    total = jnp.zeros((slot_count, width), F32)
    for rows in gathered:
        live = jnp.zeros((rows.shape[0], width), F32)
        for i in range(features // step):
            cut = slice(i * step, (i + 1) * step)
            scaled = (rows[:, cut].astype(F32) * scale[:, cut]).astype(BF16)
            live += jnp.dot(scaled, weights[cut, :].astype(BF16), preferred_element_type=F32)
        select = selection(rows[:, features:], per_target, slot_count)
        total += lax.dot_general(select, live.astype(BF16), ROWS_FIRST, preferred_element_type=F32)
    out[...] = total.astype(BF16)


def both_terms(value):
    high = value.astype(BF16).astype(F32)
    return jnp.concatenate([high, value - high], axis=0).astype(BF16)


def fold_y_kernel(nz, own, groups, place, kept, r1, r2, r3, by_z, near_kept, scale_kept, *rest):
    sends, (blocks, product) = rest[:-2], rest[-2:]
    padded = product.shape[0] // nz
    width = product.shape[1]
    members = nz // groups
    total = kept[...]
    for part in (r1, r2, r3):
        total += part[...].astype(F32)
    product[...] = jnp.zeros_like(product)
    for z in range(nz):
        block = total[z * own : (z + 1) * own, :]
        blocks[z] = block
        weight = by_z[z].astype(F32)
        product[z * padded : z * padded + own, :] = block * weight
    rest = product[...]
    ones = jnp.ones((8, width), BF16)
    sums = jnp.zeros((8, nz * padded), F32)
    for _ in range(3):
        piece = rest.astype(BF16)
        rest = rest - piece.astype(F32)
        sums += lax.dot_general(ones, piece, LANES_LAST, preferred_element_type=F32)
    scale_kept[...] = jnp.zeros_like(scale_kept)
    for j in range(-(-nz * padded // width)):
        row = sums[0:1, j * width : (j + 1) * width]
        scale_kept[j : j + 1, : row.shape[1]] = row
    both = both_terms(scale_kept[...])
    low = lax.rem(place[0], members)
    for h in range(groups):
        near_kept[h] = blocks[h * members + low]
    for k, send in enumerate(sends, 1):
        there = lax.rem(low + k, members)
        for h in range(groups):
            send[h] = blocks[h * members + there].astype(BF16)
        send[groups] = jnp.zeros_like(send[groups])
        send[groups, : both.shape[0], :] = both


def fold_low_kernel(near_kept, scale_kept, r1, r2, r3, out):
    groups, own, width = near_kept.shape
    lines = scale_kept.shape[0]
    scale = scale_kept[...]
    for part in (r1, r2, r3):
        both = part[groups, : 2 * lines, :].astype(F32)
        scale = scale + (both[:lines] + both[lines:])
    for h in range(groups):
        total = near_kept[h]
        for part in (r1, r2, r3):
            total += part[h].astype(F32)
        out[h, :own, :] = total
        out[h, own : out.shape[1] - lines, :] = jnp.zeros((out.shape[1] - lines - own, width), F32)
        out[h, out.shape[1] - lines :, :] = scale


def fold_high_kernel(factor, parts, gain, out, scale_out):
    total = parts[0]
    for h in range(1, parts.shape[0]):
        total += parts[h]
    own, lines = out.shape[0], scale_out.shape[1]
    out[...] = total[:own] * (gain[...] * factor)
    for k in range(scale_out.shape[0]):
        scale_out[k] = total[total.shape[0] - lines :]


def spread_kernel(source, out):
    for k in range(out.shape[0]):
        out[k] = source[...]


def collect_kernel(place, *refs):
    parts, out = refs[:-1], refs[-1]
    for k, part in enumerate(parts):
        y = lax.rem(place[1] + len(parts) - k, len(parts))
        for z in range(out.shape[0]):
            out[z, y] = part[z]


def share_kernel(place, source, kept, *sends):
    count = source.shape[1]
    for k, out in enumerate((kept,) + sends):
        there = lax.rem(place[1] + k, count)
        for z in range(source.shape[0]):
            out[z] = source[z, there]


def unswap_kernel(owners, capacity, place, *refs):
    parts, (out, ordered) = refs[:-2], refs[-2:]
    ny, nz, width = len(parts), ordered.shape[0], ordered.shape[3]
    encoders = nz * ny
    for k, part in enumerate(parts):
        y = lax.rem(place[1] + ny - k, ny)
        for z in range(nz):
            ordered[z, y] = part[z]
    group = 8
    slab = group * capacity
    matrix = swap_matrix(group, owners, capacity, BF16)
    for g in range(encoders // group):
        picked = [ordered[(g * group + e) // ny, (g * group + e) % ny] for e in range(group)]
        moved = jnp.dot(matrix, jnp.concatenate(picked, axis=0), preferred_element_type=F32).astype(BF16)
        for l in range(owners):
            at = (l * encoders + g * group) * capacity
            out[at : at + slab, :] = moved[l * slab : (l + 1) * slab, :]


def shifted(value, axis, size, shift):
    return lax.ppermute(value, axis, [(i, (i + shift) % size) for i in range(size)])


def all_to_all(value, axes):
    return lax.all_to_all(value, axes, split_axis=0, concat_axis=0, tiled=True)


def on_device(grad_rows, row_target, stored_context, block_scale, w_out, layer_scale):
    nz, ny, nx, nc = (lax.axis_size(a) for a in (Z, "y", "x", "c"))
    encoders, owners = nz * ny, nx * nc
    source_rows, features = grad_rows.shape
    slot_count, width = stored_context.shape
    capacity = slot_count // (encoders * owners)
    own = features // encoders
    per_target = owners * capacity
    shape = jax.ShapeDtypeStruct
    owner = lax.axis_index(("x", "c")).reshape(1)
    place = jnp.stack([lax.axis_index(Z), lax.axis_index("y")])

    send = call(
        lambda *args: context_kernel(owners, encoders, capacity, *args),
        [shape((nz, per_target, width), BF16)] * ny, (place, stored_context, block_scale), flops=10**8, scalars=1,
        scratch=[pltpu.VMEM((ny, nz, per_target, width), BF16)],
    )
    weights = all_to_all(
        call(spread_kernel, shape((nz, own, width), BF16), (w_out.T,), flops=10**6, after=(send[0],)), Z,
    )
    sent = [send[0]] + [shifted(part, "y", ny, k) for k, part in enumerate(send[1:], 1)]
    received = sent[1:]
    sent = call(
        collect_kernel, shape((nz, ny, per_target, width), BF16), (place, *sent), flops=10**8, scalars=1, after=(weights,),
    )
    slots = all_to_all(sent, Z).reshape(slot_count, width)

    wide = features + BLOCK
    mine = call(
        lambda *args: rows_kernel(capacity, *args),
        shape((source_rows, wide), BF16), (owner, grad_rows, row_target, row_target.reshape(1, source_rows)),
        flops=10**8, scalars=1, after=received,
    )
    near = call(
        stack_kernel, shape((nx * source_rows, wide), BF16), [mine] + [shifted(mine, "x", nx, k) for k in range(1, nx)],
        flops=10**8, after=(weights,),
    )
    rows = [near, shifted(near, "c", nc, 1)]
    pieces = [weights] + [shifted(weights, "y", ny, k) for k in range(1, ny)]

    share = nz * own
    kept, *sends = call(
        lambda *args: outer_kernel(nz, ny, per_target, *args),
        [shape((share, width), F32)] + [shape((share, width), BF16)] * (ny - 1),
        (place, slots, *rows), flops=10**9, scalars=1,
        scratch=[pltpu.VMEM((features, width), F32), pltpu.VMEM((ny, share, width), F32)],
    )
    parts = [shifted(send, "y", ny, k) for k, send in enumerate(sends, 1)]

    back = call(
        lambda *args: back_kernel(nz, ny, per_target, *args),
        shape((slot_count, width), BF16),
        (place, layer_scale.reshape(1, features), *pieces, *rows), flops=2 * 10**9, scalars=1, after=(kept,),
        scratch=[pltpu.VMEM((ny, nz, own, width), F32), pltpu.VMEM((features, width), F32)],
    )
    returned = all_to_all(back.reshape(nz, ny, per_target, width), Z)
    sends = call(
        share_kernel, [shape((nz, per_target, width), BF16)] * ny, (place, returned), flops=10**8, scalars=1,
    )
    sends = [sends[0]] + [shifted(send, "y", ny, k) for k, send in enumerate(sends[1:], 1)]
    grad_context = call(
        lambda *args: unswap_kernel(owners, capacity, *args),
        shape((slot_count, width), BF16), (place, *sends), flops=10**8, scalars=1,
        scratch=[pltpu.VMEM((nz, ny, per_target, width), BF16)],
    )

    groups = lax.axis_size("h")
    members = nz // groups
    padded = -(-own // 8) * 8
    lines = -(-nz * padded // width)
    low, low_scale, *sends = call(
        lambda *args: fold_y_kernel(nz, own, groups, *args),
        [shape((groups, own, width), F32), shape((lines, width), F32)]
        + [shape((groups + 1, own, width), BF16)] * (members - 1),
        (place, kept, *parts, weights), flops=2 * 10**11, scalars=1,
        scratch=[pltpu.VMEM((nz, own, width), F32), pltpu.VMEM((nz * padded, width), F32)],
    )
    parts = [shifted(send, "l", members, k) for k, send in enumerate(sends, 1)]
    rows_sent = -(-(own + lines) // 8) * 8
    total = call(
        fold_low_kernel, shape((groups, rows_sent, width), F32), (low, low_scale, *parts), flops=10**11, after=(returned,),
    )
    rescale = 1.0 / math.sqrt(source_rows * encoders * owners)
    at = lax.axis_index(Z + ("y",)) * own
    own_scale = lax.dynamic_slice(layer_scale, (at,), (own,))
    grad_weight, scale_part = call(
        lambda *args: fold_high_kernel(rescale, *args),
        [shape((own, width), F32), shape((ny * owners, lines, width), F32)],
        (all_to_all(total, "h"), own_scale.reshape(own, 1)), flops=10**8,
    )
    scale_part = all_to_all(scale_part, ("y", "x", "c")).reshape(ny, owners, lines * width)[:, :, : nz * padded]
    scale_part = jnp.sum(scale_part, axis=1).reshape(ny, nz, padded)[:, :, :own]
    grad_scale = scale_part.transpose(1, 0, 2).reshape(features) * rescale
    return (grad_context, grad_weight, grad_scale)


def solution(mesh):
    finer = Mesh(mesh.devices.reshape(4, 4, 4, 4, 2), Z + ("y", "x", "c"))
    edata, llm = Z + ("y",), ("x", "c")
    in_specs = (
        P(edata + llm, None),
        P(edata + llm, None),
        P(edata, llm),
        P(edata, llm),
        P(llm, edata),
        P(),
    )
    out_specs = (P(edata, llm), P(edata, llm), P())
    return jax.shard_map(
        on_device, mesh=finer, in_specs=in_specs, out_specs=out_specs, check_vma=False
    )
```

time: 549 us -> 195 us (0.36)
  blocking collectives: 269 us -> 0 us
  waiting for transfers between devices: 189 us -> 32.4 us
  starting transfers between devices: 42.1 us -> 130 us
  Pallas kernels: 0 us -> 18.3 us
  between operations: 14.9 us -> 1.09 us
  matrix products: 13.6 us -> 0 us
    all_gather x2 -> x0, waiting for transfers between devices: 146 us -> none  [the longest x1 92.2 us: on_device(): weights = lax.all_gather(w_out, 'edata', axis=1, tiled=True)]
    unnamed x1 -> x0, blocking collectives: 140 us -> none
    psum x1 -> x0, blocking collectives: 129 us -> none  [on_device(): grad_scale = lax.psum(partial_scale, ('edata', 'llm')) * rescale]
    ppermute x0 -> x19, starting transfers between devices: none -> 66.7 us  [shifted(): lax.ppermute(value, axis, [(i, (i + shift) % size) for i in range(size)])]
    all_to_all x1 -> x5, starting transfers between devices: 19.3 us -> 63 us  [all_to_all(): return lax.all_to_all(value, axes, split_axis=0, concat_axis=0, tiled=True)]
    all_to_all x1 -> x5, waiting for transfers between devices: 41.8 us -> 7.93 us  [all_to_all(): return lax.all_to_all(value, axes, split_axis=0, concat_axis=0, tiled=True)]
    ppermute x0 -> x19, waiting for transfers between devices: none -> 24.5 us  [shifted(): lax.ppermute(value, axis, [(i, (i + shift) % size) for i in range(size)])]
    unnamed x7 -> x0, starting transfers between devices: 22.7 us -> none
  transfers between devices with their start and end apart: 10 -> 24, of which waited for: 4 -> 8; matrix products, arithmetic and copies ran while one was open for 3% -> 1% of each run, Pallas kernels for 0% -> 8%
where the time goes in v2:
time: 195 us; the launch traced here: 193 us
  starting transfers between devices  130 us (67%)
  waiting for transfers between devices  32.4 us (17%)
  Pallas kernels  18.3 us (9%)
  local copies, waits for them, and re-layouts  10.9 us (6%)
    ppermute x19, starting transfers between devices, shifted(): lax.ppermute(value, axis, [(i, (i + shift) % size) for i in range(size)])  66.7 us
    all_to_all x5, starting transfers between devices, all_to_all(): return lax.all_to_all(value, axes, split_axis=0, concat_axis=0, tiled=True)  63 us
    ppermute x19, waiting for transfers between devices, shifted(): lax.ppermute(value, axis, [(i, (i + shift) % size) for i in range(size)])  24.5 us
    pallas_call x12, Pallas kernels, call(): pl.pallas_call(body, out_shape=out_shape, in_specs=specs + [pl.BlockSpec(...  18.3 us
    unnamed x24, local copies, waits for them, and re-layouts  9.06 us
    all_to_all x5, waiting for transfers between devices, all_to_all(): return lax.all_to_all(value, axes, split_axis=0, concat_axis=0, tiled=True)  7.93 us
  transfers between devices with their start and end apart: 24, of which 8 were waited for; matrix products, arithmetic and copies ran while one was open for 1% of the time, Pallas kernels for 8%

profile of v2, /device:TPU:1, one launch (start us, length us, event | category | flops | bytes accessed | tf_op | source)
XLA Modules:
  0.0 192.6 jit_solution(10007115580545451133)
XLA Ops:
  5.4 15.7 %all-to-all-start = ((bf16[16,50,256]{2,1,0:T(8,128)(2,1)}), bf16[16,50,256]{2,1,0:T(8,128)(2,1)S(1)}, u32[]{:S(2)}, u32[]{:S(2)}) async-start(bf16[16,50,256]{2,1,0:T(8,128)(2,1)} %shard_map.86), calls=%async_computation | async-start | bytes 917504 | tf_op jit(solution)/shard_map/all_to_all | solution.py:255
  21.2 3.2 %collective-permute-start.3 = (bf16[16,16,256]{2,1,0:T(8,128)(2,1)S(1)}, bf16[16,16,256]{2,1,0:T(8,128)(2,1)S(1)}, u32[]{:S(2)}, u32[]{:S(2)}) collective-permute-start(bf16[16,16,256]{2,1,0:T(8,128)(2,1)S(1)} %get-tuple-element.23), channel_id=1, source_target_pairs={{0,8},{8,16},{16,24},{24,0},{1,9},{9,17},{17,25},{25,1},{2,10},{10... | collective-permute-start | bytes 393224 | tf_op jit(solution)/shard_map/ppermute | solution.py:251
  24.4 4.5 %collective-permute-start.4 = (bf16[16,16,256]{2,1,0:T(8,128)(2,1)S(1)}, bf16[16,16,256]{2,1,0:T(8,128)(2,1)S(1)}, u32[]{:S(2)}, u32[]{:S(2)}) collective-permute-start(bf16[16,16,256]{2,1,0:T(8,128)(2,1)S(1)} %get-tuple-element.24), channel_id=1, source_target_pairs={{0,16},{8,24},{16,0},{24,8},{1,17},{9,25},{17,1},{25,9},{2,18},{10... | collective-permute-start | bytes 393224 | tf_op jit(solution)/shard_map/ppermute | solution.py:251
  28.9 3.0 %collective-permute-start.5 = (bf16[16,16,256]{2,1,0:T(8,128)(2,1)S(1)}, bf16[16,16,256]{2,1,0:T(8,128)(2,1)S(1)}, u32[]{:S(2)}, u32[]{:S(2)}) collective-permute-start(bf16[16,16,256]{2,1,0:T(8,128)(2,1)S(1)} %get-tuple-element.25), channel_id=1, source_target_pairs={{0,24},{8,0},{16,8},{24,16},{1,25},{9,1},{17,9},{25,17},{2,26},{10... | collective-permute-start | bytes 393224 | tf_op jit(solution)/shard_map/ppermute | solution.py:251
  35.1 3.1 %collective-permute-start.6 = (bf16[64,3328]{1,0:T(8,128)(2,1)S(1)}, bf16[64,3328]{1,0:T(8,128)(2,1)S(1)}, u32[]{:S(2)}, u32[]{:S(2)}) collective-permute-start(bf16[64,3328]{1,0:T(8,128)(2,1)S(1)} %shard_map.87.refs_0_), channel_id=1, source_target_pairs={{0,2},{2,4},{4,6},{6,0},{1,3},{3,5},{5,7},{7,1},{8,10},{10,12},{12... | collective-permute-start | bytes 1277960 | tf_op jit(solution)/shard_map/ppermute | solution.py:251
  38.2 4.4 %collective-permute-start.7 = (bf16[64,3328]{1,0:T(8,128)(2,1)S(1)}, bf16[64,3328]{1,0:T(8,128)(2,1)S(1)}, u32[]{:S(2)}, u32[]{:S(2)}) collective-permute-start(bf16[64,3328]{1,0:T(8,128)(2,1)S(1)} %shard_map.87.refs_0_), channel_id=1, source_target_pairs={{0,4},{2,6},{4,0},{6,2},{1,5},{3,7},{5,1},{7,3},{8,12},{10,14},{12... | collective-permute-start | bytes 1277960 | tf_op jit(solution)/shard_map/ppermute | solution.py:251
  42.6 3.1 %collective-permute-start.8 = (bf16[64,3328]{1,0:T(8,128)(2,1)S(1)}, bf16[64,3328]{1,0:T(8,128)(2,1)S(1)}, u32[]{:S(2)}, u32[]{:S(2)}) collective-permute-start(bf16[64,3328]{1,0:T(8,128)(2,1)S(1)} %shard_map.87.refs_0_), channel_id=1, source_target_pairs={{0,6},{2,0},{4,2},{6,4},{1,7},{3,1},{5,3},{7,5},{8,14},{10,8},{12,... | collective-permute-start | bytes 1277960 | tf_op jit(solution)/shard_map/ppermute | solution.py:251
  47.0 11.5 %all-to-all-start.1 = ((bf16[16,4,16,256]{3,2,1,0:T(8,128)(2,1)}), bf16[16,4,16,256]{3,2,1,0:T(8,128)(2,1)S(1)}, u32[]{:S(2)}, u32[]{:S(2)}) async-start(bf16[16,4,16,256]{3,2,1,0:T(8,128)(2,1)} %shard_map.89), calls=%async_computation.1 | async-start | bytes 1048576 | tf_op jit(solution)/shard_map/all_to_all | solution.py:255
  62.9 5.0 %collective-permute-start.9 = (bf16[256,3328]{1,0:T(8,128)(2,1)S(1)}, bf16[256,3328]{1,0:T(8,128)(2,1)S(1)}, u32[]{:S(2)}, u32[]{:S(2)}) collective-permute-start(bf16[256,3328]{1,0:T(8,128)(2,1)S(1)} %shard_map.88.refs_2_.refs_6_), channel_id=1, source_target_pairs={{0,1},{1,0},{2,3},{3,2},{4,5},{5,4},{6,7},{7,6},{8,9},{9,8},{10,11... | collective-permute-start | bytes 5111816 | tf_op jit(solution)/shard_map/ppermute | solution.py:251
  70.4 4.8 %collective-permute-start.1 = (bf16[16,50,256]{2,1,0:T(8,128)(2,1)S(1)}, bf16[16,50,256]{2,1,0:T(8,128)(2,1)}, u32[]{:S(2)}, u32[]{:S(2)}) collective-permute-start(bf16[16,50,256]{2,1,0:T(8,128)(2,1)S(1)} %all-to-all-done.refs_4_.refs_5_.refs_2_), channel_id=1, source_target_pairs={{0,16},{8,24},{16,0},{24,8},{1,17},{9,25},{17,1},{25,9},{2,18},{10... | collective-permute-start | bytes 1228808 | tf_op jit(solution)/shard_map/ppermute | solution.py:251
  80.6 3.7 %shard_map.90 = (f32[800,256]{1,0:T(8,128)S(1)}, bf16[800,256]{1,0:T(8,128)(2,1)}, bf16[800,256]{1,0:T(8,128)(2,1)}, bf16[800,256]{1,0:T(8,128)(2,1)}) custom-call(s32[2]{0:T(128)S(1)} %pad_add_fusion.refs_0_, bf16[1024,256]{1,0:T(8,128)(2,1)S(1)} %bitcast.11, bf16[256,3328]{1,0:T(8,128)(2,1)S(1)} %shard_map.88.refs_2_.refs_6_, bf16[256,3328]{1,0:T(8,128)(2,1)S(1)} %copy-done.1), custom_call_target="tpu_custom_call" | custom-call | flops 1000000000 | bytes 4194304 | tf_op jit(solution)/shard_map/pallas_call | solution.py:28
  86.9 4.8 %collective-permute-start.14 = (bf16[800,256]{1,0:T(8,128)(2,1)}, bf16[800,256]{1,0:T(8,128)(2,1)}, u32[]{:S(2)}, u32[]{:S(2)}) collective-permute-start(bf16[800,256]{1,0:T(8,128)(2,1)} %get-tuple-element.32), channel_id=1, source_target_pairs={{0,16},{8,24},{16,0},{24,8},{1,17},{9,25},{17,1},{25,9},{2,18},{10... | collective-permute-start | bytes 1228808 | tf_op jit(solution)/shard_map/ppermute | solution.py:251
  91.7 3.7 %collective-permute-start.15 = (bf16[800,256]{1,0:T(8,128)(2,1)}, bf16[800,256]{1,0:T(8,128)(2,1)}, u32[]{:S(2)}, u32[]{:S(2)}) collective-permute-start(bf16[800,256]{1,0:T(8,128)(2,1)} %get-tuple-element.33), channel_id=1, source_target_pairs={{0,24},{8,0},{16,8},{24,16},{1,25},{9,1},{17,9},{25,17},{2,26},{10... | collective-permute-start | bytes 1228808 | tf_op jit(solution)/shard_map/ppermute | solution.py:251
  95.4 4.8 %shard_map.91 = bf16[1024,256]{1,0:T(8,128)(2,1)} custom-call(s32[2]{0:T(128)S(1)} %pad_add_fusion.refs_0_, f32[1,3200]{1,0:T(1,128)S(1)} %reshape.33.refs_1_, bf16[16,50,256]{2,1,0:T(8,128)(2,1)S(1)} %all-to-all-done.refs_4_.refs_5_.refs_2_, bf16[16,50,256]{2,1,0:T(8,128)(2,1)} %collective-permute-done.refs_3_, ...), custom_call_target="tpu_custom_call" | custom-call | flops 2000000000 | bytes 4194304 | tf_op jit(solution)/shard_map/pallas_call | solution.py:28
  100.2 12.5 %all-to-all-start.2 = ((bf16[16,4,16,256]{3,2,1,0:T(8,128)(2,1)}), bf16[16,4,16,256]{3,2,1,0:T(8,128)(2,1)}, u32[]{:S(2)}, u32[]{:S(2)}) async-start(bf16[16,4,16,256]{3,2,1,0:T(8,128)(2,1)} %bitcast.6), calls=%async_computation.2 | async-start | bytes 1048576 | tf_op jit(solution)/shard_map/all_to_all | solution.py:255
  114.8 3.2 %collective-permute-start.16 = (bf16[5,50,256]{2,1,0:T(8,128)(2,1)S(1)}, bf16[5,50,256]{2,1,0:T(8,128)(2,1)S(1)}, u32[]{:S(2)}, u32[]{:S(2)}) collective-permute-start(bf16[5,50,256]{2,1,0:T(8,128)(2,1)S(1)} %get-tuple-element.36), channel_id=1, source_target_pairs={{0,32},{32,64},{64,96},{96,0},{1,33},{33,65},{65,97},{97,1},{2,34}... | collective-permute-start | bytes 384008 | tf_op jit(solution)/shard_map/ppermute | solution.py:251
  118.0 4.0 %collective-permute-start.17 = (bf16[5,50,256]{2,1,0:T(8,128)(2,1)S(1)}, bf16[5,50,256]{2,1,0:T(8,128)(2,1)S(1)}, u32[]{:S(2)}, u32[]{:S(2)}) collective-permute-start(bf16[5,50,256]{2,1,0:T(8,128)(2,1)S(1)} %get-tuple-element.37), channel_id=1, source_target_pairs={{0,64},{32,96},{64,0},{96,32},{1,65},{33,97},{65,1},{97,33},{2,66}... | collective-permute-start | bytes 384008 | tf_op jit(solution)/shard_map/ppermute | solution.py:251
  122.0 3.1 %collective-permute-start.18 = (bf16[5,50,256]{2,1,0:T(8,128)(2,1)S(1)}, bf16[5,50,256]{2,1,0:T(8,128)(2,1)S(1)}, u32[]{:S(2)}, u32[]{:S(2)}) collective-permute-start(bf16[5,50,256]{2,1,0:T(8,128)(2,1)S(1)} %get-tuple-element.38), channel_id=1, source_target_pairs={{0,96},{32,0},{64,32},{96,64},{1,97},{33,1},{65,33},{97,65},{2,98}... | collective-permute-start | bytes 384008 | tf_op jit(solution)/shard_map/ppermute | solution.py:251
  125.1 13.2 %collective-permute-done.16.refs_2_ = bf16[5,50,256]{2,1,0:T(8,128)(2,1)S(1)} collective-permute-done((bf16[5,50,256]{2,1,0:T(8,128)(2,1)S(1)}, bf16[5,50,256]{2,1,0:T(8,128)(2,1)S(1)}, u32[]{:S(2)}, u32[]{:S(2)}) %collective-permute-start.16) | collective-permute-done | bytes 128032 | tf_op jit(solution)/shard_map/ppermute | solution.py:251
  138.3 7.7 %collective-permute-done.17.refs_3_ = bf16[5,50,256]{2,1,0:T(8,128)(2,1)S(1)} collective-permute-done((bf16[5,50,256]{2,1,0:T(8,128)(2,1)S(1)}, bf16[5,50,256]{2,1,0:T(8,128)(2,1)S(1)}, u32[]{:S(2)}, u32[]{:S(2)}) %collective-permute-start.17) | collective-permute-done | bytes 128032 | tf_op jit(solution)/shard_map/ppermute | solution.py:251
  146.8 11.1 %all-to-all-start.3 = ((f32[4,56,256]{2,1,0:T(8,128)}), f32[4,56,256]{2,1,0:T(8,128)S(1)}, u32[]{:S(2)}, u32[]{:S(2)}) async-start(f32[4,56,256]{2,1,0:T(8,128)} %shard_map.95), calls=%async_computation.3 | async-start | bytes 458752 | tf_op jit(solution)/shard_map/all_to_all | solution.py:255
  161.8 5.1 %collective-permute-start.11 = (bf16[16,16,256]{2,1,0:T(8,128)(2,1)S(1)}, bf16[16,16,256]{2,1,0:T(8,128)(2,1)S(1)}, u32[]{:S(2)}, u32[]{:S(2)}) collective-permute-start(bf16[16,16,256]{2,1,0:T(8,128)(2,1)S(1)} %get-tuple-element.29), channel_id=1, source_target_pairs={{0,16},{8,24},{16,0},{24,8},{1,17},{9,25},{17,1},{25,9},{2,18},{10... | collective-permute-start | bytes 393224 | tf_op jit(solution)/shard_map/ppermute | solution.py:251
  171.7 12.3 %all-to-all-start.4 = ((f32[32,4,256]{2,1,0:T(4,128)}), f32[32,4,256]{2,1,0:T(4,128)S(1)}, u32[]{:S(2)}, u32[]{:S(2)}) async-start(f32[32,4,256]{2,1,0:T(4,128)} %get-tuple-element.40), calls=%async_computation.4 | async-start | bytes 262144 | tf_op jit(solution)/shard_map/all_to_all | solution.py:255
  185.7 5.9 %all-to-all-done.4 = f32[32,4,256]{2,1,0:T(4,128)S(1)} async-done(((f32[32,4,256]{2,1,0:T(4,128)}), f32[32,4,256]{2,1,0:T(4,128)S(1)}, u32[]{:S(2)}, u32[]{:S(2)}) %all-to-all-start.4) | async-done | bytes 131104 | tf_op jit(solution)/shard_map/all_to_all | solution.py:255
  (70 shorter events, 38.2 us)
Async XLA Ops:
  5.4 40.2 %all-to-all-start = ((bf16[16,50,256]{2,1,0:T(8,128)(2,1)}), bf16[16,50,256]{2,1,0:T(8,128)(2,1)S(1)}, u32[]{:S(2)}, u32[]{:S(2)}) async-start(bf16[16,50,256]{2,1,0:T(8,128)(2,1)} %shard_map.86), calls=%async_computation | async-start | bytes 917504 | tf_op jit(solution)/shard_map/all_to_all | solution.py:255
  21.2 10.9 %collective-permute-start.3 = (bf16[16,16,256]{2,1,0:T(8,128)(2,1)S(1)}, bf16[16,16,256]{2,1,0:T(8,128)(2,1)S(1)}, u32[]{:S(2)}, u32[]{:S(2)}) collective-permute-start(bf16[16,16,256]{2,1,0:T(8,128)(2,1)S(1)} %get-tuple-element.23), channel_id=1, source_target_pairs={{0,8},{8,16},{16,24},{24,0},{1,9},{9,17},{17,25},{25,1},{2,10},{10... | collective-permute-start | bytes 393224 | tf_op jit(solution)/shard_map/ppermute | solution.py:251
  24.4 8.3 %collective-permute-start.4 = (bf16[16,16,256]{2,1,0:T(8,128)(2,1)S(1)}, bf16[16,16,256]{2,1,0:T(8,128)(2,1)S(1)}, u32[]{:S(2)}, u32[]{:S(2)}) collective-permute-start(bf16[16,16,256]{2,1,0:T(8,128)(2,1)S(1)} %get-tuple-element.24), channel_id=1, source_target_pairs={{0,16},{8,24},{16,0},{24,8},{1,17},{9,25},{17,1},{25,9},{2,18},{10... | collective-permute-start | bytes 393224 | tf_op jit(solution)/shard_map/ppermute | solution.py:251
  28.9 6.0 %collective-permute-start.5 = (bf16[16,16,256]{2,1,0:T(8,128)(2,1)S(1)}, bf16[16,16,256]{2,1,0:T(8,128)(2,1)S(1)}, u32[]{:S(2)}, u32[]{:S(2)}) collective-permute-start(bf16[16,16,256]{2,1,0:T(8,128)(2,1)S(1)} %get-tuple-element.25), channel_id=1, source_target_pairs={{0,24},{8,0},{16,8},{24,16},{1,25},{9,1},{17,9},{25,17},{2,26},{10... | collective-permute-start | bytes 393224 | tf_op jit(solution)/shard_map/ppermute | solution.py:251
  35.1 23.4 %collective-permute-start.6 = (bf16[64,3328]{1,0:T(8,128)(2,1)S(1)}, bf16[64,3328]{1,0:T(8,128)(2,1)S(1)}, u32[]{:S(2)}, u32[]{:S(2)}) collective-permute-start(bf16[64,3328]{1,0:T(8,128)(2,1)S(1)} %shard_map.87.refs_0_), channel_id=1, source_target_pairs={{0,2},{2,4},{4,6},{6,0},{1,3},{3,5},{5,7},{7,1},{8,10},{10,12},{12... | collective-permute-start | bytes 1277960 | tf_op jit(solution)/shard_map/ppermute | solution.py:251
  38.2 20.3 %collective-permute-start.7 = (bf16[64,3328]{1,0:T(8,128)(2,1)S(1)}, bf16[64,3328]{1,0:T(8,128)(2,1)S(1)}, u32[]{:S(2)}, u32[]{:S(2)}) collective-permute-start(bf16[64,3328]{1,0:T(8,128)(2,1)S(1)} %shard_map.87.refs_0_), channel_id=1, source_target_pairs={{0,4},{2,6},{4,0},{6,2},{1,5},{3,7},{5,1},{7,3},{8,12},{10,14},{12... | collective-permute-start | bytes 1277960 | tf_op jit(solution)/shard_map/ppermute | solution.py:251
  42.6 17.4 %collective-permute-start.8 = (bf16[64,3328]{1,0:T(8,128)(2,1)S(1)}, bf16[64,3328]{1,0:T(8,128)(2,1)S(1)}, u32[]{:S(2)}, u32[]{:S(2)}) collective-permute-start(bf16[64,3328]{1,0:T(8,128)(2,1)S(1)} %shard_map.87.refs_0_), channel_id=1, source_target_pairs={{0,6},{2,0},{4,2},{6,4},{1,7},{3,1},{5,3},{7,5},{8,14},{10,8},{12,... | collective-permute-start | bytes 1277960 | tf_op jit(solution)/shard_map/ppermute | solution.py:251
  47.0 32.1 %all-to-all-start.1 = ((bf16[16,4,16,256]{3,2,1,0:T(8,128)(2,1)}), bf16[16,4,16,256]{3,2,1,0:T(8,128)(2,1)S(1)}, u32[]{:S(2)}, u32[]{:S(2)}) async-start(bf16[16,4,16,256]{3,2,1,0:T(8,128)(2,1)} %shard_map.89), calls=%async_computation.1 | async-start | bytes 1048576 | tf_op jit(solution)/shard_map/all_to_all | solution.py:255
  62.9 14.2 %collective-permute-start.9 = (bf16[256,3328]{1,0:T(8,128)(2,1)S(1)}, bf16[256,3328]{1,0:T(8,128)(2,1)S(1)}, u32[]{:S(2)}, u32[]{:S(2)}) collective-permute-start(bf16[256,3328]{1,0:T(8,128)(2,1)S(1)} %shard_map.88.refs_2_.refs_6_), channel_id=1, source_target_pairs={{0,1},{1,0},{2,3},{3,2},{4,5},{5,4},{6,7},{7,6},{8,9},{9,8},{10,11... | collective-permute-start | bytes 5111816 | tf_op jit(solution)/shard_map/ppermute | solution.py:251
  67.9 23.8 %collective-permute-start = (bf16[16,50,256]{2,1,0:T(8,128)(2,1)S(1)}, bf16[16,50,256]{2,1,0:T(8,128)(2,1)}, u32[]{:S(2)}, u32[]{:S(2)}) collective-permute-start(bf16[16,50,256]{2,1,0:T(8,128)(2,1)S(1)} %all-to-all-done.refs_4_.refs_5_.refs_2_), channel_id=1, source_target_pairs={{0,8},{8,16},{16,24},{24,0},{1,9},{9,17},{17,25},{25,1},{2,10},{10... | collective-permute-start | bytes 1228808 | tf_op jit(solution)/shard_map/ppermute | solution.py:251
  70.4 25.0 %collective-permute-start.1 = (bf16[16,50,256]{2,1,0:T(8,128)(2,1)S(1)}, bf16[16,50,256]{2,1,0:T(8,128)(2,1)}, u32[]{:S(2)}, u32[]{:S(2)}) collective-permute-start(bf16[16,50,256]{2,1,0:T(8,128)(2,1)S(1)} %all-to-all-done.refs_4_.refs_5_.refs_2_), channel_id=1, source_target_pairs={{0,16},{8,24},{16,0},{24,8},{1,17},{9,25},{17,1},{25,9},{2,18},{10... | collective-permute-start | bytes 1228808 | tf_op jit(solution)/shard_map/ppermute | solution.py:251
  75.2 20.3 %collective-permute-start.2 = (bf16[16,50,256]{2,1,0:T(8,128)(2,1)S(1)}, bf16[16,50,256]{2,1,0:T(8,128)(2,1)}, u32[]{:S(2)}, u32[]{:S(2)}) collective-permute-start(bf16[16,50,256]{2,1,0:T(8,128)(2,1)S(1)} %all-to-all-done.refs_4_.refs_5_.refs_2_), channel_id=1, source_target_pairs={{0,24},{8,0},{16,8},{24,16},{1,25},{9,1},{17,9},{25,17},{2,26},{10... | collective-permute-start | bytes 1228808 | tf_op jit(solution)/shard_map/ppermute | solution.py:251
  84.3 28.4 %collective-permute-start.13 = (bf16[800,256]{1,0:T(8,128)(2,1)}, bf16[800,256]{1,0:T(8,128)(2,1)S(1)}, u32[]{:S(2)}, u32[]{:S(2)}) collective-permute-start(bf16[800,256]{1,0:T(8,128)(2,1)} %get-tuple-element.31), channel_id=1, source_target_pairs={{0,8},{8,16},{16,24},{24,0},{1,9},{9,17},{17,25},{25,1},{2,10},{10... | collective-permute-start | bytes 1228808 | tf_op jit(solution)/shard_map/ppermute | solution.py:251
  86.9 25.8 %collective-permute-start.14 = (bf16[800,256]{1,0:T(8,128)(2,1)}, bf16[800,256]{1,0:T(8,128)(2,1)}, u32[]{:S(2)}, u32[]{:S(2)}) collective-permute-start(bf16[800,256]{1,0:T(8,128)(2,1)} %get-tuple-element.32), channel_id=1, source_target_pairs={{0,16},{8,24},{16,0},{24,8},{1,17},{9,25},{17,1},{25,9},{2,18},{10... | collective-permute-start | bytes 1228808 | tf_op jit(solution)/shard_map/ppermute | solution.py:251
  91.7 21.0 %collective-permute-start.15 = (bf16[800,256]{1,0:T(8,128)(2,1)}, bf16[800,256]{1,0:T(8,128)(2,1)}, u32[]{:S(2)}, u32[]{:S(2)}) collective-permute-start(bf16[800,256]{1,0:T(8,128)(2,1)} %get-tuple-element.33), channel_id=1, source_target_pairs={{0,24},{8,0},{16,8},{24,16},{1,25},{9,1},{17,9},{25,17},{2,26},{10... | collective-permute-start | bytes 1228808 | tf_op jit(solution)/shard_map/ppermute | solution.py:251
  100.2 45.8 %all-to-all-start.2 = ((bf16[16,4,16,256]{3,2,1,0:T(8,128)(2,1)}), bf16[16,4,16,256]{3,2,1,0:T(8,128)(2,1)}, u32[]{:S(2)}, u32[]{:S(2)}) async-start(bf16[16,4,16,256]{3,2,1,0:T(8,128)(2,1)} %bitcast.6), calls=%async_computation.2 | async-start | bytes 1048576 | tf_op jit(solution)/shard_map/all_to_all | solution.py:255
  114.8 23.5 %collective-permute-start.16 = (bf16[5,50,256]{2,1,0:T(8,128)(2,1)S(1)}, bf16[5,50,256]{2,1,0:T(8,128)(2,1)S(1)}, u32[]{:S(2)}, u32[]{:S(2)}) collective-permute-start(bf16[5,50,256]{2,1,0:T(8,128)(2,1)S(1)} %get-tuple-element.36), channel_id=1, source_target_pairs={{0,32},{32,64},{64,96},{96,0},{1,33},{33,65},{65,97},{97,1},{2,34}... | collective-permute-start | bytes 384008 | tf_op jit(solution)/shard_map/ppermute | solution.py:251
  118.0 28.0 %collective-permute-start.17 = (bf16[5,50,256]{2,1,0:T(8,128)(2,1)S(1)}, bf16[5,50,256]{2,1,0:T(8,128)(2,1)S(1)}, u32[]{:S(2)}, u32[]{:S(2)}) collective-permute-start(bf16[5,50,256]{2,1,0:T(8,128)(2,1)S(1)} %get-tuple-element.37), channel_id=1, source_target_pairs={{0,64},{32,96},{64,0},{96,32},{1,65},{33,97},{65,1},{97,33},{2,66}... | collective-permute-start | bytes 384008 | tf_op jit(solution)/shard_map/ppermute | solution.py:251
  122.0 24.0 %collective-permute-start.18 = (bf16[5,50,256]{2,1,0:T(8,128)(2,1)S(1)}, bf16[5,50,256]{2,1,0:T(8,128)(2,1)S(1)}, u32[]{:S(2)}, u32[]{:S(2)}) collective-permute-start(bf16[5,50,256]{2,1,0:T(8,128)(2,1)S(1)} %get-tuple-element.38), channel_id=1, source_target_pairs={{0,96},{32,0},{64,32},{96,64},{1,97},{33,1},{65,33},{97,65},{2,98}... | collective-permute-start | bytes 384008 | tf_op jit(solution)/shard_map/ppermute | solution.py:251
  146.8 24.2 %all-to-all-start.3 = ((f32[4,56,256]{2,1,0:T(8,128)}), f32[4,56,256]{2,1,0:T(8,128)S(1)}, u32[]{:S(2)}, u32[]{:S(2)}) async-start(f32[4,56,256]{2,1,0:T(8,128)} %shard_map.95), calls=%async_computation.3 | async-start | bytes 458752 | tf_op jit(solution)/shard_map/all_to_all | solution.py:255
  158.9 25.0 %collective-permute-start.10 = (bf16[16,16,256]{2,1,0:T(8,128)(2,1)S(1)}, bf16[16,16,256]{2,1,0:T(8,128)(2,1)S(1)}, u32[]{:S(2)}, u32[]{:S(2)}) collective-permute-start(bf16[16,16,256]{2,1,0:T(8,128)(2,1)S(1)} %get-tuple-element.28), channel_id=1, source_target_pairs={{0,8},{8,16},{16,24},{24,0},{1,9},{9,17},{17,25},{25,1},{2,10},{10... | collective-permute-start | bytes 393224 | tf_op jit(solution)/shard_map/ppermute | solution.py:251
  161.8 22.1 %collective-permute-start.11 = (bf16[16,16,256]{2,1,0:T(8,128)(2,1)S(1)}, bf16[16,16,256]{2,1,0:T(8,128)(2,1)S(1)}, u32[]{:S(2)}, u32[]{:S(2)}) collective-permute-start(bf16[16,16,256]{2,1,0:T(8,128)(2,1)S(1)} %get-tuple-element.29), channel_id=1, source_target_pairs={{0,16},{8,24},{16,0},{24,8},{1,17},{9,25},{17,1},{25,9},{2,18},{10... | collective-permute-start | bytes 393224 | tf_op jit(solution)/shard_map/ppermute | solution.py:251
  167.0 17.0 %collective-permute-start.12 = (bf16[16,16,256]{2,1,0:T(8,128)(2,1)S(1)}, bf16[16,16,256]{2,1,0:T(8,128)(2,1)S(1)}, u32[]{:S(2)}, u32[]{:S(2)}) collective-permute-start(bf16[16,16,256]{2,1,0:T(8,128)(2,1)S(1)} %get-tuple-element.30), channel_id=1, source_target_pairs={{0,24},{8,0},{16,8},{24,16},{1,25},{9,1},{17,9},{25,17},{2,26},{10... | collective-permute-start | bytes 393224 | tf_op jit(solution)/shard_map/ppermute | solution.py:251
  171.7 19.9 %all-to-all-start.4 = ((f32[32,4,256]{2,1,0:T(4,128)}), f32[32,4,256]{2,1,0:T(4,128)S(1)}, u32[]{:S(2)}, u32[]{:S(2)}) async-start(f32[32,4,256]{2,1,0:T(4,128)} %get-tuple-element.40), calls=%async_computation.4 | async-start | bytes 262144 | tf_op jit(solution)/shard_map/all_to_all | solution.py:255
  (11 other events, 88.4 us)

commit v3 on v2

--- a/solution.py
+++ b/solution.py
@@ -31,9 +31,17 @@
         in_specs=specs + [pl.BlockSpec(memory_space=pl.ANY)] * more,
         out_specs=jax.tree.map(lambda _: whole, out_shape),
         scratch_shapes=list(scratch),
-        compiler_params=pltpu.CompilerParams(vmem_limit_bytes=48 * 2**20),
+        compiler_params=pltpu.CompilerParams(vmem_limit_bytes=20 * 2**20),
         cost_estimate=pl.CostEstimate(flops=flops, bytes_accessed=4 * 2**20, transcendentals=0),
     )(*args, *after)
+
+
+def for_each(index, count, body):
+    for value in range(count):
+
+        @pl.when(index == value)
+        def _(value=value):
+            body(value)
 
 
 def swap_matrix(inner, outer, capacity, dtype):
@@ -91,40 +99,45 @@
 
 
 def outer_kernel(nz, ny, per_target, place, slots, *refs):
-    gathered, (kept, *sends), (total, ordered) = refs[: -ny - 2], refs[-ny - 2 : -2], refs[-2:]
-    features, width = total.shape
-    own = features // (nz * ny)
-    slot_count = slots.shape[0]
-    contexts = []
-    for rows in gathered:
-        select = selection(rows[:, features:], per_target, slot_count)
-        contexts.append(jnp.dot(select, slots[...], preferred_element_type=F32).astype(BF16))
+    gathered, (kept, *sends), ordered = refs[: -ny - 1], refs[-ny - 1 : -1], refs[-1]
+    share, width = kept.shape
+    features, own = share * ny, share // nz
+    selects = [selection(rows[:, features:], per_target, slots.shape[0]) for rows in gathered]
+    contexts = [jnp.dot(select, slots[...], preferred_element_type=F32).astype(BF16) for select in selects]
     step = 5 * BLOCK
-    for i in range(features // step):
+    for at in range(0, features, step):
         part = 0.0
         for rows, context in zip(gathered, contexts):
-            part += lax.dot_general(rows[:, i * step : (i + 1) * step], context, ROWS_FIRST, preferred_element_type=F32)
-        total[i * step : (i + 1) * step, :] = part
-    for z in range(nz):
-        for y in range(ny):
-            ordered[y, z * own : (z + 1) * own, :] = total[(z * ny + y) * own : (z * ny + y + 1) * own, :]
-    kept[...] = ordered[place[1]]
-    for k, send in enumerate(sends, 1):
-        send[...] = ordered[lax.rem(place[1] + k, ny)].astype(BF16)
+            part += lax.dot_general(rows[:, at : at + step], context, ROWS_FIRST, preferred_element_type=F32)
+        first = at
+        while first < at + step:
+            block, row = divmod(first, own)
+            count = min(own - row, at + step - first)
+            z, y = divmod(block, ny)
+            ordered[y, z * own + row : z * own + row + count, :] = part[first - at : first - at + count, :]
+            first += count
+
+    def hand_out(y):
+        kept[...] = ordered[y]
+        for k, send in enumerate(sends, 1):
+            send[...] = ordered[(y + k) % ny].astype(BF16)
+
+    for_each(place[1], ny, hand_out)
 
 
 def back_kernel(nz, ny, per_target, place, scale, w0, w1, w2, w3, *refs):
-    gathered, (out, wide, weights) = refs[:-3], refs[-3:]
+    gathered, (out, weights) = refs[:-2], refs[-2:]
     features, width = weights.shape
     own = features // (nz * ny)
-    here_y = place[1]
-    for k, piece in enumerate((w0, w1, w2, w3)):
-        y = lax.rem(here_y + ny - k, ny)
-        wide[pl.ds(y, 1)] = piece[...].astype(F32)[None]
-    for z in range(nz):
-        for y in range(ny):
-            at = (z * ny + y) * own
-            weights[at : at + own, :] = wide[y, z]
+
+    def arrange(here_y):
+        for k, piece in enumerate((w0, w1, w2, w3)):
+            y = (here_y - k) % ny
+            for z in range(nz):
+                at = (z * ny + y) * own
+                weights[at : at + own, :] = piece[z].astype(F32)
+
+    for_each(place[1], ny, arrange)
     slot_count = out.shape[0]
     step = 5 * BLOCK
     total = jnp.zeros((slot_count, width), F32)
@@ -145,7 +158,7 @@
 
 
 def fold_y_kernel(nz, own, groups, place, kept, r1, r2, r3, by_z, near_kept, scale_kept, *rest):
-    sends, (blocks, product) = rest[:-2], rest[-2:]
+    sends, (blocks, product, flat) = rest[:-3], rest[-3:]
     padded = product.shape[0] // nz
     width = product.shape[1]
     members = nz // groups
@@ -169,42 +182,46 @@
     for j in range(-(-nz * padded // width)):
         row = sums[0:1, j * width : (j + 1) * width]
         scale_kept[j : j + 1, : row.shape[1]] = row
-    both = both_terms(scale_kept[...])
-    low = lax.rem(place[0], members)
-    for h in range(groups):
-        near_kept[h] = blocks[h * members + low]
-    for k, send in enumerate(sends, 1):
-        there = lax.rem(low + k, members)
+    both = both_terms(scale_kept[...]).astype(F32)
+
+    def hand_out(low):
         for h in range(groups):
-            send[h] = blocks[h * members + there].astype(BF16)
-        send[groups] = jnp.zeros_like(send[groups])
-        send[groups, : both.shape[0], :] = both
+            near_kept[h] = blocks[h * members + low]
+        for k, send in enumerate(sends, 1):
+            for h in range(groups):
+                flat[h * own : (h + 1) * own, :] = blocks[h * members + (low + k) % members]
+            flat[groups * own :, :] = both
+            send[...] = flat[...].astype(BF16)
+
+    for_each(lax.rem(place[0], members), members, hand_out)
 
 
 def fold_low_kernel(near_kept, scale_kept, r1, r2, r3, out):
     groups, own, width = near_kept.shape
     lines = scale_kept.shape[0]
+    parts = [part[...].astype(F32) for part in (r1, r2, r3)]
     scale = scale_kept[...]
-    for part in (r1, r2, r3):
-        both = part[groups, : 2 * lines, :].astype(F32)
+    for part in parts:
+        both = part[groups * own :]
         scale = scale + (both[:lines] + both[lines:])
+    both = both_terms(scale).astype(F32)
+    gap = jnp.zeros((out.shape[1] - own - 2 * lines, width), F32)
     for h in range(groups):
         total = near_kept[h]
-        for part in (r1, r2, r3):
-            total += part[h].astype(F32)
-        out[h, :own, :] = total
-        out[h, own : out.shape[1] - lines, :] = jnp.zeros((out.shape[1] - lines - own, width), F32)
-        out[h, out.shape[1] - lines :, :] = scale
+        for part in parts:
+            total += part[h * own : (h + 1) * own]
+        out[h] = jnp.concatenate([total, gap, both], axis=0).astype(BF16)
 
 
 def fold_high_kernel(factor, parts, gain, out, scale_out):
-    total = parts[0]
+    total = parts[0].astype(F32)
     for h in range(1, parts.shape[0]):
-        total += parts[h]
+        total += parts[h].astype(F32)
     own, lines = out.shape[0], scale_out.shape[1]
     out[...] = total[:own] * (gain[...] * factor)
+    both = total[total.shape[0] - 2 * lines :]
     for k in range(scale_out.shape[0]):
-        scale_out[k] = total[total.shape[0] - lines :]
+        scale_out[k] = both[:lines] + both[lines:]
 
 
 def spread_kernel(source, out):
@@ -214,10 +231,14 @@
 
 def collect_kernel(place, *refs):
     parts, out = refs[:-1], refs[-1]
-    for k, part in enumerate(parts):
-        y = lax.rem(place[1] + len(parts) - k, len(parts))
-        for z in range(out.shape[0]):
-            out[z, y] = part[z]
+    count = len(parts)
+
+    def place_all(here):
+        for k, part in enumerate(parts):
+            for z in range(out.shape[0]):
+                out[z, (here - k) % count] = part[z]
+
+    for_each(place[1], count, place_all)
 
 
 def share_kernel(place, source, kept, *sends):
@@ -273,10 +294,9 @@
         scratch=[pltpu.VMEM((ny, nz, per_target, width), BF16)],
     )
     weights = all_to_all(
-        call(spread_kernel, shape((nz, own, width), BF16), (w_out.T,), flops=10**6, after=(send[0],)), Z,
+        call(spread_kernel, shape((nz, own, width), BF16), (w_out.T,), flops=10**6), Z,
     )
     sent = [send[0]] + [shifted(part, "y", ny, k) for k, part in enumerate(send[1:], 1)]
-    received = sent[1:]
     sent = call(
         collect_kernel, shape((nz, ny, per_target, width), BF16), (place, *sent), flops=10**8, scalars=1, after=(weights,),
     )
@@ -286,7 +306,7 @@
     mine = call(
         lambda *args: rows_kernel(capacity, *args),
         shape((source_rows, wide), BF16), (owner, grad_rows, row_target, row_target.reshape(1, source_rows)),
-        flops=10**8, scalars=1, after=received,
+        flops=10**8, scalars=1, after=(send[0],),
     )
     near = call(
         stack_kernel, shape((nx * source_rows, wide), BF16), [mine] + [shifted(mine, "x", nx, k) for k in range(1, nx)],
@@ -300,7 +320,9 @@
         lambda *args: outer_kernel(nz, ny, per_target, *args),
         [shape((share, width), F32)] + [shape((share, width), BF16)] * (ny - 1),
         (place, slots, *rows), flops=10**9, scalars=1,
-        scratch=[pltpu.VMEM((features, width), F32), pltpu.VMEM((ny, share, width), F32)],
+        scratch=[
+            pltpu.VMEM((ny, share, width), F32),
+        ],
     )
     parts = [shifted(send, "y", ny, k) for k, send in enumerate(sends, 1)]
 
@@ -308,7 +330,7 @@
         lambda *args: back_kernel(nz, ny, per_target, *args),
         shape((slot_count, width), BF16),
         (place, layer_scale.reshape(1, features), *pieces, *rows), flops=2 * 10**9, scalars=1, after=(kept,),
-        scratch=[pltpu.VMEM((ny, nz, own, width), F32), pltpu.VMEM((features, width), F32)],
+        scratch=[pltpu.VMEM((features, width), F32)],
     )
     returned = all_to_all(back.reshape(nz, ny, per_target, width), Z)
     sends = call(
@@ -328,14 +350,18 @@
     low, low_scale, *sends = call(
         lambda *args: fold_y_kernel(nz, own, groups, *args),
         [shape((groups, own, width), F32), shape((lines, width), F32)]
-        + [shape((groups + 1, own, width), BF16)] * (members - 1),
+        + [shape((groups * own + 2 * lines, width), BF16)] * (members - 1),
         (place, kept, *parts, weights), flops=2 * 10**11, scalars=1,
-        scratch=[pltpu.VMEM((nz, own, width), F32), pltpu.VMEM((nz * padded, width), F32)],
+        scratch=[
+            pltpu.VMEM((nz, own, width), F32),
+            pltpu.VMEM((nz * padded, width), F32),
+            pltpu.VMEM((groups * own + 2 * lines, width), F32),
+        ],
     )
     parts = [shifted(send, "l", members, k) for k, send in enumerate(sends, 1)]
-    rows_sent = -(-(own + lines) // 8) * 8
+    rows_sent = -(-(own + 2 * lines) // 16) * 16
     total = call(
-        fold_low_kernel, shape((groups, rows_sent, width), F32), (low, low_scale, *parts), flops=10**11, after=(returned,),
+        fold_low_kernel, shape((groups, rows_sent, width), BF16), (low, low_scale, *parts), flops=10**11, after=(returned,),
     )
     rescale = 1.0 / math.sqrt(source_rows * encoders * owners)
     at = lax.axis_index(Z + ("y",)) * own

time: 195 us -> 187 us (0.959)
  waiting for transfers between devices: 32.4 us -> 28.9 us
  starting transfers between devices: 130 us -> 128 us
    ppermute x19, waiting for transfers between devices: 24.5 us -> 22.3 us  [shifted(): lax.ppermute(value, axis, [(i, (i + shift) % size) for i in range(size)])]
    all_to_all x5, starting transfers between devices: 63 us -> 60.9 us  [all_to_all(): return lax.all_to_all(value, axes, split_axis=0, concat_axis=0, tiled=True)]
  transfers between devices with their start and end apart: 24 -> 24, of which waited for: 8 -> 6; matrix products, arithmetic and copies ran while one was open for 1% -> 1% of each run, Pallas kernels for 8% -> 9%
where the time goes in v3:
time: 187 us; the launch traced here: 185 us
  starting transfers between devices  128 us (68%)
  waiting for transfers between devices  28.9 us (15%)
  Pallas kernels  17.3 us (9%)
  local copies, waits for them, and re-layouts  9.84 us (5%)
    ppermute x19, starting transfers between devices, shifted(): lax.ppermute(value, axis, [(i, (i + shift) % size) for i in range(size)])  67.2 us
    all_to_all x5, starting transfers between devices, all_to_all(): return lax.all_to_all(value, axes, split_axis=0, concat_axis=0, tiled=True)  60.9 us
    ppermute x19, waiting for transfers between devices, shifted(): lax.ppermute(value, axis, [(i, (i + shift) % size) for i in range(size)])  22.3 us
    pallas_call x12, Pallas kernels, call(): pl.pallas_call(body, out_shape=out_shape, in_specs=specs + [pl.BlockSpec(...  17.3 us
    unnamed x24, local copies, waits for them, and re-layouts  8.02 us
    all_to_all x5, waiting for transfers between devices, all_to_all(): return lax.all_to_all(value, axes, split_axis=0, concat_axis=0, tiled=True)  6.55 us
  transfers between devices with their start and end apart: 24, of which 6 were waited for; matrix products, arithmetic and copies ran while one was open for 1% of the time, Pallas kernels for 9%

profile of v3, /device:TPU:1, one launch (start us, length us, event | category | flops | bytes accessed | tf_op | source)
XLA Modules:
  0.0 185.2 jit_solution(1529414679292427819)
XLA Ops:
  2.3 15.7 %all-to-all-start = ((bf16[16,50,256]{2,1,0:T(8,128)(2,1)}), bf16[16,50,256]{2,1,0:T(8,128)(2,1)S(1)}, u32[]{:S(2)}, u32[]{:S(2)}) async-start(bf16[16,50,256]{2,1,0:T(8,128)(2,1)} %shard_map.85), calls=%async_computation | async-start | bytes 917504 | tf_op jit(solution)/shard_map/all_to_all | solution.py:276
  20.2 3.2 %collective-permute-start.7 = (bf16[16,16,256]{2,1,0:T(8,128)(2,1)S(1)}, bf16[16,16,256]{2,1,0:T(8,128)(2,1)S(1)}, u32[]{:S(2)}, u32[]{:S(2)}) collective-permute-start(bf16[16,16,256]{2,1,0:T(8,128)(2,1)S(1)} %get-tuple-element.23), channel_id=1, source_target_pairs={{0,8},{8,16},{16,24},{24,0},{1,9},{9,17},{17,25},{25,1},{2,10},{10... | collective-permute-start | bytes 393224 | tf_op jit(solution)/shard_map/ppermute | solution.py:272
  23.6 3.1 %collective-permute-start.3 = (bf16[64,3328]{1,0:T(8,128)(2,1)S(1)}, bf16[64,3328]{1,0:T(8,128)(2,1)S(1)}, u32[]{:S(2)}, u32[]{:S(2)}) collective-permute-start(bf16[64,3328]{1,0:T(8,128)(2,1)S(1)} %shard_map.87.refs_0_), channel_id=1, source_target_pairs={{0,2},{2,4},{4,6},{6,0},{1,3},{3,5},{5,7},{7,1},{8,10},{10,12},{12... | collective-permute-start | bytes 1277960 | tf_op jit(solution)/shard_map/ppermute | solution.py:272
  26.8 4.4 %collective-permute-start.4 = (bf16[64,3328]{1,0:T(8,128)(2,1)S(1)}, bf16[64,3328]{1,0:T(8,128)(2,1)S(1)}, u32[]{:S(2)}, u32[]{:S(2)}) collective-permute-start(bf16[64,3328]{1,0:T(8,128)(2,1)S(1)} %shard_map.87.refs_0_), channel_id=1, source_target_pairs={{0,4},{2,6},{4,0},{6,2},{1,5},{3,7},{5,1},{7,3},{8,12},{10,14},{12... | collective-permute-start | bytes 1277960 | tf_op jit(solution)/shard_map/ppermute | solution.py:272
  31.1 3.1 %collective-permute-start.5 = (bf16[64,3328]{1,0:T(8,128)(2,1)S(1)}, bf16[64,3328]{1,0:T(8,128)(2,1)S(1)}, u32[]{:S(2)}, u32[]{:S(2)}) collective-permute-start(bf16[64,3328]{1,0:T(8,128)(2,1)S(1)} %shard_map.87.refs_0_), channel_id=1, source_target_pairs={{0,6},{2,0},{4,2},{6,4},{1,7},{3,1},{5,3},{7,5},{8,14},{10,8},{12,... | collective-permute-start | bytes 1277960 | tf_op jit(solution)/shard_map/ppermute | solution.py:272
  34.2 4.5 %collective-permute-start.8 = (bf16[16,16,256]{2,1,0:T(8,128)(2,1)S(1)}, bf16[16,16,256]{2,1,0:T(8,128)(2,1)S(1)}, u32[]{:S(2)}, u32[]{:S(2)}) collective-permute-start(bf16[16,16,256]{2,1,0:T(8,128)(2,1)S(1)} %get-tuple-element.24), channel_id=1, source_target_pairs={{0,16},{8,24},{16,0},{24,8},{1,17},{9,25},{17,1},{25,9},{2,18},{10... | collective-permute-start | bytes 393224 | tf_op jit(solution)/shard_map/ppermute | solution.py:272
  41.8 3.0 %collective-permute-done.9.refs_4_ = bf16[16,16,256]{2,1,0:T(8,128)(2,1)S(1)} collective-permute-done((bf16[16,16,256]{2,1,0:T(8,128)(2,1)S(1)}, bf16[16,16,256]{2,1,0:T(8,128)(2,1)S(1)}, u32[]{:S(2)}, u32[]{:S(2)}) %collective-permute-start.9) | collective-permute-done | bytes 131104 | tf_op jit(solution)/shard_map/ppermute | solution.py:272
  46.2 11.6 %all-to-all-start.1 = ((bf16[16,4,16,256]{3,2,1,0:T(8,128)(2,1)}), bf16[16,4,16,256]{3,2,1,0:T(8,128)(2,1)S(1)}, u32[]{:S(2)}, u32[]{:S(2)}) async-start(bf16[16,4,16,256]{3,2,1,0:T(8,128)(2,1)} %shard_map.89), calls=%async_computation.1 | async-start | bytes 1048576 | tf_op jit(solution)/shard_map/all_to_all | solution.py:276
  61.5 5.5 %collective-permute-start.6 = (bf16[256,3328]{1,0:T(8,128)(2,1)S(1)}, bf16[256,3328]{1,0:T(8,128)(2,1)S(1)}, u32[]{:S(2)}, u32[]{:S(2)}) collective-permute-start(bf16[256,3328]{1,0:T(8,128)(2,1)S(1)} %shard_map.88.refs_2_.refs_6_), channel_id=1, source_target_pairs={{0,1},{1,0},{2,3},{3,2},{4,5},{5,4},{6,7},{7,6},{8,9},{9,8},{10,11... | collective-permute-start | bytes 5111816 | tf_op jit(solution)/shard_map/ppermute | solution.py:272
  68.9 5.4 %collective-permute-start.1 = (bf16[16,50,256]{2,1,0:T(8,128)(2,1)S(1)}, bf16[16,50,256]{2,1,0:T(8,128)(2,1)}, u32[]{:S(2)}, u32[]{:S(2)}) collective-permute-start(bf16[16,50,256]{2,1,0:T(8,128)(2,1)S(1)} %all-to-all-done.refs_4_.refs_5_.refs_2_), channel_id=1, source_target_pairs={{0,16},{8,24},{16,0},{24,8},{1,17},{9,25},{17,1},{25,9},{2,18},{10... | collective-permute-start | bytes 1228808 | tf_op jit(solution)/shard_map/ppermute | solution.py:272
  79.5 3.3 %shard_map.90 = (f32[800,256]{1,0:T(8,128)S(1)}, bf16[800,256]{1,0:T(8,128)(2,1)}, bf16[800,256]{1,0:T(8,128)(2,1)}, bf16[800,256]{1,0:T(8,128)(2,1)}) custom-call(s32[2]{0:T(128)S(1)} %pad_add_fusion.refs_0_, bf16[1024,256]{1,0:T(8,128)(2,1)S(1)} %bitcast.11, bf16[256,3328]{1,0:T(8,128)(2,1)S(1)} %shard_map.88.refs_2_.refs_6_, bf16[256,3328]{1,0:T(8,128)(2,1)S(1)} %copy-done.1), custom_call_target="tpu_custom_call" | custom-call | flops 1000000000 | bytes 4194304 | tf_op jit(solution)/shard_map/pallas_call | solution.py:28
  85.6 5.0 %collective-permute-start.14 = (bf16[800,256]{1,0:T(8,128)(2,1)}, bf16[800,256]{1,0:T(8,128)(2,1)}, u32[]{:S(2)}, u32[]{:S(2)}) collective-permute-start(bf16[800,256]{1,0:T(8,128)(2,1)} %get-tuple-element.32), channel_id=1, source_target_pairs={{0,16},{8,24},{16,0},{24,8},{1,17},{9,25},{17,1},{25,9},{2,18},{10... | collective-permute-start | bytes 1228808 | tf_op jit(solution)/shard_map/ppermute | solution.py:272
  94.4 4.2 %shard_map.91 = bf16[1024,256]{1,0:T(8,128)(2,1)} custom-call(s32[2]{0:T(128)S(1)} %pad_add_fusion.refs_0_, f32[1,3200]{1,0:T(1,128)S(1)} %reshape.33.refs_1_, bf16[16,50,256]{2,1,0:T(8,128)(2,1)S(1)} %all-to-all-done.refs_4_.refs_5_.refs_2_, bf16[16,50,256]{2,1,0:T(8,128)(2,1)} %collective-permute-done.refs_3_, ...), custom_call_target="tpu_custom_call" | custom-call | flops 2000000000 | bytes 4194304 | tf_op jit(solution)/shard_map/pallas_call | solution.py:28
  98.5 12.1 %all-to-all-start.2 = ((bf16[16,4,16,256]{3,2,1,0:T(8,128)(2,1)}), bf16[16,4,16,256]{3,2,1,0:T(8,128)(2,1)}, u32[]{:S(2)}, u32[]{:S(2)}) async-start(bf16[16,4,16,256]{3,2,1,0:T(8,128)(2,1)} %bitcast.6), calls=%async_computation.2 | async-start | bytes 1048576 | tf_op jit(solution)/shard_map/all_to_all | solution.py:276
  112.8 3.2 %collective-permute-start.16 = (bf16[208,256]{1,0:T(8,128)(2,1)S(1)}, bf16[208,256]{1,0:T(8,128)(2,1)S(1)}, u32[]{:S(2)}, u32[]{:S(2)}) collective-permute-start(bf16[208,256]{1,0:T(8,128)(2,1)S(1)} %get-tuple-element.36), channel_id=1, source_target_pairs={{0,32},{32,64},{64,96},{96,0},{1,33},{33,65},{65,97},{97,1},{2,34}... | collective-permute-start | bytes 319496 | tf_op jit(solution)/shard_map/ppermute | solution.py:272
  116.0 4.0 %collective-permute-start.17 = (bf16[208,256]{1,0:T(8,128)(2,1)S(1)}, bf16[208,256]{1,0:T(8,128)(2,1)S(1)}, u32[]{:S(2)}, u32[]{:S(2)}) collective-permute-start(bf16[208,256]{1,0:T(8,128)(2,1)S(1)} %get-tuple-element.37), channel_id=1, source_target_pairs={{0,64},{32,96},{64,0},{96,32},{1,65},{33,97},{65,1},{97,33},{2,66}... | collective-permute-start | bytes 319496 | tf_op jit(solution)/shard_map/ppermute | solution.py:272
  120.0 3.1 %collective-permute-start.18 = (bf16[208,256]{1,0:T(8,128)(2,1)S(1)}, bf16[208,256]{1,0:T(8,128)(2,1)S(1)}, u32[]{:S(2)}, u32[]{:S(2)}) collective-permute-start(bf16[208,256]{1,0:T(8,128)(2,1)S(1)} %get-tuple-element.38), channel_id=1, source_target_pairs={{0,96},{32,0},{64,32},{96,64},{1,97},{33,1},{65,33},{97,65},{2,98}... | collective-permute-start | bytes 319496 | tf_op jit(solution)/shard_map/ppermute | solution.py:272
  123.1 11.9 %collective-permute-done.16.refs_2_ = bf16[208,256]{1,0:T(8,128)(2,1)S(1)} collective-permute-done((bf16[208,256]{1,0:T(8,128)(2,1)S(1)}, bf16[208,256]{1,0:T(8,128)(2,1)S(1)}, u32[]{:S(2)}, u32[]{:S(2)}) %collective-permute-start.16) | collective-permute-done | bytes 106528 | tf_op jit(solution)/shard_map/ppermute | solution.py:272
  135.0 6.3 %collective-permute-done.17.refs_3_ = bf16[208,256]{1,0:T(8,128)(2,1)S(1)} collective-permute-done((bf16[208,256]{1,0:T(8,128)(2,1)S(1)}, bf16[208,256]{1,0:T(8,128)(2,1)S(1)}, u32[]{:S(2)}, u32[]{:S(2)}) %collective-permute-start.17) | collective-permute-done | bytes 106528 | tf_op jit(solution)/shard_map/ppermute | solution.py:272
  142.1 11.4 %all-to-all-start.3 = ((bf16[4,64,256]{2,1,0:T(8,128)(2,1)}), bf16[4,64,256]{2,1,0:T(8,128)(2,1)S(1)}, u32[]{:S(2)}, u32[]{:S(2)}) async-start(bf16[4,64,256]{2,1,0:T(8,128)(2,1)} %shard_map.95), calls=%async_computation.3 | async-start | bytes 262144 | tf_op jit(solution)/shard_map/all_to_all | solution.py:276
  154.5 3.3 %collective-permute-start.10 = (bf16[16,16,256]{2,1,0:T(8,128)(2,1)S(1)}, bf16[16,16,256]{2,1,0:T(8,128)(2,1)S(1)}, u32[]{:S(2)}, u32[]{:S(2)}) collective-permute-start(bf16[16,16,256]{2,1,0:T(8,128)(2,1)S(1)} %get-tuple-element.28), channel_id=1, source_target_pairs={{0,8},{8,16},{16,24},{24,0},{1,9},{9,17},{17,25},{25,1},{2,10},{10... | collective-permute-start | bytes 393224 | tf_op jit(solution)/shard_map/ppermute | solution.py:272
  157.8 5.2 %collective-permute-start.11 = (bf16[16,16,256]{2,1,0:T(8,128)(2,1)S(1)}, bf16[16,16,256]{2,1,0:T(8,128)(2,1)S(1)}, u32[]{:S(2)}, u32[]{:S(2)}) collective-permute-start(bf16[16,16,256]{2,1,0:T(8,128)(2,1)S(1)} %get-tuple-element.29), channel_id=1, source_target_pairs={{0,16},{8,24},{16,0},{24,8},{1,17},{9,25},{17,1},{25,9},{2,18},{10... | collective-permute-start | bytes 393224 | tf_op jit(solution)/shard_map/ppermute | solution.py:272
  166.6 10.0 %all-to-all-start.4 = ((f32[32,4,256]{2,1,0:T(4,128)}), f32[32,4,256]{2,1,0:T(4,128)S(1)}, u32[]{:S(2)}, u32[]{:S(2)}) async-start(f32[32,4,256]{2,1,0:T(4,128)} %get-tuple-element.40), calls=%async_computation.4 | async-start | bytes 262144 | tf_op jit(solution)/shard_map/all_to_all | solution.py:276
  178.3 5.9 %all-to-all-done.4 = f32[32,4,256]{2,1,0:T(4,128)S(1)} async-done(((f32[32,4,256]{2,1,0:T(4,128)}), f32[32,4,256]{2,1,0:T(4,128)S(1)}, u32[]{:S(2)}, u32[]{:S(2)}) %all-to-all-start.4) | async-done | bytes 131104 | tf_op jit(solution)/shard_map/all_to_all | solution.py:276
  (70 shorter events, 35.7 us)
Async XLA Ops:
  2.3 42.5 %all-to-all-start = ((bf16[16,50,256]{2,1,0:T(8,128)(2,1)}), bf16[16,50,256]{2,1,0:T(8,128)(2,1)S(1)}, u32[]{:S(2)}, u32[]{:S(2)}) async-start(bf16[16,50,256]{2,1,0:T(8,128)(2,1)} %shard_map.85), calls=%async_computation | async-start | bytes 917504 | tf_op jit(solution)/shard_map/all_to_all | solution.py:276
  20.2 18.6 %collective-permute-start.7 = (bf16[16,16,256]{2,1,0:T(8,128)(2,1)S(1)}, bf16[16,16,256]{2,1,0:T(8,128)(2,1)S(1)}, u32[]{:S(2)}, u32[]{:S(2)}) collective-permute-start(bf16[16,16,256]{2,1,0:T(8,128)(2,1)S(1)} %get-tuple-element.23), channel_id=1, source_target_pairs={{0,8},{8,16},{16,24},{24,0},{1,9},{9,17},{17,25},{25,1},{2,10},{10... | collective-permute-start | bytes 393224 | tf_op jit(solution)/shard_map/ppermute | solution.py:272
  23.6 34.1 %collective-permute-start.3 = (bf16[64,3328]{1,0:T(8,128)(2,1)S(1)}, bf16[64,3328]{1,0:T(8,128)(2,1)S(1)}, u32[]{:S(2)}, u32[]{:S(2)}) collective-permute-start(bf16[64,3328]{1,0:T(8,128)(2,1)S(1)} %shard_map.87.refs_0_), channel_id=1, source_target_pairs={{0,2},{2,4},{4,6},{6,0},{1,3},{3,5},{5,7},{7,1},{8,10},{10,12},{12... | collective-permute-start | bytes 1277960 | tf_op jit(solution)/shard_map/ppermute | solution.py:272
  26.8 31.0 %collective-permute-start.4 = (bf16[64,3328]{1,0:T(8,128)(2,1)S(1)}, bf16[64,3328]{1,0:T(8,128)(2,1)S(1)}, u32[]{:S(2)}, u32[]{:S(2)}) collective-permute-start(bf16[64,3328]{1,0:T(8,128)(2,1)S(1)} %shard_map.87.refs_0_), channel_id=1, source_target_pairs={{0,4},{2,6},{4,0},{6,2},{1,5},{3,7},{5,1},{7,3},{8,12},{10,14},{12... | collective-permute-start | bytes 1277960 | tf_op jit(solution)/shard_map/ppermute | solution.py:272
  31.1 27.4 %collective-permute-start.5 = (bf16[64,3328]{1,0:T(8,128)(2,1)S(1)}, bf16[64,3328]{1,0:T(8,128)(2,1)S(1)}, u32[]{:S(2)}, u32[]{:S(2)}) collective-permute-start(bf16[64,3328]{1,0:T(8,128)(2,1)S(1)} %shard_map.87.refs_0_), channel_id=1, source_target_pairs={{0,6},{2,0},{4,2},{6,4},{1,7},{3,1},{5,3},{7,5},{8,14},{10,8},{12,... | collective-permute-start | bytes 1277960 | tf_op jit(solution)/shard_map/ppermute | solution.py:272
  34.2 7.5 %collective-permute-start.8 = (bf16[16,16,256]{2,1,0:T(8,128)(2,1)S(1)}, bf16[16,16,256]{2,1,0:T(8,128)(2,1)S(1)}, u32[]{:S(2)}, u32[]{:S(2)}) collective-permute-start(bf16[16,16,256]{2,1,0:T(8,128)(2,1)S(1)} %get-tuple-element.24), channel_id=1, source_target_pairs={{0,16},{8,24},{16,0},{24,8},{1,17},{9,25},{17,1},{25,9},{2,18},{10... | collective-permute-start | bytes 393224 | tf_op jit(solution)/shard_map/ppermute | solution.py:272
  38.8 6.0 %collective-permute-start.9 = (bf16[16,16,256]{2,1,0:T(8,128)(2,1)S(1)}, bf16[16,16,256]{2,1,0:T(8,128)(2,1)S(1)}, u32[]{:S(2)}, u32[]{:S(2)}) collective-permute-start(bf16[16,16,256]{2,1,0:T(8,128)(2,1)S(1)} %get-tuple-element.25), channel_id=1, source_target_pairs={{0,24},{8,0},{16,8},{24,16},{1,25},{9,1},{17,9},{25,17},{2,26},{10... | collective-permute-start | bytes 393224 | tf_op jit(solution)/shard_map/ppermute | solution.py:272
  46.2 31.9 %all-to-all-start.1 = ((bf16[16,4,16,256]{3,2,1,0:T(8,128)(2,1)}), bf16[16,4,16,256]{3,2,1,0:T(8,128)(2,1)S(1)}, u32[]{:S(2)}, u32[]{:S(2)}) async-start(bf16[16,4,16,256]{3,2,1,0:T(8,128)(2,1)} %shard_map.89), calls=%async_computation.1 | async-start | bytes 1048576 | tf_op jit(solution)/shard_map/all_to_all | solution.py:276
  61.5 14.8 %collective-permute-start.6 = (bf16[256,3328]{1,0:T(8,128)(2,1)S(1)}, bf16[256,3328]{1,0:T(8,128)(2,1)S(1)}, u32[]{:S(2)}, u32[]{:S(2)}) collective-permute-start(bf16[256,3328]{1,0:T(8,128)(2,1)S(1)} %shard_map.88.refs_2_.refs_6_), channel_id=1, source_target_pairs={{0,1},{1,0},{2,3},{3,2},{4,5},{5,4},{6,7},{7,6},{8,9},{9,8},{10,11... | collective-permute-start | bytes 5111816 | tf_op jit(solution)/shard_map/ppermute | solution.py:272
  67.0 23.6 %collective-permute-start = (bf16[16,50,256]{2,1,0:T(8,128)(2,1)S(1)}, bf16[16,50,256]{2,1,0:T(8,128)(2,1)}, u32[]{:S(2)}, u32[]{:S(2)}) collective-permute-start(bf16[16,50,256]{2,1,0:T(8,128)(2,1)S(1)} %all-to-all-done.refs_4_.refs_5_.refs_2_), channel_id=1, source_target_pairs={{0,8},{8,16},{16,24},{24,0},{1,9},{9,17},{17,25},{25,1},{2,10},{10... | collective-permute-start | bytes 1228808 | tf_op jit(solution)/shard_map/ppermute | solution.py:272
  68.9 24.4 %collective-permute-start.1 = (bf16[16,50,256]{2,1,0:T(8,128)(2,1)S(1)}, bf16[16,50,256]{2,1,0:T(8,128)(2,1)}, u32[]{:S(2)}, u32[]{:S(2)}) collective-permute-start(bf16[16,50,256]{2,1,0:T(8,128)(2,1)S(1)} %all-to-all-done.refs_4_.refs_5_.refs_2_), channel_id=1, source_target_pairs={{0,16},{8,24},{16,0},{24,8},{1,17},{9,25},{17,1},{25,9},{2,18},{10... | collective-permute-start | bytes 1228808 | tf_op jit(solution)/shard_map/ppermute | solution.py:272
  74.3 20.1 %collective-permute-start.2 = (bf16[16,50,256]{2,1,0:T(8,128)(2,1)S(1)}, bf16[16,50,256]{2,1,0:T(8,128)(2,1)}, u32[]{:S(2)}, u32[]{:S(2)}) collective-permute-start(bf16[16,50,256]{2,1,0:T(8,128)(2,1)S(1)} %all-to-all-done.refs_4_.refs_5_.refs_2_), channel_id=1, source_target_pairs={{0,24},{8,0},{16,8},{24,16},{1,25},{9,1},{17,9},{25,17},{2,26},{10... | collective-permute-start | bytes 1228808 | tf_op jit(solution)/shard_map/ppermute | solution.py:272
  82.8 27.9 %collective-permute-start.13 = (bf16[800,256]{1,0:T(8,128)(2,1)}, bf16[800,256]{1,0:T(8,128)(2,1)S(1)}, u32[]{:S(2)}, u32[]{:S(2)}) collective-permute-start(bf16[800,256]{1,0:T(8,128)(2,1)} %get-tuple-element.31), channel_id=1, source_target_pairs={{0,8},{8,16},{16,24},{24,0},{1,9},{9,17},{17,25},{25,1},{2,10},{10... | collective-permute-start | bytes 1228808 | tf_op jit(solution)/shard_map/ppermute | solution.py:272
  85.6 25.1 %collective-permute-start.14 = (bf16[800,256]{1,0:T(8,128)(2,1)}, bf16[800,256]{1,0:T(8,128)(2,1)}, u32[]{:S(2)}, u32[]{:S(2)}) collective-permute-start(bf16[800,256]{1,0:T(8,128)(2,1)} %get-tuple-element.32), channel_id=1, source_target_pairs={{0,16},{8,24},{16,0},{24,8},{1,17},{9,25},{17,1},{25,9},{2,18},{10... | collective-permute-start | bytes 1228808 | tf_op jit(solution)/shard_map/ppermute | solution.py:272
  90.6 20.1 %collective-permute-start.15 = (bf16[800,256]{1,0:T(8,128)(2,1)}, bf16[800,256]{1,0:T(8,128)(2,1)}, u32[]{:S(2)}, u32[]{:S(2)}) collective-permute-start(bf16[800,256]{1,0:T(8,128)(2,1)} %get-tuple-element.33), channel_id=1, source_target_pairs={{0,24},{8,0},{16,8},{24,16},{1,25},{9,1},{17,9},{25,17},{2,26},{10... | collective-permute-start | bytes 1228808 | tf_op jit(solution)/shard_map/ppermute | solution.py:272
  98.5 42.8 %all-to-all-start.2 = ((bf16[16,4,16,256]{3,2,1,0:T(8,128)(2,1)}), bf16[16,4,16,256]{3,2,1,0:T(8,128)(2,1)}, u32[]{:S(2)}, u32[]{:S(2)}) async-start(bf16[16,4,16,256]{3,2,1,0:T(8,128)(2,1)} %bitcast.6), calls=%async_computation.2 | async-start | bytes 1048576 | tf_op jit(solution)/shard_map/all_to_all | solution.py:276
  112.8 22.2 %collective-permute-start.16 = (bf16[208,256]{1,0:T(8,128)(2,1)S(1)}, bf16[208,256]{1,0:T(8,128)(2,1)S(1)}, u32[]{:S(2)}, u32[]{:S(2)}) collective-permute-start(bf16[208,256]{1,0:T(8,128)(2,1)S(1)} %get-tuple-element.36), channel_id=1, source_target_pairs={{0,32},{32,64},{64,96},{96,0},{1,33},{33,65},{65,97},{97,1},{2,34}... | collective-permute-start | bytes 319496 | tf_op jit(solution)/shard_map/ppermute | solution.py:272
  116.0 25.3 %collective-permute-start.17 = (bf16[208,256]{1,0:T(8,128)(2,1)S(1)}, bf16[208,256]{1,0:T(8,128)(2,1)S(1)}, u32[]{:S(2)}, u32[]{:S(2)}) collective-permute-start(bf16[208,256]{1,0:T(8,128)(2,1)S(1)} %get-tuple-element.37), channel_id=1, source_target_pairs={{0,64},{32,96},{64,0},{96,32},{1,65},{33,97},{65,1},{97,33},{2,66}... | collective-permute-start | bytes 319496 | tf_op jit(solution)/shard_map/ppermute | solution.py:272
  120.0 21.3 %collective-permute-start.18 = (bf16[208,256]{1,0:T(8,128)(2,1)S(1)}, bf16[208,256]{1,0:T(8,128)(2,1)S(1)}, u32[]{:S(2)}, u32[]{:S(2)}) collective-permute-start(bf16[208,256]{1,0:T(8,128)(2,1)S(1)} %get-tuple-element.38), channel_id=1, source_target_pairs={{0,96},{32,0},{64,32},{96,64},{1,97},{33,1},{65,33},{97,65},{2,98}... | collective-permute-start | bytes 319496 | tf_op jit(solution)/shard_map/ppermute | solution.py:272
  142.1 23.8 %all-to-all-start.3 = ((bf16[4,64,256]{2,1,0:T(8,128)(2,1)}), bf16[4,64,256]{2,1,0:T(8,128)(2,1)S(1)}, u32[]{:S(2)}, u32[]{:S(2)}) async-start(bf16[4,64,256]{2,1,0:T(8,128)(2,1)} %shard_map.95), calls=%async_computation.3 | async-start | bytes 262144 | tf_op jit(solution)/shard_map/all_to_all | solution.py:276
  154.5 22.1 %collective-permute-start.10 = (bf16[16,16,256]{2,1,0:T(8,128)(2,1)S(1)}, bf16[16,16,256]{2,1,0:T(8,128)(2,1)S(1)}, u32[]{:S(2)}, u32[]{:S(2)}) collective-permute-start(bf16[16,16,256]{2,1,0:T(8,128)(2,1)S(1)} %get-tuple-element.28), channel_id=1, source_target_pairs={{0,8},{8,16},{16,24},{24,0},{1,9},{9,17},{17,25},{25,1},{2,10},{10... | collective-permute-start | bytes 393224 | tf_op jit(solution)/shard_map/ppermute | solution.py:272
  157.8 18.8 %collective-permute-start.11 = (bf16[16,16,256]{2,1,0:T(8,128)(2,1)S(1)}, bf16[16,16,256]{2,1,0:T(8,128)(2,1)S(1)}, u32[]{:S(2)}, u32[]{:S(2)}) collective-permute-start(bf16[16,16,256]{2,1,0:T(8,128)(2,1)S(1)} %get-tuple-element.29), channel_id=1, source_target_pairs={{0,16},{8,24},{16,0},{24,8},{1,17},{9,25},{17,1},{25,9},{2,18},{10... | collective-permute-start | bytes 393224 | tf_op jit(solution)/shard_map/ppermute | solution.py:272
  163.1 13.6 %collective-permute-start.12 = (bf16[16,16,256]{2,1,0:T(8,128)(2,1)S(1)}, bf16[16,16,256]{2,1,0:T(8,128)(2,1)S(1)}, u32[]{:S(2)}, u32[]{:S(2)}) collective-permute-start(bf16[16,16,256]{2,1,0:T(8,128)(2,1)S(1)} %get-tuple-element.30), channel_id=1, source_target_pairs={{0,24},{8,0},{16,8},{24,16},{1,25},{9,1},{17,9},{25,17},{2,26},{10... | collective-permute-start | bytes 393224 | tf_op jit(solution)/shard_map/ppermute | solution.py:272
  166.6 17.7 %all-to-all-start.4 = ((f32[32,4,256]{2,1,0:T(4,128)}), f32[32,4,256]{2,1,0:T(4,128)S(1)}, u32[]{:S(2)}, u32[]{:S(2)}) async-start(f32[32,4,256]{2,1,0:T(4,128)} %get-tuple-element.40), calls=%async_computation.4 | async-start | bytes 262144 | tf_op jit(solution)/shard_map/all_to_all | solution.py:276
  (11 other events, 84.0 us)

commit v4 on v3

--- a/solution.py
+++ b/solution.py
@@ -297,6 +297,7 @@
         call(spread_kernel, shape((nz, own, width), BF16), (w_out.T,), flops=10**6), Z,
     )
     sent = [send[0]] + [shifted(part, "y", ny, k) for k, part in enumerate(send[1:], 1)]
+    received = sent[1:]
     sent = call(
         collect_kernel, shape((nz, ny, per_target, width), BF16), (place, *sent), flops=10**8, scalars=1, after=(weights,),
     )
@@ -308,8 +309,9 @@
         shape((source_rows, wide), BF16), (owner, grad_rows, row_target, row_target.reshape(1, source_rows)),
         flops=10**8, scalars=1, after=(send[0],),
     )
+    late = call(stack_kernel, shape((source_rows, wide), BF16), [mine], flops=10**6, after=received)
     near = call(
-        stack_kernel, shape((nx * source_rows, wide), BF16), [mine] + [shifted(mine, "x", nx, k) for k in range(1, nx)],
+        stack_kernel, shape((nx * source_rows, wide), BF16), [mine] + [shifted(mine if k < nx - 1 else late, "x", nx, k) for k in range(1, nx)],
         flops=10**8, after=(weights,),
     )
     rows = [near, shifted(near, "c", nc, 1)]

time: 187 us -> 185 us (0.989)
  starting transfers between devices: 128 us -> 125 us
    ppermute x19, starting transfers between devices: 67.2 us -> 62.1 us  [shifted(): lax.ppermute(value, axis, [(i, (i + shift) % size) for i in range(size)])]
    all_to_all x5, waiting for transfers between devices: 6.55 us -> 8.99 us  [all_to_all(): return lax.all_to_all(value, axes, split_axis=0, concat_axis=0, tiled=True)]
    ppermute x19, waiting for transfers between devices: 22.3 us -> 20.3 us  [shifted(): lax.ppermute(value, axis, [(i, (i + shift) % size) for i in range(size)])]
    all_to_all x5, starting transfers between devices: 60.9 us -> 62.8 us  [all_to_all(): return lax.all_to_all(value, axes, split_axis=0, concat_axis=0, tiled=True)]
    pallas_call x12 -> x13, Pallas kernels: 17.3 us -> 18.8 us  [call(): pl.pallas_call(body, out_shape=out_shape, in_specs=specs + [pl.BlockSpec(...]
  transfers between devices with their start and end apart: 24 -> 24, of which waited for: 6 -> 8; matrix products, arithmetic and copies ran while one was open for 1% -> 1% of each run, Pallas kernels for 9% -> 9%
where the time goes in v4:
time: 185 us; the launch traced here: 183 us
  starting transfers between devices  125 us (68%)
  waiting for transfers between devices  29.3 us (16%)
  Pallas kernels  18.8 us (10%)
  local copies, waits for them, and re-layouts  9.21 us (5%)
    all_to_all x5, starting transfers between devices, all_to_all(): return lax.all_to_all(value, axes, split_axis=0, concat_axis=0, tiled=True)  62.8 us
    ppermute x19, starting transfers between devices, shifted(): lax.ppermute(value, axis, [(i, (i + shift) % size) for i in range(size)])  62.1 us
    ppermute x19, waiting for transfers between devices, shifted(): lax.ppermute(value, axis, [(i, (i + shift) % size) for i in range(size)])  20.3 us
    pallas_call x13, Pallas kernels, call(): pl.pallas_call(body, out_shape=out_shape, in_specs=specs + [pl.BlockSpec(...  18.8 us
    all_to_all x5, waiting for transfers between devices, all_to_all(): return lax.all_to_all(value, axes, split_axis=0, concat_axis=0, tiled=True)  8.99 us
    unnamed x24, local copies, waits for them, and re-layouts  7.39 us
  transfers between devices with their start and end apart: 24, of which 8 were waited for; matrix products, arithmetic and copies ran while one was open for 1% of the time, Pallas kernels for 9%

profile of v4, /device:TPU:1, one launch (start us, length us, event | category | flops | bytes accessed | tf_op | source)
XLA Modules:
  0.0 183.5 jit_solution(5274688318927527553)
XLA Ops:
  2.3 15.7 %all-to-all-start = ((bf16[16,50,256]{2,1,0:T(8,128)(2,1)}), bf16[16,50,256]{2,1,0:T(8,128)(2,1)S(1)}, u32[]{:S(2)}, u32[]{:S(2)}) async-start(bf16[16,50,256]{2,1,0:T(8,128)(2,1)} %shard_map.85), calls=%async_computation | async-start | bytes 917504 | tf_op jit(solution)/shard_map/all_to_all | solution.py:276
  20.9 3.2 %collective-permute-start.5 = (bf16[16,16,256]{2,1,0:T(8,128)(2,1)}, bf16[16,16,256]{2,1,0:T(8,128)(2,1)S(1)}, u32[]{:S(2)}, u32[]{:S(2)}) collective-permute-start(bf16[16,16,256]{2,1,0:T(8,128)(2,1)} %get-tuple-element.23), channel_id=1, source_target_pairs={{0,8},{8,16},{16,24},{24,0},{1,9},{9,17},{17,25},{25,1},{2,10},{10... | collective-permute-start | bytes 393224 | tf_op jit(solution)/shard_map/ppermute | solution.py:272
  24.1 4.5 %collective-permute-start.6 = (bf16[16,16,256]{2,1,0:T(8,128)(2,1)}, bf16[16,16,256]{2,1,0:T(8,128)(2,1)S(1)}, u32[]{:S(2)}, u32[]{:S(2)}) collective-permute-start(bf16[16,16,256]{2,1,0:T(8,128)(2,1)} %get-tuple-element.24), channel_id=1, source_target_pairs={{0,16},{8,24},{16,0},{24,8},{1,17},{9,25},{17,1},{25,9},{2,18},{10... | collective-permute-start | bytes 393224 | tf_op jit(solution)/shard_map/ppermute | solution.py:272
  28.6 3.0 %collective-permute-start.7 = (bf16[16,16,256]{2,1,0:T(8,128)(2,1)}, bf16[16,16,256]{2,1,0:T(8,128)(2,1)S(1)}, u32[]{:S(2)}, u32[]{:S(2)}) collective-permute-start(bf16[16,16,256]{2,1,0:T(8,128)(2,1)} %get-tuple-element.25), channel_id=1, source_target_pairs={{0,24},{8,0},{16,8},{24,16},{1,25},{9,1},{17,9},{25,17},{2,26},{10... | collective-permute-start | bytes 393224 | tf_op jit(solution)/shard_map/ppermute | solution.py:272
  31.9 3.1 %collective-permute-start.3 = (bf16[64,3328]{1,0:T(8,128)(2,1)S(1)}, bf16[64,3328]{1,0:T(8,128)(2,1)S(1)}, u32[]{:S(2)}, u32[]{:S(2)}) collective-permute-start(bf16[64,3328]{1,0:T(8,128)(2,1)S(1)} %shard_map.87.refs_0_), channel_id=1, source_target_pairs={{0,2},{2,4},{4,6},{6,0},{1,3},{3,5},{5,7},{7,1},{8,10},{10,12},{12... | collective-permute-start | bytes 1277960 | tf_op jit(solution)/shard_map/ppermute | solution.py:272
  35.0 4.4 %collective-permute-start.4 = (bf16[64,3328]{1,0:T(8,128)(2,1)S(1)}, bf16[64,3328]{1,0:T(8,128)(2,1)S(1)}, u32[]{:S(2)}, u32[]{:S(2)}) collective-permute-start(bf16[64,3328]{1,0:T(8,128)(2,1)S(1)} %shard_map.87.refs_0_), channel_id=1, source_target_pairs={{0,4},{2,6},{4,0},{6,2},{1,5},{3,7},{5,1},{7,3},{8,12},{10,14},{12... | collective-permute-start | bytes 1277960 | tf_op jit(solution)/shard_map/ppermute | solution.py:272
  39.5 3.1 %collective-permute-start.8 = (bf16[64,3328]{1,0:T(8,128)(2,1)S(1)}, bf16[64,3328]{1,0:T(8,128)(2,1)}, u32[]{:S(2)}, u32[]{:S(2)}) collective-permute-start(bf16[64,3328]{1,0:T(8,128)(2,1)S(1)} %shard_map.88), channel_id=1, source_target_pairs={{0,6},{2,0},{4,2},{6,4},{1,7},{3,1},{5,3},{7,5},{8,14},{10,8},{12,... | collective-permute-start | bytes 1277960 | tf_op jit(solution)/shard_map/ppermute | solution.py:272
  43.9 11.4 %all-to-all-start.1 = ((bf16[16,4,16,256]{3,2,1,0:T(8,128)(2,1)}), bf16[16,4,16,256]{3,2,1,0:T(8,128)(2,1)S(1)}, u32[]{:S(2)}, u32[]{:S(2)}) async-start(bf16[16,4,16,256]{3,2,1,0:T(8,128)(2,1)} %shard_map.90), calls=%async_computation.1 | async-start | bytes 1048576 | tf_op jit(solution)/shard_map/all_to_all | solution.py:276
  59.5 4.0 %collective-permute-start.9 = (bf16[256,3328]{1,0:T(8,128)(2,1)S(1)}, bf16[256,3328]{1,0:T(8,128)(2,1)S(1)}, u32[]{:S(2)}, u32[]{:S(2)}) collective-permute-start(bf16[256,3328]{1,0:T(8,128)(2,1)S(1)} %shard_map.89.refs_2_.refs_6_), channel_id=1, source_target_pairs={{0,1},{1,0},{2,3},{3,2},{4,5},{5,4},{6,7},{7,6},{8,9},{9,8},{10,11... | collective-permute-start | bytes 5111816 | tf_op jit(solution)/shard_map/ppermute | solution.py:272
  68.2 3.8 %collective-permute-start.2 = (bf16[16,50,256]{2,1,0:T(8,128)(2,1)S(1)}, bf16[16,50,256]{2,1,0:T(8,128)(2,1)}, u32[]{:S(2)}, u32[]{:S(2)}) collective-permute-start(bf16[16,50,256]{2,1,0:T(8,128)(2,1)S(1)} %all-to-all-done.refs_4_.refs_5_.refs_2_), channel_id=1, source_target_pairs={{0,24},{8,0},{16,8},{24,16},{1,25},{9,1},{17,9},{25,17},{2,26},{10... | collective-permute-start | bytes 1228808 | tf_op jit(solution)/shard_map/ppermute | solution.py:272
  73.2 2.9 %all-to-all-done.1 = bf16[16,4,16,256]{3,2,1,0:T(8,128)(2,1)S(1)} async-done(((bf16[16,4,16,256]{3,2,1,0:T(8,128)(2,1)}), bf16[16,4,16,256]{3,2,1,0:T(8,128)(2,1)S(1)}, u32[]{:S(2)}, u32[]{:S(2)}) %all-to-all-start.1) | async-done | bytes 524320 | tf_op jit(solution)/shard_map/all_to_all | solution.py:276
  77.6 3.2 %shard_map.91 = (f32[800,256]{1,0:T(8,128)S(1)}, bf16[800,256]{1,0:T(8,128)(2,1)}, bf16[800,256]{1,0:T(8,128)(2,1)}, bf16[800,256]{1,0:T(8,128)(2,1)S(1)}) custom-call(s32[2]{0:T(128)S(1)} %pad_add_fusion.refs_0_, bf16[1024,256]{1,0:T(8,128)(2,1)S(1)} %bitcast.11, bf16[256,3328]{1,0:T(8,128)(2,1)S(1)} %shard_map.89.refs_2_.refs_6_, ...), custom_call_target="tpu_custom_call" | custom-call | flops 1000000000 | bytes 4194304 | tf_op jit(solution)/shard_map/pallas_call | solution.py:28
  83.1 3.9 %collective-permute-start.14 = (bf16[800,256]{1,0:T(8,128)(2,1)}, bf16[800,256]{1,0:T(8,128)(2,1)S(1)}, u32[]{:S(2)}, u32[]{:S(2)}) collective-permute-start(bf16[800,256]{1,0:T(8,128)(2,1)} %get-tuple-element.32), channel_id=1, source_target_pairs={{0,16},{8,24},{16,0},{24,8},{1,17},{9,25},{17,1},{25,9},{2,18},{10... | collective-permute-start | bytes 1228808 | tf_op jit(solution)/shard_map/ppermute | solution.py:272
  90.8 4.2 %shard_map.92 = bf16[1024,256]{1,0:T(8,128)(2,1)} custom-call(s32[2]{0:T(128)S(1)} %pad_add_fusion.refs_0_, f32[1,3200]{1,0:T(1,128)S(1)} %reshape.33.refs_1_, bf16[16,50,256]{2,1,0:T(8,128)(2,1)S(1)} %all-to-all-done.refs_4_.refs_5_.refs_2_, bf16[16,50,256]{2,1,0:T(8,128)(2,1)} %collective-permute-done.refs_3_, ...), custom_call_target="tpu_custom_call" | custom-call | flops 2000000000 | bytes 4194304 | tf_op jit(solution)/shard_map/pallas_call | solution.py:28
  95.0 12.4 %all-to-all-start.2 = ((bf16[16,4,16,256]{3,2,1,0:T(8,128)(2,1)}), bf16[16,4,16,256]{3,2,1,0:T(8,128)(2,1)}, u32[]{:S(2)}, u32[]{:S(2)}) async-start(bf16[16,4,16,256]{3,2,1,0:T(8,128)(2,1)} %bitcast.6), calls=%async_computation.2 | async-start | bytes 1048576 | tf_op jit(solution)/shard_map/all_to_all | solution.py:276
  110.5 3.2 %collective-permute-start.16 = (bf16[208,256]{1,0:T(8,128)(2,1)S(1)}, bf16[208,256]{1,0:T(8,128)(2,1)S(1)}, u32[]{:S(2)}, u32[]{:S(2)}) collective-permute-start(bf16[208,256]{1,0:T(8,128)(2,1)S(1)} %get-tuple-element.36), channel_id=1, source_target_pairs={{0,32},{32,64},{64,96},{96,0},{1,33},{33,65},{65,97},{97,1},{2,34}... | collective-permute-start | bytes 319496 | tf_op jit(solution)/shard_map/ppermute | solution.py:272
  113.7 4.1 %collective-permute-start.17 = (bf16[208,256]{1,0:T(8,128)(2,1)S(1)}, bf16[208,256]{1,0:T(8,128)(2,1)S(1)}, u32[]{:S(2)}, u32[]{:S(2)}) collective-permute-start(bf16[208,256]{1,0:T(8,128)(2,1)S(1)} %get-tuple-element.37), channel_id=1, source_target_pairs={{0,64},{32,96},{64,0},{96,32},{1,65},{33,97},{65,1},{97,33},{2,66}... | collective-permute-start | bytes 319496 | tf_op jit(solution)/shard_map/ppermute | solution.py:272
  117.8 3.0 %collective-permute-start.18 = (bf16[208,256]{1,0:T(8,128)(2,1)S(1)}, bf16[208,256]{1,0:T(8,128)(2,1)S(1)}, u32[]{:S(2)}, u32[]{:S(2)}) collective-permute-start(bf16[208,256]{1,0:T(8,128)(2,1)S(1)} %get-tuple-element.38), channel_id=1, source_target_pairs={{0,96},{32,0},{64,32},{96,64},{1,97},{33,1},{65,33},{97,65},{2,98}... | collective-permute-start | bytes 319496 | tf_op jit(solution)/shard_map/ppermute | solution.py:272
  120.8 10.9 %collective-permute-done.16.refs_2_ = bf16[208,256]{1,0:T(8,128)(2,1)S(1)} collective-permute-done((bf16[208,256]{1,0:T(8,128)(2,1)S(1)}, bf16[208,256]{1,0:T(8,128)(2,1)S(1)}, u32[]{:S(2)}, u32[]{:S(2)}) %collective-permute-start.16) | collective-permute-done | bytes 106528 | tf_op jit(solution)/shard_map/ppermute | solution.py:272
  131.7 6.3 %collective-permute-done.17.refs_3_ = bf16[208,256]{1,0:T(8,128)(2,1)S(1)} collective-permute-done((bf16[208,256]{1,0:T(8,128)(2,1)S(1)}, bf16[208,256]{1,0:T(8,128)(2,1)S(1)}, u32[]{:S(2)}, u32[]{:S(2)}) %collective-permute-start.17) | collective-permute-done | bytes 106528 | tf_op jit(solution)/shard_map/ppermute | solution.py:272
  138.8 11.4 %all-to-all-start.3 = ((bf16[4,64,256]{2,1,0:T(8,128)(2,1)}), bf16[4,64,256]{2,1,0:T(8,128)(2,1)S(1)}, u32[]{:S(2)}, u32[]{:S(2)}) async-start(bf16[4,64,256]{2,1,0:T(8,128)(2,1)} %shard_map.96), calls=%async_computation.3 | async-start | bytes 262144 | tf_op jit(solution)/shard_map/all_to_all | solution.py:276
  153.9 5.4 %collective-permute-start.11 = (bf16[16,16,256]{2,1,0:T(8,128)(2,1)S(1)}, bf16[16,16,256]{2,1,0:T(8,128)(2,1)S(1)}, u32[]{:S(2)}, u32[]{:S(2)}) collective-permute-start(bf16[16,16,256]{2,1,0:T(8,128)(2,1)S(1)} %get-tuple-element.29), channel_id=1, source_target_pairs={{0,16},{8,24},{16,0},{24,8},{1,17},{9,25},{17,1},{25,9},{2,18},{10... | collective-permute-start | bytes 393224 | tf_op jit(solution)/shard_map/ppermute | solution.py:272
  163.0 11.9 %all-to-all-start.4 = ((f32[32,4,256]{2,1,0:T(4,128)}), f32[32,4,256]{2,1,0:T(4,128)S(1)}, u32[]{:S(2)}, u32[]{:S(2)}) async-start(f32[32,4,256]{2,1,0:T(4,128)} %get-tuple-element.40), calls=%async_computation.4 | async-start | bytes 262144 | tf_op jit(solution)/shard_map/all_to_all | solution.py:276
  176.6 5.9 %all-to-all-done.4 = f32[32,4,256]{2,1,0:T(4,128)S(1)} async-done(((f32[32,4,256]{2,1,0:T(4,128)}), f32[32,4,256]{2,1,0:T(4,128)S(1)}, u32[]{:S(2)}, u32[]{:S(2)}) %all-to-all-start.4) | async-done | bytes 131104 | tf_op jit(solution)/shard_map/all_to_all | solution.py:276
  (71 shorter events, 37.6 us)
Async XLA Ops:
  2.3 40.3 %all-to-all-start = ((bf16[16,50,256]{2,1,0:T(8,128)(2,1)}), bf16[16,50,256]{2,1,0:T(8,128)(2,1)S(1)}, u32[]{:S(2)}, u32[]{:S(2)}) async-start(bf16[16,50,256]{2,1,0:T(8,128)(2,1)} %shard_map.85), calls=%async_computation | async-start | bytes 917504 | tf_op jit(solution)/shard_map/all_to_all | solution.py:276
  20.9 18.5 %collective-permute-start.5 = (bf16[16,16,256]{2,1,0:T(8,128)(2,1)}, bf16[16,16,256]{2,1,0:T(8,128)(2,1)S(1)}, u32[]{:S(2)}, u32[]{:S(2)}) collective-permute-start(bf16[16,16,256]{2,1,0:T(8,128)(2,1)} %get-tuple-element.23), channel_id=1, source_target_pairs={{0,8},{8,16},{16,24},{24,0},{1,9},{9,17},{17,25},{25,1},{2,10},{10... | collective-permute-start | bytes 393224 | tf_op jit(solution)/shard_map/ppermute | solution.py:272
  24.1 15.3 %collective-permute-start.6 = (bf16[16,16,256]{2,1,0:T(8,128)(2,1)}, bf16[16,16,256]{2,1,0:T(8,128)(2,1)S(1)}, u32[]{:S(2)}, u32[]{:S(2)}) collective-permute-start(bf16[16,16,256]{2,1,0:T(8,128)(2,1)} %get-tuple-element.24), channel_id=1, source_target_pairs={{0,16},{8,24},{16,0},{24,8},{1,17},{9,25},{17,1},{25,9},{2,18},{10... | collective-permute-start | bytes 393224 | tf_op jit(solution)/shard_map/ppermute | solution.py:272
  28.6 10.8 %collective-permute-start.7 = (bf16[16,16,256]{2,1,0:T(8,128)(2,1)}, bf16[16,16,256]{2,1,0:T(8,128)(2,1)S(1)}, u32[]{:S(2)}, u32[]{:S(2)}) collective-permute-start(bf16[16,16,256]{2,1,0:T(8,128)(2,1)} %get-tuple-element.25), channel_id=1, source_target_pairs={{0,24},{8,0},{16,8},{24,16},{1,25},{9,1},{17,9},{25,17},{2,26},{10... | collective-permute-start | bytes 393224 | tf_op jit(solution)/shard_map/ppermute | solution.py:272
  31.9 23.5 %collective-permute-start.3 = (bf16[64,3328]{1,0:T(8,128)(2,1)S(1)}, bf16[64,3328]{1,0:T(8,128)(2,1)S(1)}, u32[]{:S(2)}, u32[]{:S(2)}) collective-permute-start(bf16[64,3328]{1,0:T(8,128)(2,1)S(1)} %shard_map.87.refs_0_), channel_id=1, source_target_pairs={{0,2},{2,4},{4,6},{6,0},{1,3},{3,5},{5,7},{7,1},{8,10},{10,12},{12... | collective-permute-start | bytes 1277960 | tf_op jit(solution)/shard_map/ppermute | solution.py:272
  35.0 20.4 %collective-permute-start.4 = (bf16[64,3328]{1,0:T(8,128)(2,1)S(1)}, bf16[64,3328]{1,0:T(8,128)(2,1)S(1)}, u32[]{:S(2)}, u32[]{:S(2)}) collective-permute-start(bf16[64,3328]{1,0:T(8,128)(2,1)S(1)} %shard_map.87.refs_0_), channel_id=1, source_target_pairs={{0,4},{2,6},{4,0},{6,2},{1,5},{3,7},{5,1},{7,3},{8,12},{10,14},{12... | collective-permute-start | bytes 1277960 | tf_op jit(solution)/shard_map/ppermute | solution.py:272
  39.5 17.9 %collective-permute-start.8 = (bf16[64,3328]{1,0:T(8,128)(2,1)S(1)}, bf16[64,3328]{1,0:T(8,128)(2,1)}, u32[]{:S(2)}, u32[]{:S(2)}) collective-permute-start(bf16[64,3328]{1,0:T(8,128)(2,1)S(1)} %shard_map.88), channel_id=1, source_target_pairs={{0,6},{2,0},{4,2},{6,4},{1,7},{3,1},{5,3},{7,5},{8,14},{10,8},{12,... | collective-permute-start | bytes 1277960 | tf_op jit(solution)/shard_map/ppermute | solution.py:272
  43.9 32.2 %all-to-all-start.1 = ((bf16[16,4,16,256]{3,2,1,0:T(8,128)(2,1)}), bf16[16,4,16,256]{3,2,1,0:T(8,128)(2,1)S(1)}, u32[]{:S(2)}, u32[]{:S(2)}) async-start(bf16[16,4,16,256]{3,2,1,0:T(8,128)(2,1)} %shard_map.90), calls=%async_computation.1 | async-start | bytes 1048576 | tf_op jit(solution)/shard_map/all_to_all | solution.py:276
  59.5 12.5 %collective-permute-start.9 = (bf16[256,3328]{1,0:T(8,128)(2,1)S(1)}, bf16[256,3328]{1,0:T(8,128)(2,1)S(1)}, u32[]{:S(2)}, u32[]{:S(2)}) collective-permute-start(bf16[256,3328]{1,0:T(8,128)(2,1)S(1)} %shard_map.89.refs_2_.refs_6_), channel_id=1, source_target_pairs={{0,1},{1,0},{2,3},{3,2},{4,5},{5,4},{6,7},{7,6},{8,9},{9,8},{10,11... | collective-permute-start | bytes 5111816 | tf_op jit(solution)/shard_map/ppermute | solution.py:272
  63.4 25.2 %collective-permute-start = (bf16[16,50,256]{2,1,0:T(8,128)(2,1)S(1)}, bf16[16,50,256]{2,1,0:T(8,128)(2,1)}, u32[]{:S(2)}, u32[]{:S(2)}) collective-permute-start(bf16[16,50,256]{2,1,0:T(8,128)(2,1)S(1)} %all-to-all-done.refs_4_.refs_5_.refs_2_), channel_id=1, source_target_pairs={{0,8},{8,16},{16,24},{24,0},{1,9},{9,17},{17,25},{25,1},{2,10},{10... | collective-permute-start | bytes 1228808 | tf_op jit(solution)/shard_map/ppermute | solution.py:272
  65.7 24.8 %collective-permute-start.1 = (bf16[16,50,256]{2,1,0:T(8,128)(2,1)S(1)}, bf16[16,50,256]{2,1,0:T(8,128)(2,1)}, u32[]{:S(2)}, u32[]{:S(2)}) collective-permute-start(bf16[16,50,256]{2,1,0:T(8,128)(2,1)S(1)} %all-to-all-done.refs_4_.refs_5_.refs_2_), channel_id=1, source_target_pairs={{0,16},{8,24},{16,0},{24,8},{1,17},{9,25},{17,1},{25,9},{2,18},{10... | collective-permute-start | bytes 1228808 | tf_op jit(solution)/shard_map/ppermute | solution.py:272
  68.2 22.7 %collective-permute-start.2 = (bf16[16,50,256]{2,1,0:T(8,128)(2,1)S(1)}, bf16[16,50,256]{2,1,0:T(8,128)(2,1)}, u32[]{:S(2)}, u32[]{:S(2)}) collective-permute-start(bf16[16,50,256]{2,1,0:T(8,128)(2,1)S(1)} %all-to-all-done.refs_4_.refs_5_.refs_2_), channel_id=1, source_target_pairs={{0,24},{8,0},{16,8},{24,16},{1,25},{9,1},{17,9},{25,17},{2,26},{10... | collective-permute-start | bytes 1228808 | tf_op jit(solution)/shard_map/ppermute | solution.py:272
  80.8 26.6 %collective-permute-start.13 = (bf16[800,256]{1,0:T(8,128)(2,1)}, bf16[800,256]{1,0:T(8,128)(2,1)S(1)}, u32[]{:S(2)}, u32[]{:S(2)}) collective-permute-start(bf16[800,256]{1,0:T(8,128)(2,1)} %get-tuple-element.31), channel_id=1, source_target_pairs={{0,8},{8,16},{16,24},{24,0},{1,9},{9,17},{17,25},{25,1},{2,10},{10... | collective-permute-start | bytes 1228808 | tf_op jit(solution)/shard_map/ppermute | solution.py:272
  83.1 24.3 %collective-permute-start.14 = (bf16[800,256]{1,0:T(8,128)(2,1)}, bf16[800,256]{1,0:T(8,128)(2,1)S(1)}, u32[]{:S(2)}, u32[]{:S(2)}) collective-permute-start(bf16[800,256]{1,0:T(8,128)(2,1)} %get-tuple-element.32), channel_id=1, source_target_pairs={{0,16},{8,24},{16,0},{24,8},{1,17},{9,25},{17,1},{25,9},{2,18},{10... | collective-permute-start | bytes 1228808 | tf_op jit(solution)/shard_map/ppermute | solution.py:272
  88.6 18.8 %collective-permute-start.15 = (bf16[800,256]{1,0:T(8,128)(2,1)S(1)}, bf16[800,256]{1,0:T(8,128)(2,1)}, u32[]{:S(2)}, u32[]{:S(2)}) collective-permute-start(bf16[800,256]{1,0:T(8,128)(2,1)S(1)} %get-tuple-element.33), channel_id=1, source_target_pairs={{0,24},{8,0},{16,8},{24,16},{1,25},{9,1},{17,9},{25,17},{2,26},{10... | collective-permute-start | bytes 1228808 | tf_op jit(solution)/shard_map/ppermute | solution.py:272
  95.0 43.0 %all-to-all-start.2 = ((bf16[16,4,16,256]{3,2,1,0:T(8,128)(2,1)}), bf16[16,4,16,256]{3,2,1,0:T(8,128)(2,1)}, u32[]{:S(2)}, u32[]{:S(2)}) async-start(bf16[16,4,16,256]{3,2,1,0:T(8,128)(2,1)} %bitcast.6), calls=%async_computation.2 | async-start | bytes 1048576 | tf_op jit(solution)/shard_map/all_to_all | solution.py:276
  110.5 21.2 %collective-permute-start.16 = (bf16[208,256]{1,0:T(8,128)(2,1)S(1)}, bf16[208,256]{1,0:T(8,128)(2,1)S(1)}, u32[]{:S(2)}, u32[]{:S(2)}) collective-permute-start(bf16[208,256]{1,0:T(8,128)(2,1)S(1)} %get-tuple-element.36), channel_id=1, source_target_pairs={{0,32},{32,64},{64,96},{96,0},{1,33},{33,65},{65,97},{97,1},{2,34}... | collective-permute-start | bytes 319496 | tf_op jit(solution)/shard_map/ppermute | solution.py:272
  113.7 24.3 %collective-permute-start.17 = (bf16[208,256]{1,0:T(8,128)(2,1)S(1)}, bf16[208,256]{1,0:T(8,128)(2,1)S(1)}, u32[]{:S(2)}, u32[]{:S(2)}) collective-permute-start(bf16[208,256]{1,0:T(8,128)(2,1)S(1)} %get-tuple-element.37), channel_id=1, source_target_pairs={{0,64},{32,96},{64,0},{96,32},{1,65},{33,97},{65,1},{97,33},{2,66}... | collective-permute-start | bytes 319496 | tf_op jit(solution)/shard_map/ppermute | solution.py:272
  117.8 20.2 %collective-permute-start.18 = (bf16[208,256]{1,0:T(8,128)(2,1)S(1)}, bf16[208,256]{1,0:T(8,128)(2,1)S(1)}, u32[]{:S(2)}, u32[]{:S(2)}) collective-permute-start(bf16[208,256]{1,0:T(8,128)(2,1)S(1)} %get-tuple-element.38), channel_id=1, source_target_pairs={{0,96},{32,0},{64,32},{96,64},{1,97},{33,1},{65,33},{97,65},{2,98}... | collective-permute-start | bytes 319496 | tf_op jit(solution)/shard_map/ppermute | solution.py:272
  138.8 23.5 %all-to-all-start.3 = ((bf16[4,64,256]{2,1,0:T(8,128)(2,1)}), bf16[4,64,256]{2,1,0:T(8,128)(2,1)S(1)}, u32[]{:S(2)}, u32[]{:S(2)}) async-start(bf16[4,64,256]{2,1,0:T(8,128)(2,1)} %shard_map.96), calls=%async_computation.3 | async-start | bytes 262144 | tf_op jit(solution)/shard_map/all_to_all | solution.py:276
  151.2 23.6 %collective-permute-start.10 = (bf16[16,16,256]{2,1,0:T(8,128)(2,1)S(1)}, bf16[16,16,256]{2,1,0:T(8,128)(2,1)S(1)}, u32[]{:S(2)}, u32[]{:S(2)}) collective-permute-start(bf16[16,16,256]{2,1,0:T(8,128)(2,1)S(1)} %get-tuple-element.28), channel_id=1, source_target_pairs={{0,8},{8,16},{16,24},{24,0},{1,9},{9,17},{17,25},{25,1},{2,10},{10... | collective-permute-start | bytes 393224 | tf_op jit(solution)/shard_map/ppermute | solution.py:272
  153.9 20.9 %collective-permute-start.11 = (bf16[16,16,256]{2,1,0:T(8,128)(2,1)S(1)}, bf16[16,16,256]{2,1,0:T(8,128)(2,1)S(1)}, u32[]{:S(2)}, u32[]{:S(2)}) collective-permute-start(bf16[16,16,256]{2,1,0:T(8,128)(2,1)S(1)} %get-tuple-element.29), channel_id=1, source_target_pairs={{0,16},{8,24},{16,0},{24,8},{1,17},{9,25},{17,1},{25,9},{2,18},{10... | collective-permute-start | bytes 393224 | tf_op jit(solution)/shard_map/ppermute | solution.py:272
  159.4 15.5 %collective-permute-start.12 = (bf16[16,16,256]{2,1,0:T(8,128)(2,1)S(1)}, bf16[16,16,256]{2,1,0:T(8,128)(2,1)S(1)}, u32[]{:S(2)}, u32[]{:S(2)}) collective-permute-start(bf16[16,16,256]{2,1,0:T(8,128)(2,1)S(1)} %get-tuple-element.30), channel_id=1, source_target_pairs={{0,24},{8,0},{16,8},{24,16},{1,25},{9,1},{17,9},{25,17},{2,26},{10... | collective-permute-start | bytes 393224 | tf_op jit(solution)/shard_map/ppermute | solution.py:272
  163.0 19.5 %all-to-all-start.4 = ((f32[32,4,256]{2,1,0:T(4,128)}), f32[32,4,256]{2,1,0:T(4,128)S(1)}, u32[]{:S(2)}, u32[]{:S(2)}) async-start(f32[32,4,256]{2,1,0:T(4,128)} %get-tuple-element.40), calls=%async_computation.4 | async-start | bytes 262144 | tf_op jit(solution)/shard_map/all_to_all | solution.py:276
  (11 other events, 113.3 us)

commit v5 on v4

--- a/solution.py
+++ b/solution.py
@@ -31,7 +31,7 @@
         in_specs=specs + [pl.BlockSpec(memory_space=pl.ANY)] * more,
         out_specs=jax.tree.map(lambda _: whole, out_shape),
         scratch_shapes=list(scratch),
-        compiler_params=pltpu.CompilerParams(vmem_limit_bytes=20 * 2**20),
+        compiler_params=pltpu.CompilerParams(vmem_limit_bytes=16 * 2**20),
         cost_estimate=pl.CostEstimate(flops=flops, bytes_accessed=4 * 2**20, transcendentals=0),
     )(*args, *after)
 

time: 185 us -> 185 us (level)
  no operation moved by 1% of the time
where the time goes in v5:
time: 185 us; the launch traced here: 183 us
  starting transfers between devices  125 us (68%)
  waiting for transfers between devices  29.3 us (16%)
  Pallas kernels  18.8 us (10%)
  local copies, waits for them, and re-layouts  9.21 us (5%)
    all_to_all x5, starting transfers between devices, all_to_all(): return lax.all_to_all(value, axes, split_axis=0, concat_axis=0, tiled=True)  62.8 us
    ppermute x19, starting transfers between devices, shifted(): lax.ppermute(value, axis, [(i, (i + shift) % size) for i in range(size)])  62.1 us
    ppermute x19, waiting for transfers between devices, shifted(): lax.ppermute(value, axis, [(i, (i + shift) % size) for i in range(size)])  20.3 us
    pallas_call x13, Pallas kernels, call(): pl.pallas_call(body, out_shape=out_shape, in_specs=specs + [pl.BlockSpec(...  18.8 us
    all_to_all x5, waiting for transfers between devices, all_to_all(): return lax.all_to_all(value, axes, split_axis=0, concat_axis=0, tiled=True)  8.99 us
    unnamed x24, local copies, waits for them, and re-layouts  7.39 us
  transfers between devices with their start and end apart: 24, of which 8 were waited for; matrix products, arithmetic and copies ran while one was open for 1% of the time, Pallas kernels for 9%

profile of v5, /device:TPU:1, one launch (start us, length us, event | category | flops | bytes accessed | tf_op | source)
XLA Modules:
  0.0 183.5 jit_solution(8303494438302304481)
XLA Ops:
  2.3 15.7 %all-to-all-start = ((bf16[16,50,256]{2,1,0:T(8,128)(2,1)}), bf16[16,50,256]{2,1,0:T(8,128)(2,1)S(1)}, u32[]{:S(2)}, u32[]{:S(2)}) async-start(bf16[16,50,256]{2,1,0:T(8,128)(2,1)} %shard_map.85), calls=%async_computation | async-start | bytes 917504 | tf_op jit(solution)/shard_map/all_to_all | solution.py:276
  20.9 3.2 %collective-permute-start.5 = (bf16[16,16,256]{2,1,0:T(8,128)(2,1)}, bf16[16,16,256]{2,1,0:T(8,128)(2,1)S(1)}, u32[]{:S(2)}, u32[]{:S(2)}) collective-permute-start(bf16[16,16,256]{2,1,0:T(8,128)(2,1)} %get-tuple-element.23), channel_id=1, source_target_pairs={{0,8},{8,16},{16,24},{24,0},{1,9},{9,17},{17,25},{25,1},{2,10},{10... | collective-permute-start | bytes 393224 | tf_op jit(solution)/shard_map/ppermute | solution.py:272
  24.1 4.5 %collective-permute-start.6 = (bf16[16,16,256]{2,1,0:T(8,128)(2,1)}, bf16[16,16,256]{2,1,0:T(8,128)(2,1)S(1)}, u32[]{:S(2)}, u32[]{:S(2)}) collective-permute-start(bf16[16,16,256]{2,1,0:T(8,128)(2,1)} %get-tuple-element.24), channel_id=1, source_target_pairs={{0,16},{8,24},{16,0},{24,8},{1,17},{9,25},{17,1},{25,9},{2,18},{10... | collective-permute-start | bytes 393224 | tf_op jit(solution)/shard_map/ppermute | solution.py:272
  28.6 3.0 %collective-permute-start.7 = (bf16[16,16,256]{2,1,0:T(8,128)(2,1)}, bf16[16,16,256]{2,1,0:T(8,128)(2,1)S(1)}, u32[]{:S(2)}, u32[]{:S(2)}) collective-permute-start(bf16[16,16,256]{2,1,0:T(8,128)(2,1)} %get-tuple-element.25), channel_id=1, source_target_pairs={{0,24},{8,0},{16,8},{24,16},{1,25},{9,1},{17,9},{25,17},{2,26},{10... | collective-permute-start | bytes 393224 | tf_op jit(solution)/shard_map/ppermute | solution.py:272
  31.9 3.1 %collective-permute-start.3 = (bf16[64,3328]{1,0:T(8,128)(2,1)S(1)}, bf16[64,3328]{1,0:T(8,128)(2,1)S(1)}, u32[]{:S(2)}, u32[]{:S(2)}) collective-permute-start(bf16[64,3328]{1,0:T(8,128)(2,1)S(1)} %shard_map.87.refs_0_), channel_id=1, source_target_pairs={{0,2},{2,4},{4,6},{6,0},{1,3},{3,5},{5,7},{7,1},{8,10},{10,12},{12... | collective-permute-start | bytes 1277960 | tf_op jit(solution)/shard_map/ppermute | solution.py:272
  35.0 4.4 %collective-permute-start.4 = (bf16[64,3328]{1,0:T(8,128)(2,1)S(1)}, bf16[64,3328]{1,0:T(8,128)(2,1)S(1)}, u32[]{:S(2)}, u32[]{:S(2)}) collective-permute-start(bf16[64,3328]{1,0:T(8,128)(2,1)S(1)} %shard_map.87.refs_0_), channel_id=1, source_target_pairs={{0,4},{2,6},{4,0},{6,2},{1,5},{3,7},{5,1},{7,3},{8,12},{10,14},{12... | collective-permute-start | bytes 1277960 | tf_op jit(solution)/shard_map/ppermute | solution.py:272
  39.5 3.1 %collective-permute-start.8 = (bf16[64,3328]{1,0:T(8,128)(2,1)S(1)}, bf16[64,3328]{1,0:T(8,128)(2,1)}, u32[]{:S(2)}, u32[]{:S(2)}) collective-permute-start(bf16[64,3328]{1,0:T(8,128)(2,1)S(1)} %shard_map.88), channel_id=1, source_target_pairs={{0,6},{2,0},{4,2},{6,4},{1,7},{3,1},{5,3},{7,5},{8,14},{10,8},{12,... | collective-permute-start | bytes 1277960 | tf_op jit(solution)/shard_map/ppermute | solution.py:272
  43.9 11.4 %all-to-all-start.1 = ((bf16[16,4,16,256]{3,2,1,0:T(8,128)(2,1)}), bf16[16,4,16,256]{3,2,1,0:T(8,128)(2,1)S(1)}, u32[]{:S(2)}, u32[]{:S(2)}) async-start(bf16[16,4,16,256]{3,2,1,0:T(8,128)(2,1)} %shard_map.90), calls=%async_computation.1 | async-start | bytes 1048576 | tf_op jit(solution)/shard_map/all_to_all | solution.py:276
  59.5 4.0 %collective-permute-start.9 = (bf16[256,3328]{1,0:T(8,128)(2,1)S(1)}, bf16[256,3328]{1,0:T(8,128)(2,1)S(1)}, u32[]{:S(2)}, u32[]{:S(2)}) collective-permute-start(bf16[256,3328]{1,0:T(8,128)(2,1)S(1)} %shard_map.89.refs_2_.refs_6_), channel_id=1, source_target_pairs={{0,1},{1,0},{2,3},{3,2},{4,5},{5,4},{6,7},{7,6},{8,9},{9,8},{10,11... | collective-permute-start | bytes 5111816 | tf_op jit(solution)/shard_map/ppermute | solution.py:272
  68.2 3.8 %collective-permute-start.2 = (bf16[16,50,256]{2,1,0:T(8,128)(2,1)S(1)}, bf16[16,50,256]{2,1,0:T(8,128)(2,1)}, u32[]{:S(2)}, u32[]{:S(2)}) collective-permute-start(bf16[16,50,256]{2,1,0:T(8,128)(2,1)S(1)} %all-to-all-done.refs_4_.refs_5_.refs_2_), channel_id=1, source_target_pairs={{0,24},{8,0},{16,8},{24,16},{1,25},{9,1},{17,9},{25,17},{2,26},{10... | collective-permute-start | bytes 1228808 | tf_op jit(solution)/shard_map/ppermute | solution.py:272
  73.2 2.9 %all-to-all-done.1 = bf16[16,4,16,256]{3,2,1,0:T(8,128)(2,1)S(1)} async-done(((bf16[16,4,16,256]{3,2,1,0:T(8,128)(2,1)}), bf16[16,4,16,256]{3,2,1,0:T(8,128)(2,1)S(1)}, u32[]{:S(2)}, u32[]{:S(2)}) %all-to-all-start.1) | async-done | bytes 524320 | tf_op jit(solution)/shard_map/all_to_all | solution.py:276
  77.6 3.2 %shard_map.91 = (f32[800,256]{1,0:T(8,128)S(1)}, bf16[800,256]{1,0:T(8,128)(2,1)}, bf16[800,256]{1,0:T(8,128)(2,1)}, bf16[800,256]{1,0:T(8,128)(2,1)S(1)}) custom-call(s32[2]{0:T(128)S(1)} %pad_add_fusion.refs_0_, bf16[1024,256]{1,0:T(8,128)(2,1)S(1)} %bitcast.11, bf16[256,3328]{1,0:T(8,128)(2,1)S(1)} %shard_map.89.refs_2_.refs_6_, ...), custom_call_target="tpu_custom_call" | custom-call | flops 1000000000 | bytes 4194304 | tf_op jit(solution)/shard_map/pallas_call | solution.py:28
  83.1 3.9 %collective-permute-start.14 = (bf16[800,256]{1,0:T(8,128)(2,1)}, bf16[800,256]{1,0:T(8,128)(2,1)S(1)}, u32[]{:S(2)}, u32[]{:S(2)}) collective-permute-start(bf16[800,256]{1,0:T(8,128)(2,1)} %get-tuple-element.32), channel_id=1, source_target_pairs={{0,16},{8,24},{16,0},{24,8},{1,17},{9,25},{17,1},{25,9},{2,18},{10... | collective-permute-start | bytes 1228808 | tf_op jit(solution)/shard_map/ppermute | solution.py:272
  90.8 4.2 %shard_map.92 = bf16[1024,256]{1,0:T(8,128)(2,1)} custom-call(s32[2]{0:T(128)S(1)} %pad_add_fusion.refs_0_, f32[1,3200]{1,0:T(1,128)S(1)} %reshape.33.refs_1_, bf16[16,50,256]{2,1,0:T(8,128)(2,1)S(1)} %all-to-all-done.refs_4_.refs_5_.refs_2_, bf16[16,50,256]{2,1,0:T(8,128)(2,1)} %collective-permute-done.refs_3_, ...), custom_call_target="tpu_custom_call" | custom-call | flops 2000000000 | bytes 4194304 | tf_op jit(solution)/shard_map/pallas_call | solution.py:28
  95.0 12.4 %all-to-all-start.2 = ((bf16[16,4,16,256]{3,2,1,0:T(8,128)(2,1)}), bf16[16,4,16,256]{3,2,1,0:T(8,128)(2,1)}, u32[]{:S(2)}, u32[]{:S(2)}) async-start(bf16[16,4,16,256]{3,2,1,0:T(8,128)(2,1)} %bitcast.6), calls=%async_computation.2 | async-start | bytes 1048576 | tf_op jit(solution)/shard_map/all_to_all | solution.py:276
  110.5 3.2 %collective-permute-start.16 = (bf16[208,256]{1,0:T(8,128)(2,1)S(1)}, bf16[208,256]{1,0:T(8,128)(2,1)S(1)}, u32[]{:S(2)}, u32[]{:S(2)}) collective-permute-start(bf16[208,256]{1,0:T(8,128)(2,1)S(1)} %get-tuple-element.36), channel_id=1, source_target_pairs={{0,32},{32,64},{64,96},{96,0},{1,33},{33,65},{65,97},{97,1},{2,34}... | collective-permute-start | bytes 319496 | tf_op jit(solution)/shard_map/ppermute | solution.py:272
  113.7 4.1 %collective-permute-start.17 = (bf16[208,256]{1,0:T(8,128)(2,1)S(1)}, bf16[208,256]{1,0:T(8,128)(2,1)S(1)}, u32[]{:S(2)}, u32[]{:S(2)}) collective-permute-start(bf16[208,256]{1,0:T(8,128)(2,1)S(1)} %get-tuple-element.37), channel_id=1, source_target_pairs={{0,64},{32,96},{64,0},{96,32},{1,65},{33,97},{65,1},{97,33},{2,66}... | collective-permute-start | bytes 319496 | tf_op jit(solution)/shard_map/ppermute | solution.py:272
  117.8 3.0 %collective-permute-start.18 = (bf16[208,256]{1,0:T(8,128)(2,1)S(1)}, bf16[208,256]{1,0:T(8,128)(2,1)S(1)}, u32[]{:S(2)}, u32[]{:S(2)}) collective-permute-start(bf16[208,256]{1,0:T(8,128)(2,1)S(1)} %get-tuple-element.38), channel_id=1, source_target_pairs={{0,96},{32,0},{64,32},{96,64},{1,97},{33,1},{65,33},{97,65},{2,98}... | collective-permute-start | bytes 319496 | tf_op jit(solution)/shard_map/ppermute | solution.py:272
  120.8 10.9 %collective-permute-done.16.refs_2_ = bf16[208,256]{1,0:T(8,128)(2,1)S(1)} collective-permute-done((bf16[208,256]{1,0:T(8,128)(2,1)S(1)}, bf16[208,256]{1,0:T(8,128)(2,1)S(1)}, u32[]{:S(2)}, u32[]{:S(2)}) %collective-permute-start.16) | collective-permute-done | bytes 106528 | tf_op jit(solution)/shard_map/ppermute | solution.py:272
  131.7 6.3 %collective-permute-done.17.refs_3_ = bf16[208,256]{1,0:T(8,128)(2,1)S(1)} collective-permute-done((bf16[208,256]{1,0:T(8,128)(2,1)S(1)}, bf16[208,256]{1,0:T(8,128)(2,1)S(1)}, u32[]{:S(2)}, u32[]{:S(2)}) %collective-permute-start.17) | collective-permute-done | bytes 106528 | tf_op jit(solution)/shard_map/ppermute | solution.py:272
  138.8 11.4 %all-to-all-start.3 = ((bf16[4,64,256]{2,1,0:T(8,128)(2,1)}), bf16[4,64,256]{2,1,0:T(8,128)(2,1)S(1)}, u32[]{:S(2)}, u32[]{:S(2)}) async-start(bf16[4,64,256]{2,1,0:T(8,128)(2,1)} %shard_map.96), calls=%async_computation.3 | async-start | bytes 262144 | tf_op jit(solution)/shard_map/all_to_all | solution.py:276
  153.9 5.4 %collective-permute-start.11 = (bf16[16,16,256]{2,1,0:T(8,128)(2,1)S(1)}, bf16[16,16,256]{2,1,0:T(8,128)(2,1)S(1)}, u32[]{:S(2)}, u32[]{:S(2)}) collective-permute-start(bf16[16,16,256]{2,1,0:T(8,128)(2,1)S(1)} %get-tuple-element.29), channel_id=1, source_target_pairs={{0,16},{8,24},{16,0},{24,8},{1,17},{9,25},{17,1},{25,9},{2,18},{10... | collective-permute-start | bytes 393224 | tf_op jit(solution)/shard_map/ppermute | solution.py:272
  163.0 11.9 %all-to-all-start.4 = ((f32[32,4,256]{2,1,0:T(4,128)}), f32[32,4,256]{2,1,0:T(4,128)S(1)}, u32[]{:S(2)}, u32[]{:S(2)}) async-start(f32[32,4,256]{2,1,0:T(4,128)} %get-tuple-element.40), calls=%async_computation.4 | async-start | bytes 262144 | tf_op jit(solution)/shard_map/all_to_all | solution.py:276
  176.6 5.9 %all-to-all-done.4 = f32[32,4,256]{2,1,0:T(4,128)S(1)} async-done(((f32[32,4,256]{2,1,0:T(4,128)}), f32[32,4,256]{2,1,0:T(4,128)S(1)}, u32[]{:S(2)}, u32[]{:S(2)}) %all-to-all-start.4) | async-done | bytes 131104 | tf_op jit(solution)/shard_map/all_to_all | solution.py:276
  (71 shorter events, 37.6 us)
Async XLA Ops:
  2.3 40.3 %all-to-all-start = ((bf16[16,50,256]{2,1,0:T(8,128)(2,1)}), bf16[16,50,256]{2,1,0:T(8,128)(2,1)S(1)}, u32[]{:S(2)}, u32[]{:S(2)}) async-start(bf16[16,50,256]{2,1,0:T(8,128)(2,1)} %shard_map.85), calls=%async_computation | async-start | bytes 917504 | tf_op jit(solution)/shard_map/all_to_all | solution.py:276
  20.9 18.5 %collective-permute-start.5 = (bf16[16,16,256]{2,1,0:T(8,128)(2,1)}, bf16[16,16,256]{2,1,0:T(8,128)(2,1)S(1)}, u32[]{:S(2)}, u32[]{:S(2)}) collective-permute-start(bf16[16,16,256]{2,1,0:T(8,128)(2,1)} %get-tuple-element.23), channel_id=1, source_target_pairs={{0,8},{8,16},{16,24},{24,0},{1,9},{9,17},{17,25},{25,1},{2,10},{10... | collective-permute-start | bytes 393224 | tf_op jit(solution)/shard_map/ppermute | solution.py:272
  24.1 15.3 %collective-permute-start.6 = (bf16[16,16,256]{2,1,0:T(8,128)(2,1)}, bf16[16,16,256]{2,1,0:T(8,128)(2,1)S(1)}, u32[]{:S(2)}, u32[]{:S(2)}) collective-permute-start(bf16[16,16,256]{2,1,0:T(8,128)(2,1)} %get-tuple-element.24), channel_id=1, source_target_pairs={{0,16},{8,24},{16,0},{24,8},{1,17},{9,25},{17,1},{25,9},{2,18},{10... | collective-permute-start | bytes 393224 | tf_op jit(solution)/shard_map/ppermute | solution.py:272
  28.6 10.8 %collective-permute-start.7 = (bf16[16,16,256]{2,1,0:T(8,128)(2,1)}, bf16[16,16,256]{2,1,0:T(8,128)(2,1)S(1)}, u32[]{:S(2)}, u32[]{:S(2)}) collective-permute-start(bf16[16,16,256]{2,1,0:T(8,128)(2,1)} %get-tuple-element.25), channel_id=1, source_target_pairs={{0,24},{8,0},{16,8},{24,16},{1,25},{9,1},{17,9},{25,17},{2,26},{10... | collective-permute-start | bytes 393224 | tf_op jit(solution)/shard_map/ppermute | solution.py:272
  31.9 23.5 %collective-permute-start.3 = (bf16[64,3328]{1,0:T(8,128)(2,1)S(1)}, bf16[64,3328]{1,0:T(8,128)(2,1)S(1)}, u32[]{:S(2)}, u32[]{:S(2)}) collective-permute-start(bf16[64,3328]{1,0:T(8,128)(2,1)S(1)} %shard_map.87.refs_0_), channel_id=1, source_target_pairs={{0,2},{2,4},{4,6},{6,0},{1,3},{3,5},{5,7},{7,1},{8,10},{10,12},{12... | collective-permute-start | bytes 1277960 | tf_op jit(solution)/shard_map/ppermute | solution.py:272
  35.0 20.4 %collective-permute-start.4 = (bf16[64,3328]{1,0:T(8,128)(2,1)S(1)}, bf16[64,3328]{1,0:T(8,128)(2,1)S(1)}, u32[]{:S(2)}, u32[]{:S(2)}) collective-permute-start(bf16[64,3328]{1,0:T(8,128)(2,1)S(1)} %shard_map.87.refs_0_), channel_id=1, source_target_pairs={{0,4},{2,6},{4,0},{6,2},{1,5},{3,7},{5,1},{7,3},{8,12},{10,14},{12... | collective-permute-start | bytes 1277960 | tf_op jit(solution)/shard_map/ppermute | solution.py:272
  39.5 17.9 %collective-permute-start.8 = (bf16[64,3328]{1,0:T(8,128)(2,1)S(1)}, bf16[64,3328]{1,0:T(8,128)(2,1)}, u32[]{:S(2)}, u32[]{:S(2)}) collective-permute-start(bf16[64,3328]{1,0:T(8,128)(2,1)S(1)} %shard_map.88), channel_id=1, source_target_pairs={{0,6},{2,0},{4,2},{6,4},{1,7},{3,1},{5,3},{7,5},{8,14},{10,8},{12,... | collective-permute-start | bytes 1277960 | tf_op jit(solution)/shard_map/ppermute | solution.py:272
  43.9 32.2 %all-to-all-start.1 = ((bf16[16,4,16,256]{3,2,1,0:T(8,128)(2,1)}), bf16[16,4,16,256]{3,2,1,0:T(8,128)(2,1)S(1)}, u32[]{:S(2)}, u32[]{:S(2)}) async-start(bf16[16,4,16,256]{3,2,1,0:T(8,128)(2,1)} %shard_map.90), calls=%async_computation.1 | async-start | bytes 1048576 | tf_op jit(solution)/shard_map/all_to_all | solution.py:276
  59.5 12.5 %collective-permute-start.9 = (bf16[256,3328]{1,0:T(8,128)(2,1)S(1)}, bf16[256,3328]{1,0:T(8,128)(2,1)S(1)}, u32[]{:S(2)}, u32[]{:S(2)}) collective-permute-start(bf16[256,3328]{1,0:T(8,128)(2,1)S(1)} %shard_map.89.refs_2_.refs_6_), channel_id=1, source_target_pairs={{0,1},{1,0},{2,3},{3,2},{4,5},{5,4},{6,7},{7,6},{8,9},{9,8},{10,11... | collective-permute-start | bytes 5111816 | tf_op jit(solution)/shard_map/ppermute | solution.py:272
  63.4 25.2 %collective-permute-start = (bf16[16,50,256]{2,1,0:T(8,128)(2,1)S(1)}, bf16[16,50,256]{2,1,0:T(8,128)(2,1)}, u32[]{:S(2)}, u32[]{:S(2)}) collective-permute-start(bf16[16,50,256]{2,1,0:T(8,128)(2,1)S(1)} %all-to-all-done.refs_4_.refs_5_.refs_2_), channel_id=1, source_target_pairs={{0,8},{8,16},{16,24},{24,0},{1,9},{9,17},{17,25},{25,1},{2,10},{10... | collective-permute-start | bytes 1228808 | tf_op jit(solution)/shard_map/ppermute | solution.py:272
  65.7 24.8 %collective-permute-start.1 = (bf16[16,50,256]{2,1,0:T(8,128)(2,1)S(1)}, bf16[16,50,256]{2,1,0:T(8,128)(2,1)}, u32[]{:S(2)}, u32[]{:S(2)}) collective-permute-start(bf16[16,50,256]{2,1,0:T(8,128)(2,1)S(1)} %all-to-all-done.refs_4_.refs_5_.refs_2_), channel_id=1, source_target_pairs={{0,16},{8,24},{16,0},{24,8},{1,17},{9,25},{17,1},{25,9},{2,18},{10... | collective-permute-start | bytes 1228808 | tf_op jit(solution)/shard_map/ppermute | solution.py:272
  68.2 22.7 %collective-permute-start.2 = (bf16[16,50,256]{2,1,0:T(8,128)(2,1)S(1)}, bf16[16,50,256]{2,1,0:T(8,128)(2,1)}, u32[]{:S(2)}, u32[]{:S(2)}) collective-permute-start(bf16[16,50,256]{2,1,0:T(8,128)(2,1)S(1)} %all-to-all-done.refs_4_.refs_5_.refs_2_), channel_id=1, source_target_pairs={{0,24},{8,0},{16,8},{24,16},{1,25},{9,1},{17,9},{25,17},{2,26},{10... | collective-permute-start | bytes 1228808 | tf_op jit(solution)/shard_map/ppermute | solution.py:272
  80.8 26.6 %collective-permute-start.13 = (bf16[800,256]{1,0:T(8,128)(2,1)}, bf16[800,256]{1,0:T(8,128)(2,1)S(1)}, u32[]{:S(2)}, u32[]{:S(2)}) collective-permute-start(bf16[800,256]{1,0:T(8,128)(2,1)} %get-tuple-element.31), channel_id=1, source_target_pairs={{0,8},{8,16},{16,24},{24,0},{1,9},{9,17},{17,25},{25,1},{2,10},{10... | collective-permute-start | bytes 1228808 | tf_op jit(solution)/shard_map/ppermute | solution.py:272
  83.1 24.3 %collective-permute-start.14 = (bf16[800,256]{1,0:T(8,128)(2,1)}, bf16[800,256]{1,0:T(8,128)(2,1)S(1)}, u32[]{:S(2)}, u32[]{:S(2)}) collective-permute-start(bf16[800,256]{1,0:T(8,128)(2,1)} %get-tuple-element.32), channel_id=1, source_target_pairs={{0,16},{8,24},{16,0},{24,8},{1,17},{9,25},{17,1},{25,9},{2,18},{10... | collective-permute-start | bytes 1228808 | tf_op jit(solution)/shard_map/ppermute | solution.py:272
  88.6 18.8 %collective-permute-start.15 = (bf16[800,256]{1,0:T(8,128)(2,1)S(1)}, bf16[800,256]{1,0:T(8,128)(2,1)}, u32[]{:S(2)}, u32[]{:S(2)}) collective-permute-start(bf16[800,256]{1,0:T(8,128)(2,1)S(1)} %get-tuple-element.33), channel_id=1, source_target_pairs={{0,24},{8,0},{16,8},{24,16},{1,25},{9,1},{17,9},{25,17},{2,26},{10... | collective-permute-start | bytes 1228808 | tf_op jit(solution)/shard_map/ppermute | solution.py:272
  95.0 43.0 %all-to-all-start.2 = ((bf16[16,4,16,256]{3,2,1,0:T(8,128)(2,1)}), bf16[16,4,16,256]{3,2,1,0:T(8,128)(2,1)}, u32[]{:S(2)}, u32[]{:S(2)}) async-start(bf16[16,4,16,256]{3,2,1,0:T(8,128)(2,1)} %bitcast.6), calls=%async_computation.2 | async-start | bytes 1048576 | tf_op jit(solution)/shard_map/all_to_all | solution.py:276
  110.5 21.2 %collective-permute-start.16 = (bf16[208,256]{1,0:T(8,128)(2,1)S(1)}, bf16[208,256]{1,0:T(8,128)(2,1)S(1)}, u32[]{:S(2)}, u32[]{:S(2)}) collective-permute-start(bf16[208,256]{1,0:T(8,128)(2,1)S(1)} %get-tuple-element.36), channel_id=1, source_target_pairs={{0,32},{32,64},{64,96},{96,0},{1,33},{33,65},{65,97},{97,1},{2,34}... | collective-permute-start | bytes 319496 | tf_op jit(solution)/shard_map/ppermute | solution.py:272
  113.7 24.3 %collective-permute-start.17 = (bf16[208,256]{1,0:T(8,128)(2,1)S(1)}, bf16[208,256]{1,0:T(8,128)(2,1)S(1)}, u32[]{:S(2)}, u32[]{:S(2)}) collective-permute-start(bf16[208,256]{1,0:T(8,128)(2,1)S(1)} %get-tuple-element.37), channel_id=1, source_target_pairs={{0,64},{32,96},{64,0},{96,32},{1,65},{33,97},{65,1},{97,33},{2,66}... | collective-permute-start | bytes 319496 | tf_op jit(solution)/shard_map/ppermute | solution.py:272
  117.8 20.2 %collective-permute-start.18 = (bf16[208,256]{1,0:T(8,128)(2,1)S(1)}, bf16[208,256]{1,0:T(8,128)(2,1)S(1)}, u32[]{:S(2)}, u32[]{:S(2)}) collective-permute-start(bf16[208,256]{1,0:T(8,128)(2,1)S(1)} %get-tuple-element.38), channel_id=1, source_target_pairs={{0,96},{32,0},{64,32},{96,64},{1,97},{33,1},{65,33},{97,65},{2,98}... | collective-permute-start | bytes 319496 | tf_op jit(solution)/shard_map/ppermute | solution.py:272
  138.8 23.5 %all-to-all-start.3 = ((bf16[4,64,256]{2,1,0:T(8,128)(2,1)}), bf16[4,64,256]{2,1,0:T(8,128)(2,1)S(1)}, u32[]{:S(2)}, u32[]{:S(2)}) async-start(bf16[4,64,256]{2,1,0:T(8,128)(2,1)} %shard_map.96), calls=%async_computation.3 | async-start | bytes 262144 | tf_op jit(solution)/shard_map/all_to_all | solution.py:276
  151.2 23.6 %collective-permute-start.10 = (bf16[16,16,256]{2,1,0:T(8,128)(2,1)S(1)}, bf16[16,16,256]{2,1,0:T(8,128)(2,1)S(1)}, u32[]{:S(2)}, u32[]{:S(2)}) collective-permute-start(bf16[16,16,256]{2,1,0:T(8,128)(2,1)S(1)} %get-tuple-element.28), channel_id=1, source_target_pairs={{0,8},{8,16},{16,24},{24,0},{1,9},{9,17},{17,25},{25,1},{2,10},{10... | collective-permute-start | bytes 393224 | tf_op jit(solution)/shard_map/ppermute | solution.py:272
  153.9 20.9 %collective-permute-start.11 = (bf16[16,16,256]{2,1,0:T(8,128)(2,1)S(1)}, bf16[16,16,256]{2,1,0:T(8,128)(2,1)S(1)}, u32[]{:S(2)}, u32[]{:S(2)}) collective-permute-start(bf16[16,16,256]{2,1,0:T(8,128)(2,1)S(1)} %get-tuple-element.29), channel_id=1, source_target_pairs={{0,16},{8,24},{16,0},{24,8},{1,17},{9,25},{17,1},{25,9},{2,18},{10... | collective-permute-start | bytes 393224 | tf_op jit(solution)/shard_map/ppermute | solution.py:272
  159.4 15.5 %collective-permute-start.12 = (bf16[16,16,256]{2,1,0:T(8,128)(2,1)S(1)}, bf16[16,16,256]{2,1,0:T(8,128)(2,1)S(1)}, u32[]{:S(2)}, u32[]{:S(2)}) collective-permute-start(bf16[16,16,256]{2,1,0:T(8,128)(2,1)S(1)} %get-tuple-element.30), channel_id=1, source_target_pairs={{0,24},{8,0},{16,8},{24,16},{1,25},{9,1},{17,9},{25,17},{2,26},{10... | collective-permute-start | bytes 393224 | tf_op jit(solution)/shard_map/ppermute | solution.py:272
  163.0 19.5 %all-to-all-start.4 = ((f32[32,4,256]{2,1,0:T(4,128)}), f32[32,4,256]{2,1,0:T(4,128)S(1)}, u32[]{:S(2)}, u32[]{:S(2)}) async-start(f32[32,4,256]{2,1,0:T(4,128)} %get-tuple-element.40), calls=%async_computation.4 | async-start | bytes 262144 | tf_op jit(solution)/shard_map/all_to_all | solution.py:276
  (11 other events, 113.3 us)
